TPU v7x, 512 devices: a whole 4x4x16 slice. The times are simulated.
512 devices in a mesh: gx: 16 (over x, z_hi, core), gy: 4 (over y), gz: 8 (over z_lo).
Axes of the slice: x: 4, y: 4, z: 16 (z_hi: 2, z_lo: 8; z = z_hi * 8 + z_lo), core: 2. Of those that a mesh axis runs over, the one named last changes fastest.
Arguments:
- wave: float32 [256, 128, 1024], P('gx', 'gy', 'gz'), may hold values from -7 to 7
- external: float32 [256, 128, 1024], P('gx', 'gy', 'gz'), may hold values from 0 to 2
- weights: float32 [3, 17], replicated, may hold values from 0.02 to 0.1
Outputs:
- wave_next: float32 [256, 128, 1024], P('gx', 'gy', 'gz')
- correlation: float32 [256, 128, 1024], P('gx', 'gy', 'gz')
All inputs are finite; a program needn't handle non-finite values.
Results may differ from a plain program's by a relative error of at most 0.00029.
Values sent between devices are 32-bit elements; how exact they have to be, the bound alone decides.
No kernel may reach another device: no remote copies, remote signals or barrier semaphores. Data moves between devices by JAX's collectives and lax.ppermute only.
A program may use at most 64 MiB of HBM per device.

v0:
```python
import functools

import jax
import jax.numpy as jnp
from jax import lax
from jax.sharding import Mesh
from jax.sharding import PartitionSpec as P

SUBSTEPS = 3
GX_GY_GZ = ("gx_0", "gx_1", "gx_2", "gy", "gz")
GX = ("gx_0", "gx_1", "gx_2")


LAP_COEF = (-205.0 / 72.0, 8.0 / 5.0, -1.0 / 5.0, 8.0 / 315.0, -1.0 / 560.0)
FORMS = ("jyz,ji->iyz", "xjz,ji->xiz", "xyj,ji->xyi")


def with_halo(cells, sides, width):
    for axis, dim in sides:
        count = lax.axis_size(axis)
        ends = count - 1
        head = lax.slice_in_dim(cells, 0, width, axis=dim)
        tail = lax.slice_in_dim(cells, cells.shape[dim] - width, cells.shape[dim], axis=dim)
        cells = jnp.concatenate(
            [
                lax.ppermute(tail, axis, [(i, (i + 1) % count) for i in range(ends)]),
                cells,
                lax.ppermute(head, axis, [((i + 1) % count, i) for i in range(ends)]),
            ],
            axis=dim,
        )
    return cells


def with_halo_2(array, sides, width):
    edges = {}
    for axis, dim in sides:
        size, length = (lax.axis_size(axis), array.shape[dim])
        up = [(i, (i + 1) % size) for i in range(size - 1)]
        last = lax.slice_in_dim(array, length - width, length, axis=dim)
        leading = lax.slice_in_dim(array, 0, width, axis=dim)
        edges[dim] = (
            lax.ppermute(last, axis, up),
            lax.ppermute(leading, axis, [(b, a) for a, b in up]),
        )
    done = []
    for _, dim in sides:
        low, high = edges[dim]
        around = [(width, width) if d in done else (0, 0) for d in range(array.ndim)]
        array = jnp.concatenate([jnp.pad(low, around), array, jnp.pad(high, around)], axis=dim)
        done.append(dim)
    return array


def by_axis(array, axes):
    return functools.reduce(lax.psum, axes, array)


def band_matrix(row, size_in, flip):
    size_out = size_in - 16
    rows_at = lax.broadcasted_iota(jnp.int32, (size_in, size_out), 0)
    cols_at = lax.broadcasted_iota(jnp.int32, (size_in, size_out), 1)
    offset = rows_at - cols_at
    if flip:
        offset = 16 - offset
    taps = jnp.arange(17, dtype=jnp.int32)
    return jnp.sum(jnp.where(offset[:, :, None] == taps, row, 0.0), axis=2)


def smear(padded, weights, flip):
    for dim in range(3):
        matrix = band_matrix(weights[dim], padded.shape[dim], flip)
        padded = jnp.einsum(FORMS[dim], padded, matrix, precision=lax.Precision.HIGHEST)
    return padded


def trim(field, margin):
    return field[margin:-margin, margin:-margin, margin:-margin]


def laplace(padded):
    center = trim(padded, 4)
    total = 3.0 * LAP_COEF[0] * center
    for dim in range(3):
        length = center.shape[dim]
        for step in range(1, 5):
            upper = [slice(4, -4), slice(4, -4), slice(4, -4)]
            lower = [slice(4, -4), slice(4, -4), slice(4, -4)]
            upper[dim] = slice(4 + step, 4 + step + length)
            lower[dim] = slice(4 - step, 4 - step + length)
            total = total + LAP_COEF[step] * (padded[tuple(upper)] + padded[tuple(lower)])
    return total


def shards(wave, external, weights):
    wide = with_halo(wave, ((GX, 0), ("gy", 1), ("gz", 2)), 16)
    density_wide = wide * wide
    coarse_wide = smear(density_wide, weights, False)
    density_near = trim(density_wide, 8)
    source_near = -1.0 * density_near * coarse_wide + 0.5 * density_near * coarse_wide * coarse_wide
    coarse = trim(coarse_wide, 8)
    correlation = (
        -0.5 * coarse * coarse
        + 0.5 / 3.0 * coarse * coarse * coarse
        + smear(source_near, weights, True)
    )
    potential = correlation + external
    psi = wave
    for step in range(SUBSTEPS):
        near = with_halo_2(psi, ((GX, 0), ("gy", 1), ("gz", 2)), 4)
        psi = psi - 0.08 * (-0.5 * laplace(near) + potential * psi)
    total = by_axis(jnp.sum(psi * psi), GX_GY_GZ)
    count = float(psi.size * lax.axis_size(GX) * lax.axis_size("gy") * lax.axis_size("gz"))
    wave_next = psi * lax.rsqrt(total / count + 1e-06)
    return (wave_next, correlation)


def solution(mesh):
    torus = Mesh(
        mesh.devices.reshape(4, 2, 2, mesh.shape["gy"], mesh.shape["gz"]),
        ("gx_0", "gx_1", "gx_2", "gy", "gz"),
    )
    placed = (P(GX, "gy", "gz"), P(GX, "gy", "gz"), P())
    return jax.shard_map(
        shards,
        mesh=torus,
        in_specs=placed,
        out_specs=(P(GX, "gy", "gz"), P(GX, "gy", "gz")),
        check_vma=False,
    )
```

profile of v0, /device:TPU:8, one launch (start us, length us, event | category | flops | bytes accessed | tf_op | source)
XLA Modules:
  0.0 235.7 jit_solution(12001195429435174276)
XLA Ops:
  0.6 1.9 collective-permute-start.6
  2.5 1.3 collective-permute-start.7
  3.8 1.5 fusion.135
  5.3 16.6 %collective-permute-start.1 = (f32[4,32,128]{2,1,0:T(8,128)S(1)}, f32[4,32,128]{2,1,0:T(8,128)S(1)}, u32[]{:S(2)}, u32[]{:S(2)}) collective-permute-start(f32[4,32,128]{2,1,0:T(8,128)S(1)} %get-tuple-element.41), channel_id=1, source_target_pairs={{0,32},{32,64},{64,96},{96,128},{128,160},{160,192},{192,224},{224... | collective-permute-start | bytes 196616 | tf_op jit(solution)/shard_map/ppermute | solution.py:43
  22.0 1.3 collective-permute-start
  23.3 0.9 fusion.134
  24.1 2.4 %collective-permute-start.2 = (f32[16,4,128]{2,1,0:T(4,128)S(1)}, f32[16,4,128]{2,1,0:T(4,128)S(1)}, u32[]{:S(2)}, u32[]{:S(2)}) collective-permute-start(f32[16,4,128]{2,1,0:T(4,128)S(1)} %get-tuple-element.38), channel_id=1, source_target_pairs={{8,0},{16,8},{24,16},{9,1},{17,9},{25,17},{10,2},{18,10},{26,18},{... | collective-permute-start | bytes 98312 | tf_op jit(solution)/shard_map/ppermute | solution.py:44
  26.6 0.8 slice_bitcast_fusion
  27.4 0.7 select_reduce_fusion.2
  28.1 0.7 select_reduce_fusion.3
  29.2 0.8 select_reduce_fusion.1
  30.0 0.7 select_reduce_fusion.4
  30.7 3.5 %collective-permute-start.3 = (f32[16,4,128]{2,1,0:T(4,128)S(1)}, f32[16,4,128]{2,1,0:T(4,128)S(1)}, u32[]{:S(2)}, u32[]{:S(2)}) collective-permute-start(f32[16,4,128]{2,1,0:T(4,128)S(1)} %get-tuple-element.39), channel_id=1, source_target_pairs={{0,8},{8,16},{16,24},{1,9},{9,17},{17,25},{2,10},{10,18},{18,26},{... | collective-permute-start | bytes 98312 | tf_op jit(solution)/shard_map/ppermute | solution.py:43
  34.2 0.8 constant_dynamic-update-slice_fusion.8
  35.0 0.7 copy-done.11
  35.8 3.5 %collective-permute-start.8 = (f32[48,16,128]{2,1,0:T(8,128)S(1)}, f32[48,16,128]{2,1,0:T(8,128)S(1)}, u32[]{:S(2)}, u32[]{:S(2)}) collective-permute-start(f32[48,16,128]{2,1,0:T(8,128)S(1)} %get-tuple-element.8), channel_id=1, source_target_pairs={{0,8},{8,16},{16,24},{1,9},{9,17},{17,25},{2,10},{10,18},{18,26},{... | collective-permute-start | bytes 1179656 | tf_op jit(solution)/shard_map/ppermute | solution.py:26
  39.3 2.4 %collective-permute-start.9 = (f32[48,16,128]{2,1,0:T(8,128)S(1)}, f32[48,16,128]{2,1,0:T(8,128)S(1)}, u32[]{:S(2)}, u32[]{:S(2)}) collective-permute-start(f32[48,16,128]{2,1,0:T(8,128)S(1)} %get-tuple-element.9), channel_id=1, source_target_pairs={{8,0},{16,8},{24,16},{9,1},{17,9},{25,17},{10,2},{18,10},{26,18},{... | collective-permute-start | bytes 1179656 | tf_op jit(solution)/shard_map/ppermute | solution.py:28
  41.7 0.9 fusion.133
  42.6 0.7 select_reduce_fusion.5
  43.3 1.3 collective-permute-start.4
  44.6 0.6 pad.38
  45.2 5.2 %collective-permute-start.5 = (f32[16,32,4]{2,1,0:T(8,128)}, f32[16,32,4]{2,1,0:T(8,128)}, u32[]{:S(2)}, u32[]{:S(2)}) collective-permute-start(f32[16,32,4]{2,1,0:T(8,128)} %get-tuple-element.37), channel_id=1, source_target_pairs={{0,1},{1,2},{2,3},{3,4},{4,5},{5,6},{6,7},{8,9},{9,10},{10,11},{11... | collective-permute-start | bytes 24584 | tf_op jit(solution)/shard_map/ppermute | solution.py:43
  50.4 0.6 pad.39
  51.2 1.7 fusion.125
  52.9 2.6 %copy.9 = f32[48,64,16]{1,2,0:T(8,128)} copy(f32[48,64,16]{2,1,0:T(8,128)} %get-tuple-element.6) | data formatting | bytes 393216 | tf_op jit(solution)/shard_map/slice | solution.py:23
  55.6 3.0 %collective-permute-start.10 = (f32[48,64,16]{1,2,0:T(8,128)}, f32[48,64,16]{1,2,0:T(8,128)}, u32[]{:S(2)}, u32[]{:S(2)}) collective-permute-start(f32[48,64,16]{1,2,0:T(8,128)} %copy.9), channel_id=1, source_target_pairs={{0,1},{1,2},{2,3},{3,4},{4,5},{5,6},{6,7},{8,9},{9,10},{10,11},{11... | collective-permute-start | bytes 589832 | tf_op jit(solution)/shard_map/ppermute | solution.py:26
  58.6 1.2 copy.10
  59.8 1.5 collective-permute-start.11
  61.2 1.5 constant_dynamic-update-slice_fusion
  62.7 3.0 %select_maximum_fusion.5 = (f32[24,40,132]{2,1,0:T(8,128)}, f32[24,40,132]{2,1,0:T(8,128)}) fusion(f32[16,32,4]{2,1,0:T(8,128)} %collective-permute-done.4, f32[24,4,128]{2,1,0:T(4,128)} %pad.38, f32[24,32,128]{2,1,0:T(8,128)} %get-tuple-element.43, f32[24,4,128]{2,1,0:T(4,128)} %pad.39, f32[16,32,4]{2,1,0:T(8,128)} %collective-permute-done.5), kind=kLoop, calls=%fused_computation.23 | loop fusion | flops 1267200 | bytes 1521664 | tf_op jit(solution)/shard_map/concatenate | solution.py:50
  66.2 1.5 copy.11
  67.7 2.1 collective-permute-done.11
  69.7 2.7 %copy.12 = f32[48,64,16]{2,1,0:T(8,128)} copy(f32[48,64,16]{1,2,0:T(8,128)} %collective-permute-done.11) | data formatting | bytes 393216 | tf_op jit(solution)/shard_map/ppermute | solution.py:28
  72.4 2.7 %maximum_multiply_fusion = f32[48,64,160]{2,1,0:T(8,128)S(1)} fusion(f32[48,64,16]{2,1,0:T(8,128)} %copy.12, f32[48,16,128]{2,1,0:T(8,128)S(1)} %collective-permute-done.9, f32[48,32,128]{2,1,0:T(8,128)S(1)} %constant_dynamic-update-slice_fusion.7, f32[48,16,128]{2,1,0:T(8,128)S(1)} %collective-permute-done.8, f32[48,64,16]{2,1,0:T(8,128)S(1)} %copy.11), kind=kLoop, calls=%fused_computation | loop fusion | flops 2457600 | bytes 3932160 | tf_op jit(solution)/shard_map/mul | solution.py:97
  75.1 3.8 %fusion = f32[32,64,160]{2,0,1:T(8,128)S(1)} fusion(f32[48,64,160]{2,1,0:T(8,128)S(1)} %maximum_multiply_fusion, f32[48,32]{0,1:T(8,128)S(1)} %copy-done.8), kind=kOutput, calls=%fused_computation.1 | convolution fusion | flops 188743680 | bytes 3282944 | tf_op jit(solution)/shard_map/jyz,ji->iyz/dot_general | solution.py:73
  78.9 2.7 %fusion.2 = f32[48,32,160]{2,0,1:T(8,128)S(1)} fusion(f32[32,64,160]{2,0,1:T(8,128)S(1)} %fusion, f32[64,48]{0,1:T(8,128)S(1)} %copy-done.6), kind=kOutput, calls=%fused_computation.5 | convolution fusion | flops 188743680 | bytes 2306048 | tf_op jit(solution)/shard_map/xjz,ji->xiz/dot_general | solution.py:73
  81.6 1.6 add_multiply_fusion
  83.3 1.9 fusion.6
  85.3 1.0 convolution_bitcast_fusion
  86.4 4.6 %fusion.73 = (f32[16,32,128]{2,1,0:T(8,128)S(1)}, f32[16,32,128]{2,1,0:T(8,128)S(1)}, f32[16,32,128]{2,1,0:T(8,128)}) fusion(f32[16,32,128]{2,1,0:T(8,128)S(1)} %copy-done, f32[24,32,128]{2,1,0:T(8,128)S(1)} %copy-done.2, f32[24,4,128]{2,1,0:T(4,128)S(1)} %copy-done.5, f32[24,4,128]{2,1,0:T(4,128)S(1)} %copy-done.4, f32[24,40,132]{2,1,0:T(8,128)} %get-tuple-element.15, ...), kind=kOutput, calls=%fused_computation.137 | convolution fusion | flops 116916224 | bytes 6627328 | tf_op jit(solution)/shard_map/xyj,ji->xyi/dot_general | solution.py:73
  91.0 1.3 collective-permute-start.12
  92.3 10.5 %collective-permute-start.13 = (f32[4,32,128]{2,1,0:T(8,128)S(1)}, f32[4,32,128]{2,1,0:T(8,128)S(1)}, u32[]{:S(2)}, u32[]{:S(2)}) collective-permute-start(f32[4,32,128]{2,1,0:T(8,128)S(1)} %get-tuple-element.30), channel_id=1, source_target_pairs={{0,32},{32,64},{64,96},{96,128},{128,160},{160,192},{192,224},{224... | collective-permute-start | bytes 196616 | tf_op jit(solution)/shard_map/ppermute | solution.py:43
  102.9 1.9 collective-permute-start.14
  104.8 3.9 %collective-permute-start.15 = (f32[16,4,128]{2,1,0:T(4,128)S(1)}, f32[16,4,128]{2,1,0:T(4,128)S(1)}, u32[]{:S(2)}, u32[]{:S(2)}) collective-permute-start(f32[16,4,128]{2,1,0:T(4,128)S(1)} %get-tuple-element.28), channel_id=1, source_target_pairs={{0,8},{8,16},{16,24},{1,9},{9,17},{17,25},{2,10},{10,18},{18,26},{... | collective-permute-start | bytes 98312 | tf_op jit(solution)/shard_map/ppermute | solution.py:43
  108.8 1.3 collective-permute-start.16
  110.2 4.6 %collective-permute-start.17 = (f32[16,32,4]{2,1,0:T(8,128)S(1)}, f32[16,32,4]{2,1,0:T(8,128)S(1)}, u32[]{:S(2)}, u32[]{:S(2)}) collective-permute-start(f32[16,32,4]{2,1,0:T(8,128)S(1)} %get-tuple-element.27), channel_id=1, source_target_pairs={{0,1},{1,2},{2,3},{3,4},{4,5},{5,6},{6,7},{8,9},{9,10},{10,11},{11... | collective-permute-start | bytes 24584 | tf_op jit(solution)/shard_map/ppermute | solution.py:43
  114.9 2.2 collective-permute-done.16
  117.1 3.6 %collective-permute-done.17 = f32[16,32,4]{2,1,0:T(8,128)S(1)} collective-permute-done((f32[16,32,4]{2,1,0:T(8,128)S(1)}, f32[16,32,4]{2,1,0:T(8,128)S(1)}, u32[]{:S(2)}, u32[]{:S(2)}) %collective-permute-start.17) | collective-permute-done | bytes 8224 | tf_op jit(solution)/shard_map/ppermute | solution.py:43
  121.2 0.6 multiply_subtract_fusion.1
  121.8 1.3 collective-permute-start.18
  123.1 14.0 %collective-permute-start.19 = (f32[4,32,128]{2,1,0:T(8,128)S(1)}, f32[4,32,128]{2,1,0:T(8,128)S(1)}, u32[]{:S(2)}, u32[]{:S(2)}) collective-permute-start(f32[4,32,128]{2,1,0:T(8,128)S(1)} %get-tuple-element.24), channel_id=1, source_target_pairs={{0,32},{32,64},{64,96},{96,128},{128,160},{160,192},{192,224},{224... | collective-permute-start | bytes 196616 | tf_op jit(solution)/shard_map/ppermute | solution.py:43
  137.1 1.9 collective-permute-start.20
  139.1 3.9 %collective-permute-start.21 = (f32[16,4,128]{2,1,0:T(4,128)S(1)}, f32[16,4,128]{2,1,0:T(4,128)S(1)}, u32[]{:S(2)}, u32[]{:S(2)}) collective-permute-start(f32[16,4,128]{2,1,0:T(4,128)S(1)} %get-tuple-element.22), channel_id=1, source_target_pairs={{0,8},{8,16},{16,24},{1,9},{9,17},{17,25},{2,10},{10,18},{18,26},{... | collective-permute-start | bytes 98312 | tf_op jit(solution)/shard_map/ppermute | solution.py:43
  143.1 1.3 collective-permute-start.22
  144.4 4.7 %collective-permute-start.23 = (f32[16,32,4]{2,1,0:T(8,128)S(1)}, f32[16,32,4]{2,1,0:T(8,128)S(1)}, u32[]{:S(2)}, u32[]{:S(2)}) collective-permute-start(f32[16,32,4]{2,1,0:T(8,128)S(1)} %get-tuple-element.21), channel_id=1, source_target_pairs={{0,1},{1,2},{2,3},{3,4},{4,5},{5,6},{6,7},{8,9},{9,10},{10,11},{11... | collective-permute-start | bytes 24584 | tf_op jit(solution)/shard_map/ppermute | solution.py:43
  149.3 5.0 %collective-permute-done.22 = f32[16,32,4]{2,1,0:T(8,128)S(1)} collective-permute-done((f32[16,32,4]{2,1,0:T(8,128)S(1)}, f32[16,32,4]{2,1,0:T(8,128)S(1)}, u32[]{:S(2)}, u32[]{:S(2)}) %collective-permute-start.22) | collective-permute-done | bytes 8224 | tf_op jit(solution)/shard_map/ppermute | solution.py:44
  154.4 0.5 select_maximum_fusion.1
  154.8 1.3 multiply_reduce_fusion
  156.1 17.0 %psum.35 = f32[]{:T(128)} all-reduce(f32[]{:T(128)} %get-tuple-element.2), channel_id=1, replica_groups=mesh['gx_0'=4,'gx_1'=2,'gx_2'=2,'gy'=4,'gz'=8] {'gx_0'}, use_global_device_ids=true, to_apply=%region_7.8 | all-reduce | flops 1 | bytes 8 | tf_op jit(solution)/shard_map/psum | solution.py:56
  173.1 14.3 %psum.36 = f32[]{:T(128)} all-reduce(f32[]{:T(128)} %psum.35), channel_id=1, replica_groups=mesh['gx_0'=4,'gx_1'=2,'gx_2'=2,'gy'=4,'gz'=8] {'gx_1'}, use_global_device_ids=true, to_apply=%region_8.9 | all-reduce | flops 1 | bytes 8 | tf_op jit(solution)/shard_map/psum | solution.py:56
  187.3 3.5 %psum.37 = f32[]{:T(128)} all-reduce(f32[]{:T(128)} %psum.36), channel_id=1, replica_groups=mesh['gx_0'=4,'gx_1'=2,'gx_2'=2,'gy'=4,'gz'=8] {'gx_2'}, use_global_device_ids=true, to_apply=%region_9.10 | all-reduce | flops 1 | bytes 8 | tf_op jit(solution)/shard_map/psum | solution.py:56
  190.8 9.7 %psum.38 = f32[]{:T(128)} all-reduce(f32[]{:T(128)} %psum.37), channel_id=1, replica_groups=mesh['gx_0'=4,'gx_1'=2,'gx_2'=2,'gy'=4,'gz'=8] {'gy'}, use_global_device_ids=true, to_apply=%region_10.11 | all-reduce | flops 1 | bytes 8 | tf_op jit(solution)/shard_map/psum | solution.py:56
  200.5 33.8 %psum.39 = f32[]{:T(128)} all-reduce(f32[]{:T(128)} %psum.38), channel_id=1, replica_groups=mesh['gx_0'=4,'gx_1'=2,'gx_2'=2,'gy'=4,'gz'=8] {'gz'}, use_global_device_ids=true, to_apply=%region_11.12 | all-reduce | flops 1 | bytes 8 | tf_op jit(solution)/shard_map/psum | solution.py:56
  235.0 0.7 broadcast_multiply_fusion
  (72 shorter events, 2.2 us)
Async XLA Ops:
  0.6 33.6 %copy-start = (f32[16,32,128]{2,1,0:T(8,128)S(1)}, f32[16,32,128]{2,1,0:T(8,128)}, u32[]{:S(2)}) copy-start(f32[16,32,128]{2,1,0:T(8,128)} %param.3) | copy-start | bytes 786436
  0.6 33.5 %collective-permute-start.6 = (f32[16,32,128]{2,1,0:T(8,128)}, f32[16,32,128]{2,1,0:T(8,128)S(1)}, u32[]{:S(2)}, u32[]{:S(2)}) collective-permute-start(f32[16,32,128]{2,1,0:T(8,128)} %param.3), channel_id=1, source_target_pairs={{0,32},{32,64},{64,96},{96,128},{128,160},{160,192},{192,224},{224... | collective-permute-start | bytes 786440 | tf_op jit(solution)/shard_map/ppermute | solution.py:26
  2.5 32.5 %collective-permute-start.7 = (f32[16,32,128]{2,1,0:T(8,128)}, f32[16,32,128]{2,1,0:T(8,128)S(1)}, u32[]{:S(2)}, u32[]{:S(2)}) collective-permute-start(f32[16,32,128]{2,1,0:T(8,128)} %param.3), channel_id=1, source_target_pairs={{32,0},{64,32},{96,64},{128,96},{160,128},{192,160},{224,192},{256... | collective-permute-start | bytes 786440 | tf_op jit(solution)/shard_map/ppermute | solution.py:28
  5.3 25.3 %collective-permute-start.1 = (f32[4,32,128]{2,1,0:T(8,128)S(1)}, f32[4,32,128]{2,1,0:T(8,128)S(1)}, u32[]{:S(2)}, u32[]{:S(2)}) collective-permute-start(f32[4,32,128]{2,1,0:T(8,128)S(1)} %get-tuple-element.41), channel_id=1, source_target_pairs={{0,32},{32,64},{64,96},{96,128},{128,160},{160,192},{192,224},{224... | collective-permute-start | bytes 196616 | tf_op jit(solution)/shard_map/ppermute | solution.py:43
  22.0 39.3 %collective-permute-start = (f32[4,32,128]{2,1,0:T(8,128)}, f32[4,32,128]{2,1,0:T(8,128)}, u32[]{:S(2)}, u32[]{:S(2)}) collective-permute-start(f32[4,32,128]{2,1,0:T(8,128)} %get-tuple-element.40), channel_id=1, source_target_pairs={{32,0},{64,32},{96,64},{128,96},{160,128},{192,160},{224,192},{256... | collective-permute-start | bytes 196616 | tf_op jit(solution)/shard_map/ppermute | solution.py:44
  24.1 19.1 %collective-permute-start.2 = (f32[16,4,128]{2,1,0:T(4,128)S(1)}, f32[16,4,128]{2,1,0:T(4,128)S(1)}, u32[]{:S(2)}, u32[]{:S(2)}) collective-permute-start(f32[16,4,128]{2,1,0:T(4,128)S(1)} %get-tuple-element.38), channel_id=1, source_target_pairs={{8,0},{16,8},{24,16},{9,1},{17,9},{25,17},{10,2},{18,10},{26,18},{... | collective-permute-start | bytes 98312 | tf_op jit(solution)/shard_map/ppermute | solution.py:44
  30.7 14.5 %collective-permute-start.3 = (f32[16,4,128]{2,1,0:T(4,128)S(1)}, f32[16,4,128]{2,1,0:T(4,128)S(1)}, u32[]{:S(2)}, u32[]{:S(2)}) collective-permute-start(f32[16,4,128]{2,1,0:T(4,128)S(1)} %get-tuple-element.39), channel_id=1, source_target_pairs={{0,8},{8,16},{16,24},{1,9},{9,17},{17,25},{2,10},{10,18},{18,26},{... | collective-permute-start | bytes 98312 | tf_op jit(solution)/shard_map/ppermute | solution.py:43
  35.0 0.7 copy-start.11
  35.0 7.6 %copy-start.1 = (f32[24,32,128]{2,1,0:T(8,128)}, f32[24,32,128]{2,1,0:T(8,128)S(1)}, u32[]{:S(2)}) copy-start(f32[24,32,128]{2,1,0:T(8,128)S(1)} %get-tuple-element.33) | copy-start | bytes 1179652
  35.8 15.2 %collective-permute-start.8 = (f32[48,16,128]{2,1,0:T(8,128)S(1)}, f32[48,16,128]{2,1,0:T(8,128)S(1)}, u32[]{:S(2)}, u32[]{:S(2)}) collective-permute-start(f32[48,16,128]{2,1,0:T(8,128)S(1)} %get-tuple-element.8), channel_id=1, source_target_pairs={{0,8},{8,16},{16,24},{1,9},{9,17},{17,25},{2,10},{10,18},{18,26},{... | collective-permute-start | bytes 1179656 | tf_op jit(solution)/shard_map/ppermute | solution.py:26
  39.3 11.7 %collective-permute-start.9 = (f32[48,16,128]{2,1,0:T(8,128)S(1)}, f32[48,16,128]{2,1,0:T(8,128)S(1)}, u32[]{:S(2)}, u32[]{:S(2)}) collective-permute-start(f32[48,16,128]{2,1,0:T(8,128)S(1)} %get-tuple-element.9), channel_id=1, source_target_pairs={{8,0},{16,8},{24,16},{9,1},{17,9},{25,17},{10,2},{18,10},{26,18},{... | collective-permute-start | bytes 1179656 | tf_op jit(solution)/shard_map/ppermute | solution.py:28
  43.3 19.5 %collective-permute-start.4 = (f32[16,32,4]{2,1,0:T(8,128)}, f32[16,32,4]{2,1,0:T(8,128)}, u32[]{:S(2)}, u32[]{:S(2)}) collective-permute-start(f32[16,32,4]{2,1,0:T(8,128)} %get-tuple-element.36), channel_id=1, source_target_pairs={{1,0},{2,1},{3,2},{4,3},{5,4},{6,5},{7,6},{9,8},{10,9},{11,10},{12... | collective-permute-start | bytes 24584 | tf_op jit(solution)/shard_map/ppermute | solution.py:44
  45.2 17.5 %collective-permute-start.5 = (f32[16,32,4]{2,1,0:T(8,128)}, f32[16,32,4]{2,1,0:T(8,128)}, u32[]{:S(2)}, u32[]{:S(2)}) collective-permute-start(f32[16,32,4]{2,1,0:T(8,128)} %get-tuple-element.37), channel_id=1, source_target_pairs={{0,1},{1,2},{2,3},{3,4},{4,5},{5,6},{6,7},{8,9},{9,10},{10,11},{11... | collective-permute-start | bytes 24584 | tf_op jit(solution)/shard_map/ppermute | solution.py:43
  55.6 10.6 %collective-permute-start.10 = (f32[48,64,16]{1,2,0:T(8,128)}, f32[48,64,16]{1,2,0:T(8,128)}, u32[]{:S(2)}, u32[]{:S(2)}) collective-permute-start(f32[48,64,16]{1,2,0:T(8,128)} %copy.9), channel_id=1, source_target_pairs={{0,1},{1,2},{2,3},{3,4},{4,5},{5,6},{6,7},{8,9},{9,10},{10,11},{11... | collective-permute-start | bytes 589832 | tf_op jit(solution)/shard_map/ppermute | solution.py:26
  59.8 10.0 %collective-permute-start.11 = (f32[48,64,16]{1,2,0:T(8,128)}, f32[48,64,16]{1,2,0:T(8,128)}, u32[]{:S(2)}, u32[]{:S(2)}) collective-permute-start(f32[48,64,16]{1,2,0:T(8,128)} %copy.10), channel_id=1, source_target_pairs={{1,0},{2,1},{3,2},{4,3},{5,4},{6,5},{7,6},{9,8},{10,9},{11,10},{12... | collective-permute-start | bytes 589832 | tf_op jit(solution)/shard_map/ppermute | solution.py:28
  72.4 2.7 %copy-start.8 = (f32[48,32]{0,1:T(8,128)S(1)}, f32[48,32]{0,1:T(8,128)}, u32[]{:S(2)}) copy-start(f32[48,32]{0,1:T(8,128)} %select_reduce_fusion.4) | copy-start | bytes 18436
  75.1 3.8 %copy-start.6 = (f32[64,48]{0,1:T(8,128)S(1)}, f32[64,48]{0,1:T(8,128)}, u32[]{:S(2)}) copy-start(f32[64,48]{0,1:T(8,128)} %select_reduce_fusion.2) | copy-start | bytes 36868
  81.6 1.6 copy-start.10
  83.2 2.0 copy-start.9
  83.3 3.1 %copy-start.2 = (f32[24,32,128]{2,1,0:T(8,128)S(1)}, f32[24,32,128]{2,1,0:T(8,128)}, u32[]{:S(2)}) copy-start(f32[24,32,128]{2,1,0:T(8,128)} %get-tuple-element.43) | copy-start | bytes 1179652
  83.3 3.1 %copy-start.3 = (f32[20,32,128]{2,1,0:T(8,128)S(1)}, f32[20,32,128]{2,1,0:T(8,128)}, u32[]{:S(2)}) copy-start(f32[20,32,128]{2,1,0:T(8,128)} %get-tuple-element.42) | copy-start | bytes 983044
  83.3 3.1 %copy-start.4 = (f32[24,4,128]{2,1,0:T(4,128)S(1)}, f32[24,4,128]{2,1,0:T(4,128)}, u32[]{:S(2)}) copy-start(f32[24,4,128]{2,1,0:T(4,128)} %pad.38) | copy-start | bytes 147460
  83.3 3.1 %copy-start.5 = (f32[24,4,128]{2,1,0:T(4,128)S(1)}, f32[24,4,128]{2,1,0:T(4,128)}, u32[]{:S(2)}) copy-start(f32[24,4,128]{2,1,0:T(4,128)} %pad.39) | copy-start | bytes 147460
  83.3 3.1 %copy-start.7 = (f32[144,128]{1,0:T(8,128)S(1)}, f32[144,128]{1,0:T(8,128)}, u32[]{:S(2)}) copy-start(f32[144,128]{1,0:T(8,128)} %select_reduce_fusion.1) | copy-start | bytes 221188
  83.3 3.1 %copy-start.12 = (f32[20,32,128]{2,1,0:T(8,128)S(1)}, f32[20,32,128]{2,1,0:T(8,128)}, u32[]{:S(2)}) copy-start(f32[20,32,128]{2,1,0:T(8,128)} %copy-done.11) | copy-start | bytes 983044
  83.3 3.1 %copy-start.13 = (f32[16,32,128]{2,1,0:T(8,128)S(1)}, f32[16,32,128]{2,1,0:T(8,128)}, u32[]{:S(2)}) copy-start(f32[16,32,128]{2,1,0:T(8,128)} %param.4) | copy-start | bytes 786436
  91.0 23.8 %collective-permute-start.12 = (f32[4,32,128]{2,1,0:T(8,128)S(1)}, f32[4,32,128]{2,1,0:T(8,128)S(1)}, u32[]{:S(2)}, u32[]{:S(2)}) collective-permute-start(f32[4,32,128]{2,1,0:T(8,128)S(1)} %get-tuple-element.31), channel_id=1, source_target_pairs={{32,0},{64,32},{96,64},{128,96},{160,128},{192,160},{224,192},{256... | collective-permute-start | bytes 196616 | tf_op jit(solution)/shard_map/ppermute | solution.py:44
  92.3 22.5 %collective-permute-start.13 = (f32[4,32,128]{2,1,0:T(8,128)S(1)}, f32[4,32,128]{2,1,0:T(8,128)S(1)}, u32[]{:S(2)}, u32[]{:S(2)}) collective-permute-start(f32[4,32,128]{2,1,0:T(8,128)S(1)} %get-tuple-element.30), channel_id=1, source_target_pairs={{0,32},{32,64},{64,96},{96,128},{128,160},{160,192},{192,224},{224... | collective-permute-start | bytes 196616 | tf_op jit(solution)/shard_map/ppermute | solution.py:43
  102.9 7.3 %collective-permute-start.14 = (f32[16,4,128]{2,1,0:T(4,128)S(1)}, f32[16,4,128]{2,1,0:T(4,128)S(1)}, u32[]{:S(2)}, u32[]{:S(2)}) collective-permute-start(f32[16,4,128]{2,1,0:T(4,128)S(1)} %get-tuple-element.29), channel_id=1, source_target_pairs={{8,0},{16,8},{24,16},{9,1},{17,9},{25,17},{10,2},{18,10},{26,18},{... | collective-permute-start | bytes 98312 | tf_op jit(solution)/shard_map/ppermute | solution.py:44
  104.8 10.0 %collective-permute-start.15 = (f32[16,4,128]{2,1,0:T(4,128)S(1)}, f32[16,4,128]{2,1,0:T(4,128)S(1)}, u32[]{:S(2)}, u32[]{:S(2)}) collective-permute-start(f32[16,4,128]{2,1,0:T(4,128)S(1)} %get-tuple-element.28), channel_id=1, source_target_pairs={{0,8},{8,16},{16,24},{1,9},{9,17},{17,25},{2,10},{10,18},{18,26},{... | collective-permute-start | bytes 98312 | tf_op jit(solution)/shard_map/ppermute | solution.py:43
  108.8 8.3 %collective-permute-start.16 = (f32[16,32,4]{2,1,0:T(8,128)S(1)}, f32[16,32,4]{2,1,0:T(8,128)S(1)}, u32[]{:S(2)}, u32[]{:S(2)}) collective-permute-start(f32[16,32,4]{2,1,0:T(8,128)S(1)} %get-tuple-element.26), channel_id=1, source_target_pairs={{1,0},{2,1},{3,2},{4,3},{5,4},{6,5},{7,6},{9,8},{10,9},{11,10},{12... | collective-permute-start | bytes 24584 | tf_op jit(solution)/shard_map/ppermute | solution.py:44
  110.2 10.5 %collective-permute-start.17 = (f32[16,32,4]{2,1,0:T(8,128)S(1)}, f32[16,32,4]{2,1,0:T(8,128)S(1)}, u32[]{:S(2)}, u32[]{:S(2)}) collective-permute-start(f32[16,32,4]{2,1,0:T(8,128)S(1)} %get-tuple-element.27), channel_id=1, source_target_pairs={{0,1},{1,2},{2,3},{3,4},{4,5},{5,6},{6,7},{8,9},{9,10},{10,11},{11... | collective-permute-start | bytes 24584 | tf_op jit(solution)/shard_map/ppermute | solution.py:43
  121.8 27.4 %collective-permute-start.18 = (f32[4,32,128]{2,1,0:T(8,128)S(1)}, f32[4,32,128]{2,1,0:T(8,128)S(1)}, u32[]{:S(2)}, u32[]{:S(2)}) collective-permute-start(f32[4,32,128]{2,1,0:T(8,128)S(1)} %get-tuple-element.25), channel_id=1, source_target_pairs={{32,0},{64,32},{96,64},{128,96},{160,128},{192,160},{224,192},{256... | collective-permute-start | bytes 196616 | tf_op jit(solution)/shard_map/ppermute | solution.py:44
  123.1 26.1 %collective-permute-start.19 = (f32[4,32,128]{2,1,0:T(8,128)S(1)}, f32[4,32,128]{2,1,0:T(8,128)S(1)}, u32[]{:S(2)}, u32[]{:S(2)}) collective-permute-start(f32[4,32,128]{2,1,0:T(8,128)S(1)} %get-tuple-element.24), channel_id=1, source_target_pairs={{0,32},{32,64},{64,96},{96,128},{128,160},{160,192},{192,224},{224... | collective-permute-start | bytes 196616 | tf_op jit(solution)/shard_map/ppermute | solution.py:43
  137.1 7.3 %collective-permute-start.20 = (f32[16,4,128]{2,1,0:T(4,128)S(1)}, f32[16,4,128]{2,1,0:T(4,128)S(1)}, u32[]{:S(2)}, u32[]{:S(2)}) collective-permute-start(f32[16,4,128]{2,1,0:T(4,128)S(1)} %get-tuple-element.23), channel_id=1, source_target_pairs={{8,0},{16,8},{24,16},{9,1},{17,9},{25,17},{10,2},{18,10},{26,18},{... | collective-permute-start | bytes 98312 | tf_op jit(solution)/shard_map/ppermute | solution.py:44
  139.1 10.1 %collective-permute-start.21 = (f32[16,4,128]{2,1,0:T(4,128)S(1)}, f32[16,4,128]{2,1,0:T(4,128)S(1)}, u32[]{:S(2)}, u32[]{:S(2)}) collective-permute-start(f32[16,4,128]{2,1,0:T(4,128)S(1)} %get-tuple-element.22), channel_id=1, source_target_pairs={{0,8},{8,16},{16,24},{1,9},{9,17},{17,25},{2,10},{10,18},{18,26},{... | collective-permute-start | bytes 98312 | tf_op jit(solution)/shard_map/ppermute | solution.py:43
  143.1 11.2 %collective-permute-start.22 = (f32[16,32,4]{2,1,0:T(8,128)S(1)}, f32[16,32,4]{2,1,0:T(8,128)S(1)}, u32[]{:S(2)}, u32[]{:S(2)}) collective-permute-start(f32[16,32,4]{2,1,0:T(8,128)S(1)} %get-tuple-element.20), channel_id=1, source_target_pairs={{1,0},{2,1},{3,2},{4,3},{5,4},{6,5},{7,6},{9,8},{10,9},{11,10},{12... | collective-permute-start | bytes 24584 | tf_op jit(solution)/shard_map/ppermute | solution.py:44
  144.4 9.9 %collective-permute-start.23 = (f32[16,32,4]{2,1,0:T(8,128)S(1)}, f32[16,32,4]{2,1,0:T(8,128)S(1)}, u32[]{:S(2)}, u32[]{:S(2)}) collective-permute-start(f32[16,32,4]{2,1,0:T(8,128)S(1)} %get-tuple-element.21), channel_id=1, source_target_pairs={{0,1},{1,2},{2,3},{3,4},{4,5},{5,6},{6,7},{8,9},{9,10},{10,11},{11... | collective-permute-start | bytes 24584 | tf_op jit(solution)/shard_map/ppermute | solution.py:43
where the time goes:
time: 237 us; the launch traced here: 236 us
  starting transfers between devices  94.4 us (40%)
  blocking collectives  78.2 us (33%)
  local copies, waits for them, and re-layouts  18.5 us (8%)
  matrix products  15.6 us (7%)
  other arithmetic  13.6 us (6%)
  waiting for transfers between devices  13.4 us (6%)
    psum x5, blocking collectives, by_axis(): return functools.reduce(lax.psum, axes, array)  78.2 us
    ppermute x9, starting transfers between devices, with_halo_2(): lax.ppermute(last, axis, up)  67 us
    dot_general x6, matrix products, smear(): jnp.einsum(FORMS[dim], padded, matrix, precision=lax.Precision.HIGHEST)  15.6 us
    ppermute x9, starting transfers between devices, with_halo_2(): lax.ppermute(leading, axis, [(b, a) for a, b in up])  13.9 us
    ppermute x3, starting transfers between devices, with_halo(): lax.ppermute(tail, axis, [(i, (i + 1) % count) for i in range(ends)])  8.37 us
    ppermute x9, waiting for transfers between devices, with_halo_2(): lax.ppermute(leading, axis, [(b, a) for a, b in up])  7.3 us
    ppermute x3, starting transfers between devices, with_halo(): lax.ppermute(head, axis, [((i + 1) % count, i) for i in range(ends)])  5.13 us
  transfers between devices with their start and end apart: 24, of which 5 were waited for; matrix products, arithmetic and copies ran while one was open for 9% of the time, Pallas kernels for 0%

commit v1 on v0

--- a/solution.py
+++ b/solution.py
@@ -1,5 +1,3 @@
-import functools
-
 import jax
 import jax.numpy as jnp
 from jax import lax
@@ -7,7 +5,7 @@
 from jax.sharding import PartitionSpec as P
 
 SUBSTEPS = 3
-GX_GY_GZ = ("gx_0", "gx_1", "gx_2", "gy", "gz")
+RINGS = (("gx_1", "gx_2", "gz"), ("gx_0", "gy"))
 GX = ("gx_0", "gx_1", "gx_2")
 
 
@@ -52,8 +50,12 @@
     return array
 
 
-def by_axis(array, axes):
-    return functools.reduce(lax.psum, axes, array)
+def spread_sum(row, groups):
+    for axes in groups:
+        count = lax.axis_size(axes)
+        copies = jnp.broadcast_to(row[None], (count, *row.shape))
+        row = jnp.sum(lax.all_to_all(copies, axes, 0, 0, tiled=True), axis=0)
+    return jnp.sum(row)
 
 
 def band_matrix(row, size_in, flip):
@@ -109,7 +111,7 @@
     for step in range(SUBSTEPS):
         near = with_halo_2(psi, ((GX, 0), ("gy", 1), ("gz", 2)), 4)
         psi = psi - 0.08 * (-0.5 * laplace(near) + potential * psi)
-    total = by_axis(jnp.sum(psi * psi), GX_GY_GZ)
+    total = spread_sum(jnp.sum(psi * psi, axis=(0, 1))[None], RINGS)
     count = float(psi.size * lax.axis_size(GX) * lax.axis_size("gy") * lax.axis_size("gz"))
     wave_next = psi * lax.rsqrt(total / count + 1e-06)
     return (wave_next, correlation)

time: 237 us -> 202 us (0.85)
  the two profiles are of different devices: /device:TPU:8 before, /device:TPU:2 now
where the time goes in v1:
time: 202 us; the launch traced here: 201 us
  starting transfers between devices  100 us (50%)
  blocking collectives  37.2 us (18%)
  local copies, waits for them, and re-layouts  18.6 us (9%)
  matrix products  15.4 us (8%)
  waiting for transfers between devices  13.9 us (7%)
  other arithmetic  13.7 us (7%)
    ppermute x9, starting transfers between devices, with_halo_2(): lax.ppermute(last, axis, up)  37.5 us
    all_to_all x2, blocking collectives, spread_sum(): row = jnp.sum(lax.all_to_all(copies, axes, 0, 0, tiled=True), axis=0)  37.2 us
    ppermute x9, starting transfers between devices, with_halo_2(): lax.ppermute(leading, axis, [(b, a) for a, b in up])  36.5 us
    ppermute x3, starting transfers between devices, with_halo(): lax.ppermute(head, axis, [((i + 1) % count, i) for i in range(ends)])  17.9 us
    dot_general x6, matrix products, smear(): jnp.einsum(FORMS[dim], padded, matrix, precision=lax.Precision.HIGHEST)  15.4 us
    ppermute x3, starting transfers between devices, with_halo(): lax.ppermute(tail, axis, [(i, (i + 1) % count) for i in range(ends)])  8.59 us
    ppermute x3, waiting for transfers between devices, with_halo(): lax.ppermute(head, axis, [((i + 1) % count, i) for i in range(ends)])  6.42 us
    ppermute x9, waiting for transfers between devices, with_halo_2(): lax.ppermute(last, axis, up)  4.78 us
  transfers between devices with their start and end apart: 24, of which 7 were waited for; matrix products, arithmetic and copies ran while one was open for 11% of the time, Pallas kernels for 0%

profile of v1, /device:TPU:2, one launch (start us, length us, event | category | flops | bytes accessed | tf_op | source)
XLA Modules:
  0.0 201.2 jit_solution(9684292511474023858)
XLA Ops:
  0.6 2.1 %collective-permute-start.6 = (f32[16,32,128]{2,1,0:T(8,128)}, f32[16,32,128]{2,1,0:T(8,128)S(1)}, u32[]{:S(2)}, u32[]{:S(2)}) collective-permute-start(f32[16,32,128]{2,1,0:T(8,128)} %param.3), channel_id=1, source_target_pairs={{0,32},{32,64},{64,96},{96,128},{128,160},{160,192},{192,224},{224... | collective-permute-start | bytes 786440 | tf_op jit(solution)/shard_map/ppermute | solution.py:24
  2.7 15.1 %collective-permute-start.7 = (f32[16,32,128]{2,1,0:T(8,128)}, f32[16,32,128]{2,1,0:T(8,128)S(1)}, u32[]{:S(2)}, u32[]{:S(2)}) collective-permute-start(f32[16,32,128]{2,1,0:T(8,128)} %param.3), channel_id=1, source_target_pairs={{32,0},{64,32},{96,64},{128,96},{160,128},{192,160},{224,192},{256... | collective-permute-start | bytes 786440 | tf_op jit(solution)/shard_map/ppermute | solution.py:26
  17.8 1.5 fusion.135
  19.4 2.6 %collective-permute-start.1 = (f32[4,32,128]{2,1,0:T(8,128)S(1)}, f32[4,32,128]{2,1,0:T(8,128)S(1)}, u32[]{:S(2)}, u32[]{:S(2)}) collective-permute-start(f32[4,32,128]{2,1,0:T(8,128)S(1)} %get-tuple-element.41), channel_id=1, source_target_pairs={{0,32},{32,64},{64,96},{96,128},{128,160},{160,192},{192,224},{224... | collective-permute-start | bytes 196616 | tf_op jit(solution)/shard_map/ppermute | solution.py:41
  22.0 12.6 %collective-permute-start = (f32[4,32,128]{2,1,0:T(8,128)}, f32[4,32,128]{2,1,0:T(8,128)}, u32[]{:S(2)}, u32[]{:S(2)}) collective-permute-start(f32[4,32,128]{2,1,0:T(8,128)} %get-tuple-element.40), channel_id=1, source_target_pairs={{32,0},{64,32},{96,64},{128,96},{160,128},{192,160},{224,192},{256... | collective-permute-start | bytes 196616 | tf_op jit(solution)/shard_map/ppermute | solution.py:42
  34.6 0.9 fusion.134
  35.4 1.3 collective-permute-start.2
  36.8 0.8 slice_bitcast_fusion
  37.6 0.7 select_reduce_fusion.2
  38.3 0.7 select_reduce_fusion.3
  39.4 0.8 select_reduce_fusion.1
  40.2 0.7 select_reduce_fusion.4
  40.9 4.5 %collective-permute-start.3 = (f32[16,4,128]{2,1,0:T(4,128)S(1)}, f32[16,4,128]{2,1,0:T(4,128)S(1)}, u32[]{:S(2)}, u32[]{:S(2)}) collective-permute-start(f32[16,4,128]{2,1,0:T(4,128)S(1)} %get-tuple-element.39), channel_id=1, source_target_pairs={{0,8},{8,16},{16,24},{1,9},{9,17},{17,25},{2,10},{10,18},{18,26},{... | collective-permute-start | bytes 98312 | tf_op jit(solution)/shard_map/ppermute | solution.py:41
  45.5 0.8 constant_dynamic-update-slice_fusion.8
  46.3 0.7 copy-done.11
  47.1 3.5 %collective-permute-start.8 = (f32[48,16,128]{2,1,0:T(8,128)S(1)}, f32[48,16,128]{2,1,0:T(8,128)S(1)}, u32[]{:S(2)}, u32[]{:S(2)}) collective-permute-start(f32[48,16,128]{2,1,0:T(8,128)S(1)} %get-tuple-element.8), channel_id=1, source_target_pairs={{0,8},{8,16},{16,24},{1,9},{9,17},{17,25},{2,10},{10,18},{18,26},{... | collective-permute-start | bytes 1179656 | tf_op jit(solution)/shard_map/ppermute | solution.py:24
  50.7 1.3 collective-permute-start.9
  52.0 0.9 fusion.133
  52.8 0.7 select_reduce_fusion.5
  53.5 1.3 collective-permute-start.4
  54.8 0.6 pad.38
  55.4 6.5 %collective-permute-start.5 = (f32[16,32,4]{2,1,0:T(8,128)}, f32[16,32,4]{2,1,0:T(8,128)}, u32[]{:S(2)}, u32[]{:S(2)}) collective-permute-start(f32[16,32,4]{2,1,0:T(8,128)} %get-tuple-element.37), channel_id=1, source_target_pairs={{0,1},{1,2},{2,3},{3,4},{4,5},{5,6},{6,7},{8,9},{9,10},{10,11},{11... | collective-permute-start | bytes 24584 | tf_op jit(solution)/shard_map/ppermute | solution.py:41
  61.9 0.6 pad.39
  62.5 1.5 collective-permute-done.9
  64.2 1.7 fusion.125
  65.9 2.6 %copy.17 = f32[48,64,16]{1,2,0:T(8,128)} copy(f32[48,64,16]{2,1,0:T(8,128)} %get-tuple-element.6) | data formatting | bytes 393216 | tf_op jit(solution)/shard_map/slice | solution.py:21
  68.5 3.0 %collective-permute-start.10 = (f32[48,64,16]{1,2,0:T(8,128)}, f32[48,64,16]{1,2,0:T(8,128)}, u32[]{:S(2)}, u32[]{:S(2)}) collective-permute-start(f32[48,64,16]{1,2,0:T(8,128)} %copy.17), channel_id=1, source_target_pairs={{0,1},{1,2},{2,3},{3,4},{4,5},{5,6},{6,7},{8,9},{9,10},{10,11},{11... | collective-permute-start | bytes 589832 | tf_op jit(solution)/shard_map/ppermute | solution.py:24
  71.5 1.2 copy.18
  72.8 1.5 collective-permute-start.11
  74.2 1.5 constant_dynamic-update-slice_fusion
  75.8 3.1 %select_maximum_fusion.5 = (f32[24,40,132]{2,1,0:T(8,128)}, f32[24,40,132]{2,1,0:T(8,128)}) fusion(f32[16,32,4]{2,1,0:T(8,128)} %collective-permute-done.4, f32[24,4,128]{2,1,0:T(4,128)} %pad.38, f32[24,32,128]{2,1,0:T(8,128)} %get-tuple-element.43, f32[24,4,128]{2,1,0:T(4,128)} %pad.39, f32[16,32,4]{2,1,0:T(8,128)} %collective-permute-done.5), kind=kLoop, calls=%fused_computation.23 | loop fusion | flops 1267200 | bytes 1521664 | tf_op jit(solution)/shard_map/concatenate | solution.py:48
  78.8 1.5 copy.19
  80.3 4.9 %collective-permute-done.11 = f32[48,64,16]{1,2,0:T(8,128)} collective-permute-done((f32[48,64,16]{1,2,0:T(8,128)}, f32[48,64,16]{1,2,0:T(8,128)}, u32[]{:S(2)}, u32[]{:S(2)}) %collective-permute-start.11) | collective-permute-done | bytes 196640 | tf_op jit(solution)/shard_map/ppermute | solution.py:26
  85.2 2.6 %copy.20 = f32[48,64,16]{2,1,0:T(8,128)} copy(f32[48,64,16]{1,2,0:T(8,128)} %collective-permute-done.11) | data formatting | bytes 393216 | tf_op jit(solution)/shard_map/ppermute | solution.py:26
  87.9 2.7 %maximum_multiply_fusion = f32[48,64,160]{2,1,0:T(8,128)S(1)} fusion(f32[48,64,16]{2,1,0:T(8,128)} %copy.20, f32[48,16,128]{2,1,0:T(8,128)S(1)} %collective-permute-done.9, f32[48,32,128]{2,1,0:T(8,128)S(1)} %constant_dynamic-update-slice_fusion.7, f32[48,16,128]{2,1,0:T(8,128)S(1)} %collective-permute-done.8, f32[48,64,16]{2,1,0:T(8,128)S(1)} %copy.19), kind=kLoop, calls=%fused_computation | loop fusion | flops 2457600 | bytes 3932160 | tf_op jit(solution)/shard_map/mul | solution.py:99
  90.6 3.8 %fusion = f32[32,64,160]{2,0,1:T(8,128)S(1)} fusion(f32[48,64,160]{2,1,0:T(8,128)S(1)} %maximum_multiply_fusion, f32[48,32]{0,1:T(8,128)S(1)} %copy-done.8), kind=kOutput, calls=%fused_computation.1 | convolution fusion | flops 188743680 | bytes 3282944 | tf_op jit(solution)/shard_map/jyz,ji->iyz/dot_general | solution.py:75
  94.4 2.7 %fusion.2 = f32[48,32,160]{2,0,1:T(8,128)S(1)} fusion(f32[32,64,160]{2,0,1:T(8,128)S(1)} %fusion, f32[64,48]{0,1:T(8,128)S(1)} %copy-done.6), kind=kOutput, calls=%fused_computation.5 | convolution fusion | flops 188743680 | bytes 2306048 | tf_op jit(solution)/shard_map/xjz,ji->xiz/dot_general | solution.py:75
  97.1 1.6 add_multiply_fusion
  98.8 1.9 fusion.6
  100.8 1.0 convolution_bitcast_fusion
  101.9 4.4 %fusion.73 = (f32[16,32,128]{2,1,0:T(8,128)S(1)}, f32[16,32,128]{2,1,0:T(8,128)S(1)}, f32[16,32,128]{2,1,0:T(8,128)}) fusion(f32[16,32,128]{2,1,0:T(8,128)S(1)} %copy-done, f32[24,32,128]{2,1,0:T(8,128)S(1)} %copy-done.2, f32[24,4,128]{2,1,0:T(4,128)S(1)} %copy-done.5, f32[24,4,128]{2,1,0:T(4,128)S(1)} %copy-done.4, f32[24,40,132]{2,1,0:T(8,128)} %get-tuple-element.15, ...), kind=kOutput, calls=%fused_computation.137 | convolution fusion | flops 116916224 | bytes 6627328 | tf_op jit(solution)/shard_map/xyj,ji->xyi/dot_general | solution.py:75
  106.3 4.6 %collective-permute-start.12 = (f32[4,32,128]{2,1,0:T(8,128)S(1)}, f32[4,32,128]{2,1,0:T(8,128)S(1)}, u32[]{:S(2)}, u32[]{:S(2)}) collective-permute-start(f32[4,32,128]{2,1,0:T(8,128)S(1)} %get-tuple-element.31), channel_id=1, source_target_pairs={{32,0},{64,32},{96,64},{128,96},{160,128},{192,160},{224,192},{256... | collective-permute-start | bytes 196616 | tf_op jit(solution)/shard_map/ppermute | solution.py:42
  110.9 1.9 collective-permute-start.13
  112.8 1.3 collective-permute-start.14
  114.1 4.5 %collective-permute-start.15 = (f32[16,4,128]{2,1,0:T(4,128)S(1)}, f32[16,4,128]{2,1,0:T(4,128)S(1)}, u32[]{:S(2)}, u32[]{:S(2)}) collective-permute-start(f32[16,4,128]{2,1,0:T(4,128)S(1)} %get-tuple-element.28), channel_id=1, source_target_pairs={{0,8},{8,16},{16,24},{1,9},{9,17},{17,25},{2,10},{10,18},{18,26},{... | collective-permute-start | bytes 98312 | tf_op jit(solution)/shard_map/ppermute | solution.py:41
  118.8 1.3 collective-permute-start.16
  120.1 4.6 %collective-permute-start.17 = (f32[16,32,4]{2,1,0:T(8,128)S(1)}, f32[16,32,4]{2,1,0:T(8,128)S(1)}, u32[]{:S(2)}, u32[]{:S(2)}) collective-permute-start(f32[16,32,4]{2,1,0:T(8,128)S(1)} %get-tuple-element.27), channel_id=1, source_target_pairs={{0,1},{1,2},{2,3},{3,4},{4,5},{5,6},{6,7},{8,9},{9,10},{10,11},{11... | collective-permute-start | bytes 24584 | tf_op jit(solution)/shard_map/ppermute | solution.py:41
  124.8 1.8 collective-permute-done.13
  127.1 1.5 collective-permute-done.17
  128.6 0.5 select_maximum_fusion.3
  129.0 0.6 multiply_subtract_fusion.1
  129.7 11.6 %collective-permute-start.18 = (f32[4,32,128]{2,1,0:T(8,128)S(1)}, f32[4,32,128]{2,1,0:T(8,128)S(1)}, u32[]{:S(2)}, u32[]{:S(2)}) collective-permute-start(f32[4,32,128]{2,1,0:T(8,128)S(1)} %get-tuple-element.25), channel_id=1, source_target_pairs={{32,0},{64,32},{96,64},{128,96},{160,128},{192,160},{224,192},{256... | collective-permute-start | bytes 196616 | tf_op jit(solution)/shard_map/ppermute | solution.py:42
  141.3 1.9 collective-permute-start.19
  143.2 1.3 collective-permute-start.20
  144.5 6.2 %collective-permute-start.21 = (f32[16,4,128]{2,1,0:T(4,128)S(1)}, f32[16,4,128]{2,1,0:T(4,128)S(1)}, u32[]{:S(2)}, u32[]{:S(2)}) collective-permute-start(f32[16,4,128]{2,1,0:T(4,128)S(1)} %get-tuple-element.22), channel_id=1, source_target_pairs={{0,8},{8,16},{16,24},{1,9},{9,17},{17,25},{2,10},{10,18},{18,26},{... | collective-permute-start | bytes 98312 | tf_op jit(solution)/shard_map/ppermute | solution.py:41
  150.9 1.3 collective-permute-start.22
  152.2 4.7 %collective-permute-start.23 = (f32[16,32,4]{2,1,0:T(8,128)S(1)}, f32[16,32,4]{2,1,0:T(8,128)S(1)}, u32[]{:S(2)}, u32[]{:S(2)}) collective-permute-start(f32[16,32,4]{2,1,0:T(8,128)S(1)} %get-tuple-element.21), channel_id=1, source_target_pairs={{0,1},{1,2},{2,3},{3,4},{4,5},{5,6},{6,7},{8,9},{9,10},{10,11},{11... | collective-permute-start | bytes 24584 | tf_op jit(solution)/shard_map/ppermute | solution.py:41
  157.1 2.2 %collective-permute-done.22 = f32[16,32,4]{2,1,0:T(8,128)S(1)} collective-permute-done((f32[16,32,4]{2,1,0:T(8,128)S(1)}, f32[16,32,4]{2,1,0:T(8,128)S(1)}, u32[]{:S(2)}, u32[]{:S(2)}) %collective-permute-start.22) | collective-permute-done | bytes 8224 | tf_op jit(solution)/shard_map/ppermute | solution.py:42
  159.3 1.5 collective-permute-done.23
  161.2 0.7 multiply_reduce_fusion
  161.9 23.9 %all_to_all.10 = f32[32,1,128]{2,1,0:T(1,128)S(1)} all-to-all(f32[32,1,128]{2,1,0:T(1,128)S(1)} %broadcast_in_dim.78), channel_id=1, replica_groups=mesh['gx_0'=4,'gx_1'=2,'gx_2'=2,'gy'=4,'gz'=8] {'gx_1','gx_2','gz'}, dimensions={0} | all-to-all | bytes 32768 | tf_op jit(solution)/shard_map/all_to_all | solution.py:57
  185.8 13.4 %all_to_all.11 = f32[16,1,128]{2,1,0:T(1,128)S(1)} all-to-all(f32[16,1,128]{2,1,0:T(1,128)S(1)} %broadcast_in_dim.79), channel_id=1, replica_groups=mesh['gx_0'=4,'gx_1'=2,'gx_2'=2,'gy'=4,'gz'=8] {'gx_0','gy'}, dimensions={0} | all-to-all | bytes 16384 | tf_op jit(solution)/shard_map/all_to_all | solution.py:57
  199.2 0.6 reduce_sum.93
  200.5 0.7 broadcast_multiply_fusion
  (73 shorter events, 2.2 us)
Async XLA Ops:
  0.6 44.9 %copy-start = (f32[16,32,128]{2,1,0:T(8,128)S(1)}, f32[16,32,128]{2,1,0:T(8,128)}, u32[]{:S(2)}) copy-start(f32[16,32,128]{2,1,0:T(8,128)} %param.3) | copy-start | bytes 786436
  0.6 44.8 %collective-permute-start.6 = (f32[16,32,128]{2,1,0:T(8,128)}, f32[16,32,128]{2,1,0:T(8,128)S(1)}, u32[]{:S(2)}, u32[]{:S(2)}) collective-permute-start(f32[16,32,128]{2,1,0:T(8,128)} %param.3), channel_id=1, source_target_pairs={{0,32},{32,64},{64,96},{96,128},{128,160},{160,192},{192,224},{224... | collective-permute-start | bytes 786440 | tf_op jit(solution)/shard_map/ppermute | solution.py:24
  2.7 43.6 %collective-permute-start.7 = (f32[16,32,128]{2,1,0:T(8,128)}, f32[16,32,128]{2,1,0:T(8,128)S(1)}, u32[]{:S(2)}, u32[]{:S(2)}) collective-permute-start(f32[16,32,128]{2,1,0:T(8,128)} %param.3), channel_id=1, source_target_pairs={{32,0},{64,32},{96,64},{128,96},{160,128},{192,160},{224,192},{256... | collective-permute-start | bytes 786440 | tf_op jit(solution)/shard_map/ppermute | solution.py:26
  19.4 21.5 %collective-permute-start.1 = (f32[4,32,128]{2,1,0:T(8,128)S(1)}, f32[4,32,128]{2,1,0:T(8,128)S(1)}, u32[]{:S(2)}, u32[]{:S(2)}) collective-permute-start(f32[4,32,128]{2,1,0:T(8,128)S(1)} %get-tuple-element.41), channel_id=1, source_target_pairs={{0,32},{32,64},{64,96},{96,128},{128,160},{160,192},{192,224},{224... | collective-permute-start | bytes 196616 | tf_op jit(solution)/shard_map/ppermute | solution.py:41
  22.0 52.3 %collective-permute-start = (f32[4,32,128]{2,1,0:T(8,128)}, f32[4,32,128]{2,1,0:T(8,128)}, u32[]{:S(2)}, u32[]{:S(2)}) collective-permute-start(f32[4,32,128]{2,1,0:T(8,128)} %get-tuple-element.40), channel_id=1, source_target_pairs={{32,0},{64,32},{96,64},{128,96},{160,128},{192,160},{224,192},{256... | collective-permute-start | bytes 196616 | tf_op jit(solution)/shard_map/ppermute | solution.py:42
  35.4 18.1 %collective-permute-start.2 = (f32[16,4,128]{2,1,0:T(4,128)S(1)}, f32[16,4,128]{2,1,0:T(4,128)S(1)}, u32[]{:S(2)}, u32[]{:S(2)}) collective-permute-start(f32[16,4,128]{2,1,0:T(4,128)S(1)} %get-tuple-element.38), channel_id=1, source_target_pairs={{8,0},{16,8},{24,16},{9,1},{17,9},{25,17},{10,2},{18,10},{26,18},{... | collective-permute-start | bytes 98312 | tf_op jit(solution)/shard_map/ppermute | solution.py:42
  40.9 14.5 %collective-permute-start.3 = (f32[16,4,128]{2,1,0:T(4,128)S(1)}, f32[16,4,128]{2,1,0:T(4,128)S(1)}, u32[]{:S(2)}, u32[]{:S(2)}) collective-permute-start(f32[16,4,128]{2,1,0:T(4,128)S(1)} %get-tuple-element.39), channel_id=1, source_target_pairs={{0,8},{8,16},{16,24},{1,9},{9,17},{17,25},{2,10},{10,18},{18,26},{... | collective-permute-start | bytes 98312 | tf_op jit(solution)/shard_map/ppermute | solution.py:41
  46.3 0.7 copy-start.11
  46.3 6.5 %copy-start.1 = (f32[24,32,128]{2,1,0:T(8,128)}, f32[24,32,128]{2,1,0:T(8,128)S(1)}, u32[]{:S(2)}) copy-start(f32[24,32,128]{2,1,0:T(8,128)S(1)} %get-tuple-element.33) | copy-start | bytes 1179652
  47.1 15.4 %collective-permute-start.8 = (f32[48,16,128]{2,1,0:T(8,128)S(1)}, f32[48,16,128]{2,1,0:T(8,128)S(1)}, u32[]{:S(2)}, u32[]{:S(2)}) collective-permute-start(f32[48,16,128]{2,1,0:T(8,128)S(1)} %get-tuple-element.8), channel_id=1, source_target_pairs={{0,8},{8,16},{16,24},{1,9},{9,17},{17,25},{2,10},{10,18},{18,26},{... | collective-permute-start | bytes 1179656 | tf_op jit(solution)/shard_map/ppermute | solution.py:24
  50.7 13.3 %collective-permute-start.9 = (f32[48,16,128]{2,1,0:T(8,128)S(1)}, f32[48,16,128]{2,1,0:T(8,128)S(1)}, u32[]{:S(2)}, u32[]{:S(2)}) collective-permute-start(f32[48,16,128]{2,1,0:T(8,128)S(1)} %get-tuple-element.9), channel_id=1, source_target_pairs={{8,0},{16,8},{24,16},{9,1},{17,9},{25,17},{10,2},{18,10},{26,18},{... | collective-permute-start | bytes 1179656 | tf_op jit(solution)/shard_map/ppermute | solution.py:26
  53.5 22.2 %collective-permute-start.4 = (f32[16,32,4]{2,1,0:T(8,128)}, f32[16,32,4]{2,1,0:T(8,128)}, u32[]{:S(2)}, u32[]{:S(2)}) collective-permute-start(f32[16,32,4]{2,1,0:T(8,128)} %get-tuple-element.36), channel_id=1, source_target_pairs={{1,0},{2,1},{3,2},{4,3},{5,4},{6,5},{7,6},{9,8},{10,9},{11,10},{12... | collective-permute-start | bytes 24584 | tf_op jit(solution)/shard_map/ppermute | solution.py:42
  55.4 20.3 %collective-permute-start.5 = (f32[16,32,4]{2,1,0:T(8,128)}, f32[16,32,4]{2,1,0:T(8,128)}, u32[]{:S(2)}, u32[]{:S(2)}) collective-permute-start(f32[16,32,4]{2,1,0:T(8,128)} %get-tuple-element.37), channel_id=1, source_target_pairs={{0,1},{1,2},{2,3},{3,4},{4,5},{5,6},{6,7},{8,9},{9,10},{10,11},{11... | collective-permute-start | bytes 24584 | tf_op jit(solution)/shard_map/ppermute | solution.py:41
  68.5 10.3 %collective-permute-start.10 = (f32[48,64,16]{1,2,0:T(8,128)}, f32[48,64,16]{1,2,0:T(8,128)}, u32[]{:S(2)}, u32[]{:S(2)}) collective-permute-start(f32[48,64,16]{1,2,0:T(8,128)} %copy.17), channel_id=1, source_target_pairs={{0,1},{1,2},{2,3},{3,4},{4,5},{5,6},{6,7},{8,9},{9,10},{10,11},{11... | collective-permute-start | bytes 589832 | tf_op jit(solution)/shard_map/ppermute | solution.py:24
  72.8 12.5 %collective-permute-start.11 = (f32[48,64,16]{1,2,0:T(8,128)}, f32[48,64,16]{1,2,0:T(8,128)}, u32[]{:S(2)}, u32[]{:S(2)}) collective-permute-start(f32[48,64,16]{1,2,0:T(8,128)} %copy.18), channel_id=1, source_target_pairs={{1,0},{2,1},{3,2},{4,3},{5,4},{6,5},{7,6},{9,8},{10,9},{11,10},{12... | collective-permute-start | bytes 589832 | tf_op jit(solution)/shard_map/ppermute | solution.py:26
  87.9 2.7 %copy-start.8 = (f32[48,32]{0,1:T(8,128)S(1)}, f32[48,32]{0,1:T(8,128)}, u32[]{:S(2)}) copy-start(f32[48,32]{0,1:T(8,128)} %select_reduce_fusion.4) | copy-start | bytes 18436
  90.6 3.8 %copy-start.6 = (f32[64,48]{0,1:T(8,128)S(1)}, f32[64,48]{0,1:T(8,128)}, u32[]{:S(2)}) copy-start(f32[64,48]{0,1:T(8,128)} %select_reduce_fusion.2) | copy-start | bytes 36868
  97.1 1.6 copy-start.10
  98.7 2.0 %copy-start.9 = (f32[48,32]{0,1:T(8,128)S(1)}, f32[48,32]{0,1:T(8,128)}, u32[]{:S(2)}) copy-start(f32[48,32]{0,1:T(8,128)} %select_reduce_fusion.3) | copy-start | bytes 18436
  98.8 3.1 %copy-start.2 = (f32[24,32,128]{2,1,0:T(8,128)S(1)}, f32[24,32,128]{2,1,0:T(8,128)}, u32[]{:S(2)}) copy-start(f32[24,32,128]{2,1,0:T(8,128)} %get-tuple-element.43) | copy-start | bytes 1179652
  98.8 3.1 %copy-start.3 = (f32[20,32,128]{2,1,0:T(8,128)S(1)}, f32[20,32,128]{2,1,0:T(8,128)}, u32[]{:S(2)}) copy-start(f32[20,32,128]{2,1,0:T(8,128)} %get-tuple-element.42) | copy-start | bytes 983044
  98.8 3.1 %copy-start.4 = (f32[24,4,128]{2,1,0:T(4,128)S(1)}, f32[24,4,128]{2,1,0:T(4,128)}, u32[]{:S(2)}) copy-start(f32[24,4,128]{2,1,0:T(4,128)} %pad.38) | copy-start | bytes 147460
  98.8 3.1 %copy-start.5 = (f32[24,4,128]{2,1,0:T(4,128)S(1)}, f32[24,4,128]{2,1,0:T(4,128)}, u32[]{:S(2)}) copy-start(f32[24,4,128]{2,1,0:T(4,128)} %pad.39) | copy-start | bytes 147460
  98.8 3.1 %copy-start.7 = (f32[144,128]{1,0:T(8,128)S(1)}, f32[144,128]{1,0:T(8,128)}, u32[]{:S(2)}) copy-start(f32[144,128]{1,0:T(8,128)} %select_reduce_fusion.1) | copy-start | bytes 221188
  98.8 3.1 %copy-start.12 = (f32[20,32,128]{2,1,0:T(8,128)S(1)}, f32[20,32,128]{2,1,0:T(8,128)}, u32[]{:S(2)}) copy-start(f32[20,32,128]{2,1,0:T(8,128)} %copy-done.11) | copy-start | bytes 983044
  98.8 3.1 %copy-start.13 = (f32[16,32,128]{2,1,0:T(8,128)S(1)}, f32[16,32,128]{2,1,0:T(8,128)}, u32[]{:S(2)}) copy-start(f32[16,32,128]{2,1,0:T(8,128)} %param.4) | copy-start | bytes 786436
  106.3 18.5 %collective-permute-start.12 = (f32[4,32,128]{2,1,0:T(8,128)S(1)}, f32[4,32,128]{2,1,0:T(8,128)S(1)}, u32[]{:S(2)}, u32[]{:S(2)}) collective-permute-start(f32[4,32,128]{2,1,0:T(8,128)S(1)} %get-tuple-element.31), channel_id=1, source_target_pairs={{32,0},{64,32},{96,64},{128,96},{160,128},{192,160},{224,192},{256... | collective-permute-start | bytes 196616 | tf_op jit(solution)/shard_map/ppermute | solution.py:42
  110.9 15.7 %collective-permute-start.13 = (f32[4,32,128]{2,1,0:T(8,128)S(1)}, f32[4,32,128]{2,1,0:T(8,128)S(1)}, u32[]{:S(2)}, u32[]{:S(2)}) collective-permute-start(f32[4,32,128]{2,1,0:T(8,128)S(1)} %get-tuple-element.30), channel_id=1, source_target_pairs={{0,32},{32,64},{64,96},{96,128},{128,160},{160,192},{192,224},{224... | collective-permute-start | bytes 196616 | tf_op jit(solution)/shard_map/ppermute | solution.py:41
  112.8 7.3 %collective-permute-start.14 = (f32[16,4,128]{2,1,0:T(4,128)S(1)}, f32[16,4,128]{2,1,0:T(4,128)S(1)}, u32[]{:S(2)}, u32[]{:S(2)}) collective-permute-start(f32[16,4,128]{2,1,0:T(4,128)S(1)} %get-tuple-element.29), channel_id=1, source_target_pairs={{8,0},{16,8},{24,16},{9,1},{17,9},{25,17},{10,2},{18,10},{26,18},{... | collective-permute-start | bytes 98312 | tf_op jit(solution)/shard_map/ppermute | solution.py:42
  114.1 10.6 %collective-permute-start.15 = (f32[16,4,128]{2,1,0:T(4,128)S(1)}, f32[16,4,128]{2,1,0:T(4,128)S(1)}, u32[]{:S(2)}, u32[]{:S(2)}) collective-permute-start(f32[16,4,128]{2,1,0:T(4,128)S(1)} %get-tuple-element.28), channel_id=1, source_target_pairs={{0,8},{8,16},{16,24},{1,9},{9,17},{17,25},{2,10},{10,18},{18,26},{... | collective-permute-start | bytes 98312 | tf_op jit(solution)/shard_map/ppermute | solution.py:41
  118.8 8.3 %collective-permute-start.16 = (f32[16,32,4]{2,1,0:T(8,128)S(1)}, f32[16,32,4]{2,1,0:T(8,128)S(1)}, u32[]{:S(2)}, u32[]{:S(2)}) collective-permute-start(f32[16,32,4]{2,1,0:T(8,128)S(1)} %get-tuple-element.26), channel_id=1, source_target_pairs={{1,0},{2,1},{3,2},{4,3},{5,4},{6,5},{7,6},{9,8},{10,9},{11,10},{12... | collective-permute-start | bytes 24584 | tf_op jit(solution)/shard_map/ppermute | solution.py:42
  120.1 8.4 %collective-permute-start.17 = (f32[16,32,4]{2,1,0:T(8,128)S(1)}, f32[16,32,4]{2,1,0:T(8,128)S(1)}, u32[]{:S(2)}, u32[]{:S(2)}) collective-permute-start(f32[16,32,4]{2,1,0:T(8,128)S(1)} %get-tuple-element.27), channel_id=1, source_target_pairs={{0,1},{1,2},{2,3},{3,4},{4,5},{5,6},{6,7},{8,9},{9,10},{10,11},{11... | collective-permute-start | bytes 24584 | tf_op jit(solution)/shard_map/ppermute | solution.py:41
  129.7 27.2 %collective-permute-start.18 = (f32[4,32,128]{2,1,0:T(8,128)S(1)}, f32[4,32,128]{2,1,0:T(8,128)S(1)}, u32[]{:S(2)}, u32[]{:S(2)}) collective-permute-start(f32[4,32,128]{2,1,0:T(8,128)S(1)} %get-tuple-element.25), channel_id=1, source_target_pairs={{32,0},{64,32},{96,64},{128,96},{160,128},{192,160},{224,192},{256... | collective-permute-start | bytes 196616 | tf_op jit(solution)/shard_map/ppermute | solution.py:42
  141.3 15.7 %collective-permute-start.19 = (f32[4,32,128]{2,1,0:T(8,128)S(1)}, f32[4,32,128]{2,1,0:T(8,128)S(1)}, u32[]{:S(2)}, u32[]{:S(2)}) collective-permute-start(f32[4,32,128]{2,1,0:T(8,128)S(1)} %get-tuple-element.24), channel_id=1, source_target_pairs={{0,32},{32,64},{64,96},{96,128},{128,160},{160,192},{192,224},{224... | collective-permute-start | bytes 196616 | tf_op jit(solution)/shard_map/ppermute | solution.py:41
  143.2 9.0 %collective-permute-start.20 = (f32[16,4,128]{2,1,0:T(4,128)S(1)}, f32[16,4,128]{2,1,0:T(4,128)S(1)}, u32[]{:S(2)}, u32[]{:S(2)}) collective-permute-start(f32[16,4,128]{2,1,0:T(4,128)S(1)} %get-tuple-element.23), channel_id=1, source_target_pairs={{8,0},{16,8},{24,16},{9,1},{17,9},{25,17},{10,2},{18,10},{26,18},{... | collective-permute-start | bytes 98312 | tf_op jit(solution)/shard_map/ppermute | solution.py:42
  144.5 12.4 %collective-permute-start.21 = (f32[16,4,128]{2,1,0:T(4,128)S(1)}, f32[16,4,128]{2,1,0:T(4,128)S(1)}, u32[]{:S(2)}, u32[]{:S(2)}) collective-permute-start(f32[16,4,128]{2,1,0:T(4,128)S(1)} %get-tuple-element.22), channel_id=1, source_target_pairs={{0,8},{8,16},{16,24},{1,9},{9,17},{17,25},{2,10},{10,18},{18,26},{... | collective-permute-start | bytes 98312 | tf_op jit(solution)/shard_map/ppermute | solution.py:41
  150.9 8.4 %collective-permute-start.22 = (f32[16,32,4]{2,1,0:T(8,128)S(1)}, f32[16,32,4]{2,1,0:T(8,128)S(1)}, u32[]{:S(2)}, u32[]{:S(2)}) collective-permute-start(f32[16,32,4]{2,1,0:T(8,128)S(1)} %get-tuple-element.20), channel_id=1, source_target_pairs={{1,0},{2,1},{3,2},{4,3},{5,4},{6,5},{7,6},{9,8},{10,9},{11,10},{12... | collective-permute-start | bytes 24584 | tf_op jit(solution)/shard_map/ppermute | solution.py:42
  152.2 8.6 %collective-permute-start.23 = (f32[16,32,4]{2,1,0:T(8,128)S(1)}, f32[16,32,4]{2,1,0:T(8,128)S(1)}, u32[]{:S(2)}, u32[]{:S(2)}) collective-permute-start(f32[16,32,4]{2,1,0:T(8,128)S(1)} %get-tuple-element.21), channel_id=1, source_target_pairs={{0,1},{1,2},{2,3},{3,4},{4,5},{5,6},{6,7},{8,9},{9,10},{10,11},{11... | collective-permute-start | bytes 24584 | tf_op jit(solution)/shard_map/ppermute | solution.py:41

commit v2 on v1

v2 whole, which is shorter than its diff:
```python
import functools

import jax
import jax.numpy as jnp
from jax import lax
from jax.experimental import pallas as pl
from jax.experimental.pallas import tpu as pltpu
from jax.sharding import Mesh
from jax.sharding import PartitionSpec as P

RINGS = (("gx_1", "gx_2", "gz"), ("gx_0", "gy"))
GX = ("gx_0", "gx_1", "gx_2")
LAP_COEF = (-205.0 / 72.0, 8.0 / 5.0, -1.0 / 5.0, 8.0 / 315.0, -1.0 / 560.0)
STEP = 0.08
F32 = jnp.float32
LANES = 128


def lane_ids(shape):
    return lax.broadcasted_iota(jnp.int32, shape, len(shape) - 1)


def pack(rows_of, count, cells, offset):
    lanes = lane_ids((8, LANES))
    first = last = None
    for q in range(count):
        at = offset + cells * q
        here = (lanes >= at) & (lanes < at + cells)
        rows = rows_of(q)
        head = pltpu.roll(rows, at, 1) if at else rows
        tail = pltpu.roll(rows, (at + cells) % LANES, 1)
        first = jnp.where(here, head, 0.0 if first is None else first)
        last = jnp.where(here, tail, 0.0 if last is None else last)
    return first, last


def unpack(right, left, at, cells):
    lanes = lane_ids((8, LANES))
    high = pltpu.roll(right, (LANES - at) % LANES, 1) if at % LANES else right
    low = pltpu.roll(left, (2 * LANES - cells - at) % LANES, 1)
    return jnp.where(lanes < cells, high, jnp.where(lanes >= LANES - cells, low, 0.0))


def call(body, outs, scratch, *args, scalars=0, flops=0, after=()):
    specs = [pl.BlockSpec(memory_space=pltpu.SMEM)] * scalars
    specs += [pl.BlockSpec(memory_space=pltpu.VMEM)] * (len(args) - scalars)
    specs += [pl.BlockSpec(memory_space=pl.ANY)] * len(after)
    inputs = len(args)
    if after:
        inner = body

        def body(*refs):
            inner(*refs[:inputs], *refs[inputs + len(after) :])

    shapes = [jax.ShapeDtypeStruct(s, F32) for s in outs]
    nbytes = 4 * sum(a.size for a in args) + 4 * sum(s.size for s in shapes)
    return pl.pallas_call(
        body,
        out_shape=shapes,
        in_specs=specs,
        out_specs=[pl.BlockSpec(memory_space=pltpu.VMEM)] * len(outs),
        scratch_shapes=[pltpu.VMEM(s, F32) for s in scratch],
        compiler_params=pltpu.CompilerParams(vmem_limit_bytes=40 * 1024 * 1024),
        cost_estimate=pl.CostEstimate(flops=flops, bytes_accessed=nbytes, transcendentals=0),
    )(*args, *after)


def rows_from(x, q, low, mid, high, edge):
    middle = mid.shape[1] // 8
    if q < edge:
        return low[x, 8 * q : 8 * q + 8, :]
    if q < edge + middle:
        return mid[x, 8 * (q - edge) : 8 * (q - edge) + 8, :]
    return high[x, 8 * (q - edge - middle) : 8 * (q - edge - middle) + 8, :]


def pack_wave(mid, low, high, first, last):
    def plane(x, carry):
        first[x], last[x] = pack(lambda q: rows_from(x, q, low, mid, high, 2), 8, 16, 0)
        return carry

    lax.fori_loop(0, mid.shape[0], plane, 0)


def assemble(own, rim, mid, low, high, right, left):
    own[:, 0:16, :] = low[...]
    own[:, 16:48, :] = mid[...]
    own[:, 48:64, :] = high[...]

    def plane(x, carry):
        for q in range(8):
            rim[x, 8 * q : 8 * q + 8, :] = unpack(right[x], left[x], 16 * q, 16)
        return carry

    lax.fori_loop(0, mid.shape[0], plane, 0)


def halves(x):
    top = x.astype(jnp.bfloat16)
    return top, (x - top.astype(F32)).astype(jnp.bfloat16)


def times(x, matrix_halves):
    top, rest = halves(x)
    big, small = matrix_halves
    dot = functools.partial(jnp.dot, preferred_element_type=F32)
    return dot(top, big) + (dot(top, small) + dot(rest, big))


def slide(src, dst, taps, groups):
    count = dst.shape[0]

    def column(g, carry):
        rows = pl.ds(pl.multiple_of(8 * g, 8), 8)
        sums = {}
        for j in range(count + 16):
            value = src[j, rows, :]
            for a in range(17):
                i = j - a
                if 0 <= i < count:
                    term = taps[a] * value
                    sums[i] = sums[i] + term if a else term
            if j >= 16:
                dst[j - 16, rows, :] = sums.pop(j - 16)
        return carry

    lax.fori_loop(0, groups, column, 0)


def along_rows(src, x, taps, count):
    total = taps[0] * src[x, 0:count, :]
    for b in range(1, 17):
        total = total + taps[b] * src[x, b : b + count, :]
    return total


def smears(
    flags, weights, mid, low, high, right, left, spread, gather, external, corr, potential, outward, inward,
    own, rim, g_own, g_rim, h_own, h_rim, s_own, s_rim, c_own, t_own, t_rim, u_own, u_rim,
):
    assemble(own, rim, mid, low, high, right, left)
    spread_halves = halves(spread[...])
    per = 4

    def along_z(k, carry):
        planes = pl.ds(k * per, per)
        a = own[planes].reshape(per * 64, LANES)
        b = rim[planes].reshape(per * 64, LANES)
        both = jnp.concatenate([a * a, b * b], axis=1)
        out = times(both, spread_halves)
        g_own[planes] = out[:, :LANES].reshape(per, 64, LANES)
        g_rim[planes] = out[:, LANES:].reshape(per, 64, LANES)
        return carry

    lax.fori_loop(0, 48 // per, along_z, 0)
    x_taps = [weights[0, a] for a in range(17)]
    y_taps = [weights[1, a] for a in range(17)]
    slide(g_own, h_own, x_taps, 8)
    slide(g_rim, h_rim, x_taps, 8)

    def source(x, carry):
        for h, e, s in ((h_own, own, s_own), (h_rim, rim, s_rim)):
            coarse = along_rows(h, x, y_taps, 48)
            wave = e[x + 8, 8:56, :]
            density = wave * wave
            s[x] = -1.0 * density * coarse + 0.5 * density * coarse * coarse
            if h is h_own:
                c_own[x] = coarse
        return carry

    lax.fori_loop(0, 32, source, 0)
    slide(s_own, t_own, x_taps[::-1], 6)
    slide(s_rim, t_rim, x_taps[::-1], 6)

    def back(x, carry):
        u_own[x] = along_rows(t_own, x, y_taps[::-1], 32)
        u_rim[x] = along_rows(t_rim, x, y_taps[::-1], 32)
        return carry

    lax.fori_loop(0, 16, back, 0)
    gather_halves = halves(gather[...])
    for k in range(2):
        planes = pl.ds(8 * k, 8)
        both = jnp.concatenate([u_own[planes].reshape(256, LANES), u_rim[planes].reshape(256, LANES)], axis=1)
        smeared = times(both, gather_halves).reshape(8, 32, LANES)
        coarse = c_own[pl.ds(8 + 8 * k, 8), 8:40, :]
        value = -0.5 * coarse * coarse + 0.5 / 3.0 * coarse * coarse * coarse + smeared
        corr[planes] = value
        potential[planes] = value + external[planes]
    upper = flags[0]
    outward[...] = potential[pl.ds(8 * upper, 8)]
    inward[...] = potential[pl.ds(8 * (1 - upper), 8)]


def laplace(own, rim, x, start, count, with_rim):
    lanes = lane_ids((count, LANES))
    rows = slice(start, start + count)
    centers = own[x, rows, :], rim[x, rows, :]
    totals = []
    for ref, other in ((0, 1), (1, 0))[: 2 if with_rim else 1]:
        field = (own, rim)[ref]
        center = centers[ref]
        total = (1.0 + 0.5 * STEP * 3.0 * LAP_COEF[0]) * center
        for k in range(1, 5):
            near = field[x + k, rows, :] + field[x - k, rows, :]
            near = near + (field[x, start + k : start + k + count, :] + field[x, start - k : start - k + count, :])
            ahead = jnp.where(
                lanes < LANES - k, pltpu.roll(center, LANES - k, 1), pltpu.roll(centers[other], LANES - k, 1)
            )
            behind = jnp.where(lanes >= k, pltpu.roll(center, k, 1), pltpu.roll(centers[other], k, 1))
            total = total + (0.5 * STEP * LAP_COEF[k]) * (near + (ahead + behind))
        totals.append(total)
    return totals


def first_step(mid, low, high, right, left, p_own, p_rim, q_own, q_rim, own, rim):
    assemble(own, rim, mid, low, high, right, left)

    def plane(x, carry):
        p_own[x], p_rim[x] = laplace(own, rim, x + 8, 8, 48, True)
        q_own[x] = own[x + 8, 8:56, :]
        q_rim[x] = rim[x + 8, 8:56, :]
        return carry

    lax.fori_loop(0, 32, plane, 0)


def join_planes(flags, mid, outer, inner, joined, head, tail):
    upper = flags[0]
    joined[8:24] = mid[...]

    @pl.when(upper == 0)
    def _():
        joined[0:8] = outer[...]
        joined[24:32] = inner[...]

    @pl.when(upper != 0)
    def _():
        joined[0:8] = inner[...]
        joined[24:32] = outer[...]

    head[...] = joined[:, 0:8, :]
    tail[...] = joined[:, 24:32, :]


def pack_potential(mid, low, high, first, last):
    def plane(x, carry):
        one = pack(lambda q: rows_from(x, q, low, mid, high, 1), 6, 8, 0)
        two = pack(lambda q: rows_from(x + 16, q, low, mid, high, 1), 6, 8, 48)
        first[x] = one[0] + two[0]
        last[x] = one[1] + two[1]
        return carry

    lax.fori_loop(0, 16, plane, 0)


def last_steps(
    flags, p_own, p_rim, q_own, q_rim, mid, low, high, right, left, psi, squares,
    v_own, v_rim, a_own, a_rim, b_own, b_rim,
):
    v_own[:, 0:8, :] = low[...]
    v_own[:, 8:40, :] = mid[...]
    v_own[:, 40:48, :] = high[...]

    def rims(x, carry):
        for q in range(6):
            v_rim[x, 8 * q : 8 * q + 8, :] = unpack(right[x], left[x], 8 * q, 8)
            v_rim[x + 16, 8 * q : 8 * q + 8, :] = unpack(right[x], left[x], 48 + 8 * q, 8)
        return carry

    lax.fori_loop(0, 16, rims, 0)

    def masks(count, edge):
        rows = lax.broadcasted_iota(jnp.int32, (count, LANES), 0) - edge
        lanes = lane_ids((count, LANES))
        in_rows = (rows >= flags[3]) & (rows < flags[4])
        in_rim = ((lanes >= 64) & (flags[5] != 0)) | ((lanes < 64) & (flags[6] != 0))
        rows_one = jnp.where(in_rows, 1.0, 0.0)
        return rows_one, jnp.where(in_rim, rows_one, 0.0)

    def inside(x, edge):
        return jnp.where((x - edge >= flags[1]) & (x - edge < flags[2]), 1.0, 0.0)

    keep_own, keep_rim = masks(48, 8)

    def one(x, carry):
        keep = inside(x, 8)
        a_own[x] = (p_own[x] - STEP * v_own[x] * q_own[x]) * (keep * keep_own)
        a_rim[x] = (p_rim[x] - STEP * v_rim[x] * q_rim[x]) * (keep * keep_rim)
        return carry

    lax.fori_loop(0, 32, one, 0)
    mid_own, mid_rim = masks(40, 4)

    def two(x, carry):
        keep = inside(x, 4)
        own, rim = laplace(a_own, a_rim, x + 4, 4, 40, True)
        v = v_own[x + 4, 4:44, :] * a_own[x + 4, 4:44, :]
        b_own[x] = (own - STEP * v) * (keep * mid_own)
        v = v_rim[x + 4, 4:44, :] * a_rim[x + 4, 4:44, :]
        b_rim[x] = (rim - STEP * v) * (keep * mid_rim)
        return carry

    lax.fori_loop(0, 24, two, 0)

    def three(x, total):
        (own,) = laplace(b_own, b_rim, x + 4, 4, 32, False)
        value = own - STEP * (v_own[x + 8, 8:40, :] * b_own[x + 4, 4:36, :])
        psi[x] = value
        return total + value * value

    total = lax.fori_loop(0, 16, three, jnp.zeros((32, LANES), F32))
    squares[...] = jnp.sum(total, axis=0, keepdims=True)


def band(row, flip):
    places = jnp.arange(256, dtype=jnp.int32)
    places = jnp.where(places < 192, places, places - 256)
    into = places[:LANES] if flip else places
    margin = 0 if flip else 8
    offset = (into[None, :] - places[:, None] if flip else places[:, None] - into[None, :]) + 8
    valid = (into >= -margin) & (into < LANES + margin)
    reach = (places >= -margin - 8) & (places < LANES + margin + 8)
    hits = (offset[:, :, None] == jnp.arange(17, dtype=jnp.int32)) & (valid[None, :] & reach[:, None])[:, :, None]
    return jnp.sum(jnp.where(hits, row, 0.0), axis=2)


def swap_x(outward, inward):
    count = lax.axis_size(GX)
    far = [p for k in range(1, count - 1, 2) for p in ((k, k + 1), (k + 1, k))]
    near = [(k, k ^ 1) for k in range(count)]
    return lax.ppermute(outward, GX, far), lax.ppermute(inward, GX, near)


def shift(head, tail, axis):
    ends = lax.axis_size(axis) - 1
    low = lax.ppermute(tail, axis, [(i, i + 1) for i in range(ends)])
    high = lax.ppermute(head, axis, [(i + 1, i) for i in range(ends)])
    return low, high


def spread_sum(row, groups):
    for axes in groups:
        count = lax.axis_size(axes)
        copies = jnp.broadcast_to(row[None], (count, *row.shape))
        row = jnp.sum(lax.all_to_all(copies, axes, 0, 0, tiled=True), axis=0)
    return jnp.sum(row)


def shards(wave, external, weights):
    at = [lax.axis_index(axis) for axis in (GX, "gy", "gz")]
    last = [at[d] == lax.axis_size(axis) - 1 for d, axis in enumerate((GX, "gy", "gz"))]
    far = 1 << 20
    flags = jnp.stack(
        [
            lax.axis_index("gx_2"),
            jnp.where(at[0] == 0, 0, -far),
            jnp.where(last[0], wave.shape[0], far),
            jnp.where(at[1] == 0, 0, -far),
            jnp.where(last[1], wave.shape[1], far),
            jnp.where(at[2] == 0, 0, 1),
            jnp.where(last[2], 0, 1),
        ]
    ).astype(jnp.int32)
    upper = lax.axis_index("gx_2")
    outer, inner = swap_x(wave, wave)
    mid = jnp.concatenate(
        [jnp.where(upper == 0, outer, inner), wave, jnp.where(upper == 0, inner, outer)], axis=0
    )
    low, high = shift(mid[:, :16, :], mid[:, 16:, :], "gy")
    first, final = call(pack_wave, [(48, 8, LANES)] * 2, [], mid, low, high)
    left, right = shift(first, final, "gz")

    wide, narrow, thin = (48, 64, LANES), (32, 64, LANES), (32, 48, LANES)
    block = wave.shape
    corr, potential, outward, inward = call(
        smears,
        [block, block, (8, 32, LANES), (8, 32, LANES)],
        [wide] * 4 + [narrow] * 2 + [thin] * 3 + [(16, 48, LANES)] * 2 + [block] * 2,
        flags, weights, mid, low, high, right, left, band(weights[2], False), band(weights[2], True), external,
        scalars=2, flops=4 * 10**9,
    )
    v_outer, v_inner = swap_x(outward, inward)
    fields = call(first_step, [thin] * 4, [wide] * 2, mid, low, high, right, left, flops=2 * 10**9)
    v_mid, head, tail = call(
        join_planes,
        [(32, 32, LANES), (32, 8, LANES), (32, 8, LANES)],
        [],
        flags, potential, v_outer, v_inner,
        scalars=1, after=fields[:1],
    )
    v_low, v_high = shift(head, tail, "gy")
    first, final = call(pack_potential, [(16, 8, LANES)] * 2, [], v_mid, v_low, v_high)
    v_left, v_right = shift(first, final, "gz")
    psi, squares = call(
        last_steps,
        [block, (1, LANES)],
        [thin] * 4 + [(24, 40, LANES)] * 2,
        flags, *fields, v_mid, v_low, v_high, v_right, v_left,
        scalars=1, flops=2 * 10**9,
    )
    total = spread_sum(squares, RINGS)
    count = float(psi.size * lax.axis_size(GX) * lax.axis_size("gy") * lax.axis_size("gz"))
    wave_next = psi * lax.rsqrt(total / count + 1e-06)
    return (wave_next, corr)


def solution(mesh):
    torus = Mesh(
        mesh.devices.reshape(4, 2, 2, mesh.shape["gy"], mesh.shape["gz"]),
        ("gx_0", "gx_1", "gx_2", "gy", "gz"),
    )
    placed = (P(GX, "gy", "gz"), P(GX, "gy", "gz"), P())
    return jax.shard_map(
        shards,
        mesh=torus,
        in_specs=placed,
        out_specs=(P(GX, "gy", "gz"), P(GX, "gy", "gz")),
        check_vma=False,
    )
```

time: 202 us -> 180 us (0.89)
  starting transfers between devices: 100 us -> 58.1 us
  Pallas kernels: 0 us -> 40.3 us
  waiting for transfers between devices: 13.9 us -> 36.6 us
  local copies, waits for them, and re-layouts: 18.6 us -> 0.86 us
  matrix products: 15.4 us -> 0 us
  other arithmetic: 13.7 us -> 3.27 us
    ppermute x24 -> x12, starting transfers between devices: 100 us -> 58.1 us  [the longest x4 34.2 us: swap_x(): return (lax.ppermute(outward, GX, far), lax.ppermute(inward, GX, near))]
    pallas_call x0 -> x6, Pallas kernels: none -> 40.3 us  [call(): pl.pallas_call(body, out_shape=shapes, in_specs=specs, out_specs=[pl.Bloc...]
    ppermute x24 -> x12, waiting for transfers between devices: 13.9 us -> 36.6 us  [the longest x4 18.8 us: swap_x(): return (lax.ppermute(outward, GX, far), lax.ppermute(inward, GX, near))]
    dot_general x6 -> x0, matrix products: 15.4 us -> none  [smear(): jnp.einsum(FORMS[dim], padded, matrix, precision=lax.Precision.HIGHEST)]
    slice x13 -> x2, local copies, waits for them, and re-layouts: 9.2 us -> 0.06 us  [the longest x1 0.05 us: shards(): low, high = shift(mid[:, :16, :], mid[:, 16:, :], 'gy')]
    concatenate x6 -> x1, other arithmetic: 4.27 us -> 0.05 us  [shards(): jnp.concatenate([jnp.where(upper == 0, outer, inner), wave, jnp.where(upp...]
    ppermute x2 -> x0, local copies, waits for them, and re-layouts: 4.12 us -> none  [the longest x1 2.65 us: with_halo(): lax.ppermute(head, axis, [((i + 1) % count, i) for i in range(ends)])]
    reduce_sum x7 -> x2, other arithmetic: 4.66 us -> 1.42 us  [band(): return jnp.sum(jnp.where(hits, row, 0.0), axis=2)]
  transfers between devices with their start and end apart: 24 -> 12, of which waited for: 7 -> 9; matrix products, arithmetic and copies ran while one was open for 11% -> 1% of each run, Pallas kernels for 0% -> 6%
where the time goes in v2:
time: 180 us; the launch traced here: 179 us
  starting transfers between devices  58.1 us (32%)
  Pallas kernels  40.3 us (22%)
  blocking collectives  38.5 us (21%)
  waiting for transfers between devices  36.6 us (20%)
  other arithmetic  3.27 us (2%)
    pallas_call x6, Pallas kernels, call(): pl.pallas_call(body, out_shape=shapes, in_specs=specs, out_specs=[pl.Bloc...  40.3 us
    all_to_all x2, blocking collectives, spread_sum(): row = jnp.sum(lax.all_to_all(copies, axes, 0, 0, tiled=True), axis=0)  38.5 us
    ppermute x4, starting transfers between devices, swap_x(): return (lax.ppermute(outward, GX, far), lax.ppermute(inward, GX, near))  34.2 us
    ppermute x4, waiting for transfers between devices, swap_x(): return (lax.ppermute(outward, GX, far), lax.ppermute(inward, GX, near))  18.8 us
    ppermute x4, starting transfers between devices, shift(): low = lax.ppermute(tail, axis, [(i, i + 1) for i in range(ends)])  18.7 us
    ppermute x4, waiting for transfers between devices, shift(): high = lax.ppermute(head, axis, [(i + 1, i) for i in range(ends)])  12.2 us
    ppermute x4, waiting for transfers between devices, shift(): low = lax.ppermute(tail, axis, [(i, i + 1) for i in range(ends)])  5.55 us
    ppermute x4, starting transfers between devices, shift(): high = lax.ppermute(head, axis, [(i + 1, i) for i in range(ends)])  5.17 us
  transfers between devices with their start and end apart: 12, of which 9 were waited for; matrix products, arithmetic and copies ran while one was open for 1% of the time, Pallas kernels for 6%

profile of v2, /device:TPU:2, one launch (start us, length us, event | category | flops | bytes accessed | tf_op | source)
XLA Modules:
  0.0 179.3 jit_solution(6187118086775052552)
XLA Ops:
  0.6 0.0 copy-start.2
  0.6 15.3 %collective-permute-start = (f32[16,32,128]{2,1,0:T(8,128)}, f32[16,32,128]{2,1,0:T(8,128)S(1)}, u32[]{:S(2)}, u32[]{:S(2)}) collective-permute-start(f32[16,32,128]{2,1,0:T(8,128)} %param.3), channel_id=1, source_target_pairs={{32,64},{64,32},{96,128},{128,96},{160,192},{192,160},{224,256},{2... | collective-permute-start | bytes 786440 | tf_op jit(solution)/shard_map/ppermute | solution.py:332
  15.9 2.6 %collective-permute-start.1 = (f32[16,32,128]{2,1,0:T(8,128)}, f32[16,32,128]{2,1,0:T(8,128)S(1)}, u32[]{:S(2)}, u32[]{:S(2)}) collective-permute-start(f32[16,32,128]{2,1,0:T(8,128)} %param.3), channel_id=1, source_target_pairs={{0,32},{32,0},{64,96},{96,64},{128,160},{160,128},{192,224},{224,1... | collective-permute-start | bytes 786440 | tf_op jit(solution)/shard_map/ppermute | solution.py:332
  18.6 0.1 subtract_add_fusion.1
  18.7 0.1 broadcast_and_fusion
  18.8 0.7 slice_bitcast_fusion
  19.5 0.1 subtract_add_fusion
  19.6 18.8 %collective-permute-done = f32[16,32,128]{2,1,0:T(8,128)S(1)} collective-permute-done((f32[16,32,128]{2,1,0:T(8,128)}, f32[16,32,128]{2,1,0:T(8,128)S(1)}, u32[]{:S(2)}, u32[]{:S(2)}) %collective-permute-start) | collective-permute-done | bytes 262176 | tf_op jit(solution)/shard_map/ppermute | solution.py:332
  38.4 0.0 collective-permute-done.1
  38.5 0.0 copy-done.2
  38.5 0.1 pad_maximum_fusion.mid
  38.5 0.1 fusion.2
  38.6 1.3 collective-permute-start.3
  39.9 4.6 %collective-permute-start.2 = (f32[48,16,128]{2,1,0:T(8,128)S(1)}, f32[48,16,128]{2,1,0:T(8,128)S(1)}, u32[]{:S(2)}, u32[]{:S(2)}) collective-permute-start(f32[48,16,128]{2,1,0:T(8,128)S(1)} %get-tuple-element.37), channel_id=1, source_target_pairs={{0,8},{8,16},{16,24},{1,9},{9,17},{17,25},{2,10},{10,18},{18,26},{... | collective-permute-start | bytes 1179656 | tf_op jit(solution)/shard_map/ppermute | solution.py:337
  44.5 0.9 select_reduce_fusion.spread
  45.4 0.0 copy-start
  45.4 0.0 copy-start.1
  45.4 6.4 %collective-permute-done.3.high = f32[48,16,128]{2,1,0:T(8,128)S(1)} collective-permute-done((f32[48,16,128]{2,1,0:T(8,128)S(1)}, f32[48,16,128]{2,1,0:T(8,128)S(1)}, u32[]{:S(2)}, u32[]{:S(2)}) %collective-permute-start.3) | collective-permute-done | bytes 393248 | tf_op jit(solution)/shard_map/ppermute | solution.py:338
  51.8 1.2 collective-permute-done.2.low
  53.0 4.0 %shard_map.50 = (f32[48,8,128]{2,1,0:T(8,128)S(1)}, f32[48,8,128]{2,1,0:T(8,128)S(1)}) custom-call(f32[48,32,128]{2,1,0:T(8,128)S(1)} %pad_maximum_fusion.mid, f32[48,16,128]{2,1,0:T(8,128)S(1)} %collective-permute-done.2.low, f32[48,16,128]{2,1,0:T(8,128)S(1)} %collective-permute-done.3.high), custom_call_target="tpu_custom_call" | custom-call | bytes 1966080 | tf_op jit(solution)/shard_map/pallas_call | solution.py:57
  57.0 1.3 collective-permute-start.4
  58.3 4.7 %collective-permute-start.5 = (f32[48,8,128]{2,1,0:T(8,128)S(1)}, f32[48,8,128]{2,1,0:T(8,128)S(1)}, u32[]{:S(2)}, u32[]{:S(2)}) collective-permute-start(f32[48,8,128]{2,1,0:T(8,128)S(1)} %get-tuple-element.20), channel_id=1, source_target_pairs={{0,1},{1,2},{2,3},{3,4},{4,5},{5,6},{6,7},{8,9},{9,10},{10,11},{11... | collective-permute-start | bytes 589832 | tf_op jit(solution)/shard_map/ppermute | solution.py:337
  63.0 0.1 broadcast_and_fusion.1
  63.2 0.1 stack.31.flags.refs_0_
  63.3 0.5 select_reduce_fusion.1.gather
  63.7 1.4 collective-permute-done.4.right
  65.1 1.2 collective-permute-done.5.left
  66.3 0.0 copy-done
  66.3 0.0 copy-done.1
  66.3 15.5 %shard_map.52 = (f32[16,32,128]{2,1,0:T(8,128)}, f32[16,32,128]{2,1,0:T(8,128)S(1)}, f32[8,32,128]{2,1,0:T(8,128)S(1)}, f32[8,32,128]{2,1,0:T(8,128)S(1)}) custom-call(s32[7]{0:T(128)S(1)} %stack.31.flags.refs_0_, f32[3,17]{1,0:T(4,128)S(1)} %copy-done.1, f32[48,32,128]{2,1,0:T(8,128)S(1)} %pad_maximum_fusion.mid, ...), custom_call_target="tpu_custom_call" | custom-call | flops 4000000000 | bytes 3408104 | tf_op jit(solution)/shard_map/pallas_call | solution.py:57
  81.8 8.1 %collective-permute-start.6 = (f32[8,32,128]{2,1,0:T(8,128)S(1)}, f32[8,32,128]{2,1,0:T(8,128)S(1)}, u32[]{:S(2)}, u32[]{:S(2)}) collective-permute-start(f32[8,32,128]{2,1,0:T(8,128)S(1)} %get-tuple-element.26), channel_id=1, source_target_pairs={{32,64},{64,32},{96,128},{128,96},{160,192},{192,160},{224,256},{2... | collective-permute-start | bytes 393224 | tf_op jit(solution)/shard_map/ppermute | solution.py:332
  89.9 8.2 %collective-permute-start.7 = (f32[8,32,128]{2,1,0:T(8,128)S(1)}, f32[8,32,128]{2,1,0:T(8,128)S(1)}, u32[]{:S(2)}, u32[]{:S(2)}) collective-permute-start(f32[8,32,128]{2,1,0:T(8,128)S(1)} %get-tuple-element.27), channel_id=1, source_target_pairs={{0,32},{32,0},{64,96},{96,64},{128,160},{160,128},{192,224},{224,1... | collective-permute-start | bytes 393224 | tf_op jit(solution)/shard_map/ppermute | solution.py:332
  98.1 10.0 %shard_map.51 = (f32[32,48,128]{2,1,0:T(8,128)S(1)}, f32[32,48,128]{2,1,0:T(8,128)S(1)}, f32[32,48,128]{2,1,0:T(8,128)S(1)}, f32[32,48,128]{2,1,0:T(8,128)S(1)}) custom-call(f32[48,32,128]{2,1,0:T(8,128)S(1)} %pad_maximum_fusion.mid, f32[48,16,128]{2,1,0:T(8,128)S(1)} %collective-permute-done.2.low, f32[48,16,128]{2,1,0:T(8,128)S(1)} %collective-permute-done.3.high, ...), custom_call_target="tpu_custom_call" | custom-call | flops 2000000000 | bytes 5111808 | tf_op jit(solution)/shard_map/pallas_call | solution.py:57
  108.1 0.0 collective-permute-done.6.refs_2_
  108.1 0.0 collective-permute-done.7.refs_3_
  108.1 0.6 shard_map.53
  108.7 4.4 %collective-permute-start.8 = (f32[32,8,128]{2,1,0:T(8,128)S(1)}, f32[32,8,128]{2,1,0:T(8,128)S(1)}, u32[]{:S(2)}, u32[]{:S(2)}) collective-permute-start(f32[32,8,128]{2,1,0:T(8,128)S(1)} %get-tuple-element.29), channel_id=1, source_target_pairs={{0,8},{8,16},{16,24},{1,9},{9,17},{17,25},{2,10},{10,18},{18,26},{... | collective-permute-start | bytes 393224 | tf_op jit(solution)/shard_map/ppermute | solution.py:337
  113.1 1.3 collective-permute-start.9
  114.4 1.6 collective-permute-done.8.low
  116.0 4.1 %collective-permute-done.9.high = f32[32,8,128]{2,1,0:T(8,128)S(1)} collective-permute-done((f32[32,8,128]{2,1,0:T(8,128)S(1)}, f32[32,8,128]{2,1,0:T(8,128)S(1)}, u32[]{:S(2)}, u32[]{:S(2)}) %collective-permute-start.9) | collective-permute-done | bytes 131104 | tf_op jit(solution)/shard_map/ppermute | solution.py:338
  120.2 1.5 shard_map.54
  121.7 1.3 collective-permute-start.10
  123.0 5.0 %collective-permute-start.11 = (f32[16,8,128]{2,1,0:T(8,128)S(1)}, f32[16,8,128]{2,1,0:T(8,128)S(1)}, u32[]{:S(2)}, u32[]{:S(2)}) collective-permute-start(f32[16,8,128]{2,1,0:T(8,128)S(1)} %get-tuple-element.32), channel_id=1, source_target_pairs={{0,1},{1,2},{2,3},{3,4},{4,5},{5,6},{6,7},{8,9},{9,10},{10,11},{11... | collective-permute-start | bytes 196616 | tf_op jit(solution)/shard_map/ppermute | solution.py:337
  128.0 0.3 collective-permute-done.10.right
  128.3 1.6 collective-permute-done.11.left
  129.9 8.8 %shard_map.55 = (f32[16,32,128]{2,1,0:T(8,128)S(1)}, f32[1,128]{1,0:T(1,128)S(1)}) custom-call(s32[7]{0:T(128)S(1)} %stack.31.flags.refs_0_, f32[32,48,128]{2,1,0:T(8,128)S(1)} %get-tuple-element.21.refs_4_.p_own, f32[32,48,128]{2,1,0:T(8,128)S(1)} %get-tuple-element.22.p_rim, f32[32,48,128]{2,1,0:T(8,128)S(1)} %get-tuple-element.23.q_own, ...), custom_call_target="tpu_custom_call" | custom-call | flops 2000000000 | bytes 4325916 | tf_op jit(solution)/shard_map/pallas_call | solution.py:57
  138.7 21.8 %all_to_all.10 = f32[32,1,128]{2,1,0:T(1,128)S(1)} all-to-all(f32[32,1,128]{2,1,0:T(1,128)S(1)} %broadcast_in_dim.27), channel_id=1, replica_groups=mesh['gx_0'=4,'gx_1'=2,'gx_2'=2,'gy'=4,'gz'=8] {'gx_1','gx_2','gz'}, dimensions={0} | all-to-all | bytes 32768 | tf_op jit(solution)/shard_map/all_to_all | solution.py:346
  160.5 16.7 %all_to_all.11 = f32[16,1,128]{2,1,0:T(1,128)S(1)} all-to-all(f32[16,1,128]{2,1,0:T(1,128)S(1)} %broadcast_in_dim.28), channel_id=1, replica_groups=mesh['gx_0'=4,'gx_1'=2,'gx_2'=2,'gy'=4,'gz'=8] {'gx_0','gy'}, dimensions={0} | all-to-all | bytes 16384 | tf_op jit(solution)/shard_map/all_to_all | solution.py:346
  177.2 0.6 reduce_sum.43
  178.5 0.7 broadcast_multiply_fusion
  (8 shorter events, 0.1 us)
Async XLA Ops:
  0.6 37.8 %copy-start.2 = (f32[16,32,128]{2,1,0:T(8,128)S(1)}, f32[16,32,128]{2,1,0:T(8,128)}, u32[]{:S(2)}) copy-start(f32[16,32,128]{2,1,0:T(8,128)} %param.3) | copy-start | bytes 786436
  0.6 37.8 %collective-permute-start = (f32[16,32,128]{2,1,0:T(8,128)}, f32[16,32,128]{2,1,0:T(8,128)S(1)}, u32[]{:S(2)}, u32[]{:S(2)}) collective-permute-start(f32[16,32,128]{2,1,0:T(8,128)} %param.3), channel_id=1, source_target_pairs={{32,64},{64,32},{96,128},{128,96},{160,192},{192,160},{224,256},{2... | collective-permute-start | bytes 786440 | tf_op jit(solution)/shard_map/ppermute | solution.py:332
  15.9 22.5 %collective-permute-start.1 = (f32[16,32,128]{2,1,0:T(8,128)}, f32[16,32,128]{2,1,0:T(8,128)S(1)}, u32[]{:S(2)}, u32[]{:S(2)}) collective-permute-start(f32[16,32,128]{2,1,0:T(8,128)} %param.3), channel_id=1, source_target_pairs={{0,32},{32,0},{64,96},{96,64},{128,160},{160,128},{192,224},{224,1... | collective-permute-start | bytes 786440 | tf_op jit(solution)/shard_map/ppermute | solution.py:332
  38.6 13.2 %collective-permute-start.3 = (f32[48,16,128]{2,1,0:T(8,128)S(1)}, f32[48,16,128]{2,1,0:T(8,128)S(1)}, u32[]{:S(2)}, u32[]{:S(2)}) collective-permute-start(f32[48,16,128]{2,1,0:T(8,128)S(1)} %get-tuple-element.36), channel_id=1, source_target_pairs={{8,0},{16,8},{24,16},{9,1},{17,9},{25,17},{10,2},{18,10},{26,18},{... | collective-permute-start | bytes 1179656 | tf_op jit(solution)/shard_map/ppermute | solution.py:338
  39.9 13.1 %collective-permute-start.2 = (f32[48,16,128]{2,1,0:T(8,128)S(1)}, f32[48,16,128]{2,1,0:T(8,128)S(1)}, u32[]{:S(2)}, u32[]{:S(2)}) collective-permute-start(f32[48,16,128]{2,1,0:T(8,128)S(1)} %get-tuple-element.37), channel_id=1, source_target_pairs={{0,8},{8,16},{16,24},{1,9},{9,17},{17,25},{2,10},{10,18},{18,26},{... | collective-permute-start | bytes 1179656 | tf_op jit(solution)/shard_map/ppermute | solution.py:337
  45.4 20.9 %copy-start = (f32[16,32,128]{2,1,0:T(8,128)S(1)}, f32[16,32,128]{2,1,0:T(8,128)}, u32[]{:S(2)}) copy-start(f32[16,32,128]{2,1,0:T(8,128)} %external.1) | copy-start | bytes 786436
  45.4 20.9 %copy-start.1 = (f32[3,17]{1,0:T(4,128)S(1)}, f32[3,17]{1,0:T(4,128)}, u32[]{:S(2)}) copy-start(f32[3,17]{1,0:T(4,128)} %weights.1) | copy-start | bytes 616
  57.0 8.1 %collective-permute-start.4 = (f32[48,8,128]{2,1,0:T(8,128)S(1)}, f32[48,8,128]{2,1,0:T(8,128)S(1)}, u32[]{:S(2)}, u32[]{:S(2)}) collective-permute-start(f32[48,8,128]{2,1,0:T(8,128)S(1)} %get-tuple-element.19), channel_id=1, source_target_pairs={{1,0},{2,1},{3,2},{4,3},{5,4},{6,5},{7,6},{9,8},{10,9},{11,10},{12... | collective-permute-start | bytes 589832 | tf_op jit(solution)/shard_map/ppermute | solution.py:338
  58.3 8.0 %collective-permute-start.5 = (f32[48,8,128]{2,1,0:T(8,128)S(1)}, f32[48,8,128]{2,1,0:T(8,128)S(1)}, u32[]{:S(2)}, u32[]{:S(2)}) collective-permute-start(f32[48,8,128]{2,1,0:T(8,128)S(1)} %get-tuple-element.20), channel_id=1, source_target_pairs={{0,1},{1,2},{2,3},{3,4},{4,5},{5,6},{6,7},{8,9},{9,10},{10,11},{11... | collective-permute-start | bytes 589832 | tf_op jit(solution)/shard_map/ppermute | solution.py:337
  81.8 26.3 %collective-permute-start.6 = (f32[8,32,128]{2,1,0:T(8,128)S(1)}, f32[8,32,128]{2,1,0:T(8,128)S(1)}, u32[]{:S(2)}, u32[]{:S(2)}) collective-permute-start(f32[8,32,128]{2,1,0:T(8,128)S(1)} %get-tuple-element.26), channel_id=1, source_target_pairs={{32,64},{64,32},{96,128},{128,96},{160,192},{192,160},{224,256},{2... | collective-permute-start | bytes 393224 | tf_op jit(solution)/shard_map/ppermute | solution.py:332
  89.9 18.2 %collective-permute-start.7 = (f32[8,32,128]{2,1,0:T(8,128)S(1)}, f32[8,32,128]{2,1,0:T(8,128)S(1)}, u32[]{:S(2)}, u32[]{:S(2)}) collective-permute-start(f32[8,32,128]{2,1,0:T(8,128)S(1)} %get-tuple-element.27), channel_id=1, source_target_pairs={{0,32},{32,0},{64,96},{96,64},{128,160},{160,128},{192,224},{224,1... | collective-permute-start | bytes 393224 | tf_op jit(solution)/shard_map/ppermute | solution.py:332
  108.7 7.3 %collective-permute-start.8 = (f32[32,8,128]{2,1,0:T(8,128)S(1)}, f32[32,8,128]{2,1,0:T(8,128)S(1)}, u32[]{:S(2)}, u32[]{:S(2)}) collective-permute-start(f32[32,8,128]{2,1,0:T(8,128)S(1)} %get-tuple-element.29), channel_id=1, source_target_pairs={{0,8},{8,16},{16,24},{1,9},{9,17},{17,25},{2,10},{10,18},{18,26},{... | collective-permute-start | bytes 393224 | tf_op jit(solution)/shard_map/ppermute | solution.py:337
  113.1 7.0 %collective-permute-start.9 = (f32[32,8,128]{2,1,0:T(8,128)S(1)}, f32[32,8,128]{2,1,0:T(8,128)S(1)}, u32[]{:S(2)}, u32[]{:S(2)}) collective-permute-start(f32[32,8,128]{2,1,0:T(8,128)S(1)} %get-tuple-element.30), channel_id=1, source_target_pairs={{8,0},{16,8},{24,16},{9,1},{17,9},{25,17},{10,2},{18,10},{26,18},{... | collective-permute-start | bytes 393224 | tf_op jit(solution)/shard_map/ppermute | solution.py:338
  121.7 6.6 %collective-permute-start.10 = (f32[16,8,128]{2,1,0:T(8,128)S(1)}, f32[16,8,128]{2,1,0:T(8,128)S(1)}, u32[]{:S(2)}, u32[]{:S(2)}) collective-permute-start(f32[16,8,128]{2,1,0:T(8,128)S(1)} %get-tuple-element.31), channel_id=1, source_target_pairs={{1,0},{2,1},{3,2},{4,3},{5,4},{6,5},{7,6},{9,8},{10,9},{11,10},{12... | collective-permute-start | bytes 196616 | tf_op jit(solution)/shard_map/ppermute | solution.py:338
  123.0 6.9 %collective-permute-start.11 = (f32[16,8,128]{2,1,0:T(8,128)S(1)}, f32[16,8,128]{2,1,0:T(8,128)S(1)}, u32[]{:S(2)}, u32[]{:S(2)}) collective-permute-start(f32[16,8,128]{2,1,0:T(8,128)S(1)} %get-tuple-element.32), channel_id=1, source_target_pairs={{0,1},{1,2},{2,3},{3,4},{4,5},{5,6},{6,7},{8,9},{9,10},{10,11},{11... | collective-permute-start | bytes 196616 | tf_op jit(solution)/shard_map/ppermute | solution.py:337

commit v3 on v2

v3 whole, which is shorter than its diff:
```python
import functools

import jax
import jax.numpy as jnp
from jax import lax
from jax.experimental import pallas as pl
from jax.experimental.pallas import tpu as pltpu
from jax.sharding import Mesh
from jax.sharding import PartitionSpec as P

RINGS = (("gx_1", "gx_2", "gz"), ("gx_0", "gy"))
GX = ("gx_0", "gx_1", "gx_2")
LAP_COEF = (-205.0 / 72.0, 8.0 / 5.0, -1.0 / 5.0, 8.0 / 315.0, -1.0 / 560.0)
STEP = 0.08
F32 = jnp.float32
LANES = 128


def lane_ids(shape):
    return lax.broadcasted_iota(jnp.int32, shape, len(shape) - 1)


def pack(rows_of, count, cells, offset):
    lanes = lane_ids((8, LANES))
    first = last = None
    for q in range(count):
        at = offset + cells * q
        here = (lanes >= at) & (lanes < at + cells)
        rows = rows_of(q)
        head = pltpu.roll(rows, at, 1) if at else rows
        tail = pltpu.roll(rows, (at + cells) % LANES, 1)
        first = jnp.where(here, head, 0.0 if first is None else first)
        last = jnp.where(here, tail, 0.0 if last is None else last)
    return first, last


def unpack(right, left, at, cells):
    lanes = lane_ids((8, LANES))
    high = pltpu.roll(right, (LANES - at) % LANES, 1) if at % LANES else right
    low = pltpu.roll(left, (2 * LANES - cells - at) % LANES, 1)
    return jnp.where(lanes < cells, high, jnp.where(lanes >= LANES - cells, low, 0.0))


def skipping(body, start, count, *refs):
    body(*refs[:start], *refs[start + count :])


def call(body, outs, scratch, *args, scalars=0, flops=0, aliases=None, after=()):
    specs = [pl.BlockSpec(memory_space=pltpu.SMEM)] * scalars
    specs += [pl.BlockSpec(memory_space=pltpu.VMEM)] * (len(args) - scalars)
    specs += [pl.BlockSpec(memory_space=pl.ANY)] * len(after)
    body = functools.partial(skipping, body, len(args), len(after))
    shapes = [jax.ShapeDtypeStruct(s, F32) for s in outs]
    nbytes = 4 * sum(a.size for a in args) + 4 * sum(s.size for s in shapes)
    return pl.pallas_call(
        body,
        out_shape=shapes,
        in_specs=specs,
        out_specs=[pl.BlockSpec(memory_space=pltpu.VMEM)] * len(outs),
        scratch_shapes=[pltpu.VMEM(s, F32) for s in scratch],
        input_output_aliases=aliases or {},
        compiler_params=pltpu.CompilerParams(vmem_limit_bytes=20 * 1024 * 1024),
        cost_estimate=pl.CostEstimate(flops=flops, bytes_accessed=nbytes, transcendentals=0),
    )(*args, *after)


def cut(wave, external, head, tail):
    head[:, 0:24, :] = wave[:, 0:24, :]
    head[:, 24:32, :] = external[:, 0:8, :]
    tail[:, 0:24, :] = wave[:, 8:32, :]
    tail[:, 24:32, :] = external[:, 24:32, :]


def cut_outer(outer, head, tail):
    head[...] = outer[:, 0:24, :]
    tail[...] = outer[:, 8:32, :]


def stacked(x, low, mid, high):
    def rows_of(q):
        for ref, start, stop in (low, mid, high):
            count = (stop - start) // 8
            if q < count:
                return ref[x, start + 8 * q : start + 8 * q + 8, :]
            q -= count

    return rows_of


def pack_wave(wave, low, high, first, last):
    def plane(x, carry):
        rows_of = stacked(x, (low, 0, 24), (wave, 0, 32), (high, 0, 24))
        for r in range(2):
            rows = slice(8 * r, 8 * r + 8)
            first[x, rows, :], last[x, rows, :] = pack(lambda q: rows_of(q + 5 * r), 5, 24, 0)
        return carry

    lax.fori_loop(0, 16, plane, 0)


def pack_both(wave, external, low, high, first, last):
    pack_wave(wave, low, high, first, last)

    def plane(x, carry):
        rows_of = stacked(x, (low, 24, 32), (external, 0, 32), (high, 24, 32))
        first[x, 16:24, :], last[x, 16:24, :] = pack(rows_of, 6, 8, 0)
        return carry

    lax.fori_loop(0, 16, plane, 0)


def fill(own, rim, base, mid, low, high, right, left):
    def plane(x, carry):
        own[base + x, 0:24, :] = low[x, 0:24, :]
        own[base + x, 24:56, :] = mid[x]
        own[base + x, 56:80, :] = high[x, 0:24, :]
        for g in range(10):
            rows = slice(8 * (g // 5), 8 * (g // 5) + 8)
            rim[base + x, 8 * g : 8 * g + 8, :] = unpack(right[x, rows, :], left[x, rows, :], 24 * (g % 5), 24)
        return carry

    lax.fori_loop(0, 16, plane, 0)


def halves(x):
    top = x.astype(jnp.bfloat16)
    return top, (x - top.astype(F32)).astype(jnp.bfloat16)


def times(x, matrix_halves):
    top, rest = halves(x)
    big, small = matrix_halves
    dot = functools.partial(jnp.dot, preferred_element_type=F32)
    return dot(top, big) + (dot(top, small) + dot(rest, big))


def slide(src, dst, taps, groups):
    count = dst.shape[0]

    def column(g, carry):
        rows = pl.ds(pl.multiple_of(8 * g, 8), 8)
        sums = {}
        for j in range(count + 16):
            value = src[j, rows, :]
            for a in range(17):
                i = j - a
                if 0 <= i < count:
                    term = taps[a] * value
                    sums[i] = sums[i] + term if a else term
            if j >= 16:
                dst[j - 16, rows, :] = sums.pop(j - 16)
        return carry

    lax.fori_loop(0, groups, column, 0)


def along_rows(src, x, taps, count):
    total = taps[0] * src[x, 0:count, :]
    for b in range(1, 17):
        total = total + taps[b] * src[x, b : b + count, :]
    return total


def along_z(own, rim, g_own, g_rim, base, spread_halves):
    def chunk(k, carry):
        planes = pl.ds(base + 2 * k, 2)
        a = own[planes].reshape(160, LANES)
        b = rim[planes].reshape(160, LANES)
        out = times(jnp.concatenate([a * a, b * b], axis=1), spread_halves)
        g_own[planes] = out[:, :LANES].reshape(2, 80, LANES)
        g_rim[planes] = out[:, LANES:].reshape(2, 80, LANES)
        return carry

    lax.fori_loop(0, 8, chunk, 0)


def prepare(
    flags, spread, wave, low, high, right, left, inner, i_low, i_high, i_right, i_left, own, rim, g_own, g_rim
):
    spread_halves = halves(spread[...])
    base = 32 * (1 - flags[0])
    fill(own, rim, 16, wave, low, high, right, left)
    along_z(own, rim, g_own, g_rim, 16, spread_halves)
    fill(own, rim, base, inner, i_low, i_high, i_right, i_left)
    along_z(own, rim, g_own, g_rim, base, spread_halves)


def smears(
    flags, weights, spread, gather, external, low, high, right, left, outer, o_low, o_high, o_right, o_left,
    own_in, rim_in, g_own_in, g_rim_in, corr, v_own, v_rim, outward, inward, own, rim, g_own, g_rim,
    h_own, h_rim, s_own, s_rim, c_own, c_rim, t_own, t_rim, u_own, u_rim,
):
    upper = flags[0]
    base = 32 * upper
    fill(own, rim, base, outer, o_low, o_high, o_right, o_left)
    along_z(own, rim, g_own, g_rim, base, halves(spread[...]))
    x_taps = [weights[0, a] for a in range(17)]
    y_taps = [weights[1, a] for a in range(17)]
    slide(g_own, h_own, x_taps, 10)
    slide(g_rim, h_rim, x_taps, 10)

    def source(x, carry):
        for h, e, s, c in ((h_own, own, s_own, c_own), (h_rim, rim, s_rim, c_rim)):
            coarse = along_rows(h, x, y_taps, 64)
            wave = e[x + 8, 8:72, :]
            density = wave * wave
            s[x] = -1.0 * density * coarse + 0.5 * density * coarse * coarse
            c[x] = coarse
        return carry

    lax.fori_loop(0, 32, source, 0)
    slide(s_own, t_own, x_taps[::-1], 8)
    slide(s_rim, t_rim, x_taps[::-1], 8)

    def back(x, carry):
        u_own[x] = along_rows(t_own, x, y_taps[::-1], 48)
        u_rim[x] = along_rows(t_rim, x, y_taps[::-1], 48)
        return carry

    lax.fori_loop(0, 16, back, 0)
    gather_halves = halves(gather[...])

    def finish(k, carry):
        planes = pl.ds(4 * k, 4)
        both = jnp.concatenate([u_own[planes].reshape(192, LANES), u_rim[planes].reshape(192, LANES)], axis=1)
        smeared = times(both, gather_halves)
        for c, v, part in ((c_own, v_own, smeared[:, :LANES]), (c_rim, v_rim, smeared[:, LANES:])):
            coarse = c[pl.ds(8 + 4 * k, 4), 8:56, :]
            v[planes] = -0.5 * coarse * coarse + 0.5 / 3.0 * coarse * coarse * coarse + part.reshape(4, 48, LANES)
        corr[planes] = v_own[planes, 8:40, :]
        v_own[planes, 0:8, :] += low[planes, 24:32, :]
        v_own[planes, 8:40, :] += external[planes]
        v_own[planes, 40:48, :] += high[planes, 24:32, :]
        for i in range(4):
            x = 4 * k + i
            for q in range(6):
                v_rim[x, 8 * q : 8 * q + 8, :] += unpack(right[x, 16:24, :], left[x, 16:24, :], 8 * q, 8)
        return carry

    lax.fori_loop(0, 4, finish, 0)

    lanes = lane_ids((8, LANES))
    for out, side in ((outward, upper), (inward, 1 - upper)):
        edge, beyond = 12 * side, 4 + 4 * side
        rims = jnp.zeros((8, LANES), F32)
        for i in range(4):
            for q in range(5):
                out[5 * i + q] = v_own[edge + i, 4 + 8 * q : 12 + 8 * q, :]
            for q in range(4):
                out[20 + 4 * i + q] = v_own[beyond + i, 8 + 8 * q : 16 + 8 * q, :]
                at = 8 * (4 * i + q)
                here = (lanes >= at) & (lanes < at + 8)
                rims = jnp.where(here, pltpu.roll(v_rim[edge + i, 8 + 8 * q : 16 + 8 * q, :], (at + 4) % LANES, 1), rims)
        out[36] = rims


def laplace(own, rim, x, start, count, with_rim):
    lanes = lane_ids((count, LANES))
    rows = slice(start, start + count)
    centers = own[x, rows, :], rim[x, rows, :]
    totals = []
    for ref, other in ((0, 1), (1, 0))[: 2 if with_rim else 1]:
        field = (own, rim)[ref]
        center = centers[ref]
        total = (1.0 + 0.5 * STEP * 3.0 * LAP_COEF[0]) * center
        for k in range(1, 5):
            near = field[x + k, rows, :] + field[x - k, rows, :]
            near = near + (field[x, start + k : start + k + count, :] + field[x, start - k : start - k + count, :])
            ahead = jnp.where(
                lanes < LANES - k, pltpu.roll(center, LANES - k, 1), pltpu.roll(centers[other], LANES - k, 1)
            )
            behind = jnp.where(lanes >= k, pltpu.roll(center, k, 1), pltpu.roll(centers[other], k, 1))
            total = total + (0.5 * STEP * LAP_COEF[k]) * (near + (ahead + behind))
        totals.append(total)
    return totals


def first_step(own, rim, p_own, p_rim):
    def plane(x, carry):
        p_own[x], p_rim[x] = laplace(own, rim, x + 8, 16, 48, True)
        return carry

    lax.fori_loop(0, 32, plane, 0)


def last_steps(
    flags, p_own, p_rim, q_own, q_rim, mid_own, mid_rim, outer, inner, psi, squares,
    v_own, v_rim, a_own, a_rim, b_own, b_rim,
):
    upper = flags[0]
    v_own[8:24] = mid_own[...]
    v_rim[8:24] = mid_rim[...]
    lanes = lane_ids((8, LANES))
    for ref, side in ((outer, upper), (inner, 1 - upper)):
        edge, beyond = 4 + 20 * side, 28 * side
        for i in range(4):
            v_own[beyond + i] = jnp.zeros((48, LANES), F32)
            v_rim[beyond + i] = jnp.zeros((48, LANES), F32)
            v_own[edge + i] = jnp.zeros((48, LANES), F32)
            v_rim[edge + i] = jnp.zeros((48, LANES), F32)
            for q in range(5):
                v_own[edge + i, 4 + 8 * q : 12 + 8 * q, :] = ref[5 * i + q]
            for q in range(4):
                v_own[beyond + i, 8 + 8 * q : 16 + 8 * q, :] = ref[20 + 4 * i + q]
                rim = pltpu.roll(ref[36], LANES - 4 - 8 * (4 * i + q) + (LANES if 4 * i + q == 15 else 0), 1)
                v_rim[edge + i, 8 + 8 * q : 16 + 8 * q, :] = jnp.where((lanes < 4) | (lanes >= LANES - 4), rim, 0.0)

    def masks(count, edge):
        rows = lax.broadcasted_iota(jnp.int32, (count, LANES), 0) - edge
        lanes = lane_ids((count, LANES))
        in_rows = (rows >= flags[3]) & (rows < flags[4])
        in_rim = ((lanes >= 64) & (flags[5] != 0)) | ((lanes < 64) & (flags[6] != 0))
        rows_one = jnp.where(in_rows, 1.0, 0.0)
        return rows_one, jnp.where(in_rim, rows_one, 0.0)

    def inside(x, edge):
        return jnp.where((x - edge >= flags[1]) & (x - edge < flags[2]), 1.0, 0.0)

    keep_own, keep_rim = masks(48, 8)

    def one(x, carry):
        keep = inside(x, 8)
        a_own[x] = (p_own[x] - STEP * v_own[x] * q_own[x + 8, 16:64, :]) * (keep * keep_own)
        a_rim[x] = (p_rim[x] - STEP * v_rim[x] * q_rim[x + 8, 16:64, :]) * (keep * keep_rim)
        return carry

    lax.fori_loop(0, 32, one, 0)
    mid_own, mid_rim = masks(40, 4)

    def two(x, carry):
        keep = inside(x, 4)
        own, rim = laplace(a_own, a_rim, x + 4, 4, 40, True)
        v = v_own[x + 4, 4:44, :] * a_own[x + 4, 4:44, :]
        b_own[x] = (own - STEP * v) * (keep * mid_own)
        v = v_rim[x + 4, 4:44, :] * a_rim[x + 4, 4:44, :]
        b_rim[x] = (rim - STEP * v) * (keep * mid_rim)
        return carry

    lax.fori_loop(0, 24, two, 0)

    def three(x, total):
        (own,) = laplace(b_own, b_rim, x + 4, 4, 32, False)
        value = own - STEP * (v_own[x + 8, 8:40, :] * b_own[x + 4, 4:36, :])
        psi[x] = value
        return total + value * value

    total = lax.fori_loop(0, 16, three, jnp.zeros((32, LANES), F32))
    squares[...] = jnp.sum(total, axis=0, keepdims=True)


def scale(count, rows, psi, out):
    total = jnp.sum(rows[...].reshape(-1, LANES), axis=0, keepdims=True)
    total = jnp.sum(total, axis=1, keepdims=True)
    factor = lax.rsqrt(total / count + 1e-06)
    out[...] = psi[...] * factor[None]


def band(row, flip):
    places = jnp.arange(256, dtype=jnp.int32)
    places = jnp.where(places < 192, places, places - 256)
    margin = 8 if flip else 16
    offset = (places[None, :] - places[:, None] if flip else places[:, None] - places[None, :]) + 8
    valid = (places >= -margin) & (places < LANES + margin)
    reach = (places >= -margin - 8) & (places < LANES + margin + 8)
    hits = (offset[:, :, None] == jnp.arange(17, dtype=jnp.int32)) & (valid[None, :] & reach[:, None])[:, :, None]
    return jnp.sum(jnp.where(hits, row, 0.0), axis=2)


def swap_far(planes):
    count = lax.axis_size(GX)
    return lax.ppermute(planes, GX, [p for k in range(1, count - 1, 2) for p in ((k, k + 1), (k + 1, k))])


def swap_near(planes):
    return lax.ppermute(planes, GX, [(k, k ^ 1) for k in range(lax.axis_size(GX))])


def shift(head, tail, axis):
    ends = lax.axis_size(axis) - 1
    low = lax.ppermute(tail, axis, [(i, i + 1) for i in range(ends)])
    high = lax.ppermute(head, axis, [(i + 1, i) for i in range(ends)])
    return low, high


def spread(row, axes):
    count = lax.axis_size(axes)
    return lax.all_to_all(jnp.broadcast_to(row[None], (count, *row.shape)), axes, 0, 0, tiled=True)


def shards(wave, external, weights):
    at = [lax.axis_index(axis) for axis in (GX, "gy", "gz")]
    last = [at[d] == lax.axis_size(axis) - 1 for d, axis in enumerate((GX, "gy", "gz"))]
    far = 1 << 20
    flags = jnp.stack(
        [
            lax.axis_index("gx_2"),
            jnp.where(at[0] == 0, 0, -far),
            jnp.where(last[0], wave.shape[0], far),
            jnp.where(at[1] == 0, 0, -far),
            jnp.where(last[1], wave.shape[1], far),
            jnp.where(at[2] == 0, 0, 1),
            jnp.where(last[2], 0, 1),
        ]
    ).astype(jnp.int32)
    block = wave.shape
    outer, inner = swap_far(wave), swap_near(wave)
    low, high = shift(*call(cut, [block] * 2, [], wave, external), "gy")
    first, final = call(pack_both, [(16, 24, LANES)] * 2, [], wave, external, low, high)
    left, right = shift(first, final, "gz")
    i_low, i_high, i_left, i_right = (swap_near(a) for a in (low, high, left, right))
    o_low, o_high = shift(*call(cut_outer, [(16, 24, LANES)] * 2, [], outer, after=(left, right, i_low, i_high)), "gy")
    first, final = call(pack_wave, [(16, 16, LANES)] * 2, [], outer, o_low, o_high)
    o_left, o_right = shift(first, final, "gz")

    wide, thin, box = (48, 80, LANES), (32, 48, LANES), (16, 48, LANES)
    smear_z, gather_z = band(weights[2], False), band(weights[2], True)
    fields = call(
        prepare, [wide] * 4, [],
        flags, smear_z, wave, low, high, right, left, inner, i_low, i_high, i_right, i_left,
        scalars=1, flops=2 * 10**9,
    )
    corr, v_own, v_rim, outward, inward, own, rim, _, _ = call(
        smears,
        [block, box, box, (37, 8, LANES), (37, 8, LANES)] + [wide] * 4,
        [(32, 80, LANES)] * 2 + [(32, 64, LANES)] * 4 + [(16, 64, LANES)] * 2 + [box] * 2,
        flags, weights, smear_z, gather_z, external, low, high, right, left,
        outer, o_low, o_high, o_right, o_left, *fields,
        scalars=2, flops=4 * 10**9, aliases={14: 5, 15: 6, 16: 7, 17: 8},
    )
    v_outer, v_inner = swap_far(outward), swap_near(inward)
    p_own, p_rim = call(first_step, [thin] * 2, [], own, rim, flops=2 * 10**9)
    psi, squares = call(
        last_steps,
        [block, (1, LANES)],
        [thin] * 4 + [(24, 40, LANES)] * 2,
        flags, p_own, p_rim, own, rim, v_own, v_rim, v_outer, v_inner,
        scalars=1, flops=2 * 10**9,
    )
    rows = spread(jnp.sum(spread(squares, RINGS[0]), axis=0), RINGS[1])
    count = float(psi.size * lax.axis_size(GX) * lax.axis_size("gy") * lax.axis_size("gz"))
    (wave_next,) = call(functools.partial(scale, count), [block], [], rows, psi)
    return (wave_next, corr)


def solution(mesh):
    torus = Mesh(
        mesh.devices.reshape(4, 2, 2, mesh.shape["gy"], mesh.shape["gz"]),
        ("gx_0", "gx_1", "gx_2", "gy", "gz"),
    )
    placed = (P(GX, "gy", "gz"), P(GX, "gy", "gz"), P())
    return jax.shard_map(
        shards,
        mesh=torus,
        in_specs=placed,
        out_specs=(P(GX, "gy", "gz"), P(GX, "gy", "gz")),
        check_vma=False,
    )
```

time: 180 us -> 160 us (0.89)
  waiting for transfers between devices: 36.6 us -> 16.7 us
  Pallas kernels: 40.3 us -> 42.4 us
    ppermute x4 -> x8, waiting for transfers between devices: 18.8 us -> 2.9 us  [the longest x2 2.89 us: swap_far(): lax.ppermute(planes, GX, [p for k in range(1, count - 1, 2) for p in ((k,...]
    ppermute x4, waiting for transfers between devices: 12.2 us -> 7.41 us  [shift(): high = lax.ppermute(head, axis, [(i + 1, i) for i in range(ends)])]
    ppermute x4, starting transfers between devices: 18.7 us -> 16.1 us  [shift(): low = lax.ppermute(tail, axis, [(i, i + 1) for i in range(ends)])]
    pallas_call x6 -> x9, Pallas kernels: 40.3 us -> 42.4 us  [call(): pl.pallas_call(body, out_shape=shapes, in_specs=specs, out_specs=[pl.Bloc...]
    ppermute x4 -> x8, starting transfers between devices: 34.2 us -> 35.1 us  [the longest x2 21.2 us: swap_far(): lax.ppermute(planes, GX, [p for k in range(1, count - 1, 2) for p in ((k,...]
  transfers between devices with their start and end apart: 12 -> 16, of which waited for: 9 -> 6; matrix products, arithmetic and copies ran while one was open for 1% -> 1% of each run, Pallas kernels for 6% -> 13%
where the time goes in v3:
time: 160 us; the launch traced here: 159 us
  starting transfers between devices  56.4 us (35%)
  Pallas kernels  42.4 us (26%)
  blocking collectives  39.7 us (25%)
  waiting for transfers between devices  16.7 us (10%)
  other arithmetic  2.08 us (1%)
    pallas_call x9, Pallas kernels, call(): pl.pallas_call(body, out_shape=shapes, in_specs=specs, out_specs=[pl.Bloc...  42.4 us
    all_to_all x2, blocking collectives, spread(): lax.all_to_all(jnp.broadcast_to(row[None], (count, *row.shape)), axes, 0,...  39.7 us
    ppermute x2, starting transfers between devices, swap_far(): lax.ppermute(planes, GX, [p for k in range(1, count - 1, 2) for p in ((k,...  21.2 us
    ppermute x4, starting transfers between devices, shift(): low = lax.ppermute(tail, axis, [(i, i + 1) for i in range(ends)])  16.1 us
    ppermute x6, starting transfers between devices, swap_near(): lax.ppermute(planes, GX, [(k, k ^ 1) for k in range(lax.axis_size(GX))])  13.9 us
    ppermute x4, waiting for transfers between devices, shift(): high = lax.ppermute(head, axis, [(i + 1, i) for i in range(ends)])  7.41 us
    ppermute x4, waiting for transfers between devices, shift(): low = lax.ppermute(tail, axis, [(i, i + 1) for i in range(ends)])  6.36 us
    ppermute x4, starting transfers between devices, shift(): high = lax.ppermute(head, axis, [(i + 1, i) for i in range(ends)])  5.17 us
  transfers between devices with their start and end apart: 16, of which 6 were waited for; matrix products, arithmetic and copies ran while one was open for 1% of the time, Pallas kernels for 13%

profile of v3, /device:TPU:2, one launch (start us, length us, event | category | flops | bytes accessed | tf_op | source)
XLA Modules:
  0.0 159.3 jit_solution(4362387084760345363)
XLA Ops:
  0.6 15.1 %collective-permute-start.4 = (f32[16,32,128]{2,1,0:T(8,128)}, f32[16,32,128]{2,1,0:T(8,128)S(1)}, u32[]{:S(2)}, u32[]{:S(2)}) collective-permute-start(f32[16,32,128]{2,1,0:T(8,128)} %refs_2_.1), channel_id=1, source_target_pairs={{32,64},{64,32},{96,128},{128,96},{160,192},{192,160},{224,256},{2... | collective-permute-start | bytes 786440 | tf_op jit(solution)/shard_map/ppermute | solution.py:371
  15.8 0.0 copy-start
  15.8 0.9 copy-done
  16.7 0.0 copy-start.2
  16.7 1.0 shard_map.50
  17.7 3.5 %collective-permute-start = (f32[16,32,128]{2,1,0:T(8,128)S(1)}, f32[16,32,128]{2,1,0:T(8,128)S(1)}, u32[]{:S(2)}, u32[]{:S(2)}) collective-permute-start(f32[16,32,128]{2,1,0:T(8,128)S(1)} %get-tuple-element.25), channel_id=1, source_target_pairs={{0,8},{8,16},{16,24},{1,9},{9,17},{17,25},{2,10},{10,18},{18,26},{... | collective-permute-start | bytes 786440 | tf_op jit(solution)/shard_map/ppermute | solution.py:380
  21.2 1.3 collective-permute-start.1
  22.6 0.1 subtract_add_fusion.1
  22.7 5.0 %collective-permute-done.refs_2_.refs_3_.refs_5_ = f32[16,32,128]{2,1,0:T(8,128)S(1)} collective-permute-done((f32[16,32,128]{2,1,0:T(8,128)S(1)}, f32[16,32,128]{2,1,0:T(8,128)S(1)}, u32[]{:S(2)}, u32[]{:S(2)}) %collective-permute-start) | collective-permute-done | bytes 262176 | tf_op jit(solution)/shard_map/ppermute | solution.py:380
  27.6 1.9 %collective-permute-start.5 = (f32[16,32,128]{2,1,0:T(8,128)S(1)}, f32[16,32,128]{2,1,0:T(8,128)S(1)}, u32[]{:S(2)}, u32[]{:S(2)}) collective-permute-start(f32[16,32,128]{2,1,0:T(8,128)S(1)} %collective-permute-done.refs_2_.refs_3_.refs_5_), channel_id=1, source_target_pairs={{0,32},{32,0},{64,96},{96,64},{128,160},{160,128},{192,224},{224,1... | collective-permute-start | bytes 786440 | tf_op jit(solution)/shard_map/ppermute | solution.py:375
  29.6 2.2 %collective-permute-done.1.refs_3_.refs_4_.refs_6_ = f32[16,32,128]{2,1,0:T(8,128)S(1)} collective-permute-done((f32[16,32,128]{2,1,0:T(8,128)S(1)}, f32[16,32,128]{2,1,0:T(8,128)S(1)}, u32[]{:S(2)}, u32[]{:S(2)}) %collective-permute-start.1) | collective-permute-done | bytes 262176 | tf_op jit(solution)/shard_map/ppermute | solution.py:381
  31.8 1.9 %collective-permute-start.6 = (f32[16,32,128]{2,1,0:T(8,128)S(1)}, f32[16,32,128]{2,1,0:T(8,128)S(1)}, u32[]{:S(2)}, u32[]{:S(2)}) collective-permute-start(f32[16,32,128]{2,1,0:T(8,128)S(1)} %collective-permute-done.1.refs_3_.refs_4_.refs_6_), channel_id=1, source_target_pairs={{0,32},{32,0},{64,96},{96,64},{128,160},{160,128},{192,224},{224,1... | collective-permute-start | bytes 786440 | tf_op jit(solution)/shard_map/ppermute | solution.py:375
  33.7 0.1 broadcast_and_fusion.1
  33.8 3.6 %shard_map.51 = (f32[16,24,128]{2,1,0:T(8,128)S(1)}, f32[16,24,128]{2,1,0:T(8,128)S(1)}) custom-call(f32[16,32,128]{2,1,0:T(8,128)} %refs_2_.1, f32[16,32,128]{2,1,0:T(8,128)S(1)} %copy-done, f32[16,32,128]{2,1,0:T(8,128)S(1)} %collective-permute-done.refs_2_.refs_3_.refs_5_, f32[16,32,128]{2,1,0:T(8,128)S(1)} %collective-permute-done.1.refs_3_.refs_4_.refs_6_), custom_call_target="tpu_custom_call" | custom-call | bytes 1441792 | tf_op jit(solution)/shard_map/pallas_call | solution.py:55
  37.5 1.3 collective-permute-start.2
  38.8 4.6 %collective-permute-start.3 = (f32[16,24,128]{2,1,0:T(8,128)S(1)}, f32[16,24,128]{2,1,0:T(8,128)S(1)}, u32[]{:S(2)}, u32[]{:S(2)}) collective-permute-start(f32[16,24,128]{2,1,0:T(8,128)S(1)} %get-tuple-element.28), channel_id=1, source_target_pairs={{0,1},{1,2},{2,3},{3,4},{4,5},{5,6},{6,7},{8,9},{9,10},{10,11},{11... | collective-permute-start | bytes 589832 | tf_op jit(solution)/shard_map/ppermute | solution.py:380
  43.3 0.0 copy-done.2
  43.3 0.0 collective-permute-done.4.refs_0_.refs_9_
  43.4 1.9 %collective-permute-start.11 = (f32[16,32,128]{2,1,0:T(8,128)}, f32[16,32,128]{2,1,0:T(8,128)S(1)}, u32[]{:S(2)}, u32[]{:S(2)}) collective-permute-start(f32[16,32,128]{2,1,0:T(8,128)} %refs_2_.1), channel_id=1, source_target_pairs={{0,32},{32,0},{64,96},{96,64},{128,160},{160,128},{192,224},{224,1... | collective-permute-start | bytes 786440 | tf_op jit(solution)/shard_map/ppermute | solution.py:375
  45.3 1.4 collective-permute-done.2.refs_2_.refs_5_.refs_7_
  46.7 1.9 %collective-permute-start.12 = (f32[16,24,128]{2,1,0:T(8,128)S(1)}, f32[16,24,128]{2,1,0:T(8,128)S(1)}, u32[]{:S(2)}, u32[]{:S(2)}) collective-permute-start(f32[16,24,128]{2,1,0:T(8,128)S(1)} %collective-permute-done.2.refs_2_.refs_5_.refs_7_), channel_id=1, source_target_pairs={{0,32},{32,0},{64,96},{96,64},{128,160},{160,128},{192,224},{224,1... | collective-permute-start | bytes 589832 | tf_op jit(solution)/shard_map/ppermute | solution.py:375
  48.6 0.0 collective-permute-done.3.refs_1_.refs_6_.refs_8_
  48.6 2.4 %collective-permute-start.13 = (f32[16,24,128]{2,1,0:T(8,128)S(1)}, f32[16,24,128]{2,1,0:T(8,128)S(1)}, u32[]{:S(2)}, u32[]{:S(2)}) collective-permute-start(f32[16,24,128]{2,1,0:T(8,128)S(1)} %collective-permute-done.3.refs_1_.refs_6_.refs_8_), channel_id=1, source_target_pairs={{0,32},{32,0},{64,96},{96,64},{128,160},{160,128},{192,224},{224,1... | collective-permute-start | bytes 589832 | tf_op jit(solution)/shard_map/ppermute | solution.py:375
  51.0 0.0 collective-permute-done.5.refs_3_.refs_8_
  51.0 0.0 collective-permute-done.6.refs_4_.refs_9_
  51.0 0.7 shard_map.52
  51.7 3.5 %collective-permute-start.7 = (f32[16,24,128]{2,1,0:T(8,128)}, f32[16,24,128]{2,1,0:T(8,128)S(1)}, u32[]{:S(2)}, u32[]{:S(2)}) collective-permute-start(f32[16,24,128]{2,1,0:T(8,128)} %get-tuple-element.29), channel_id=1, source_target_pairs={{0,8},{8,16},{16,24},{1,9},{9,17},{17,25},{2,10},{10,18},{18,26},{... | collective-permute-start | bytes 589832 | tf_op jit(solution)/shard_map/ppermute | solution.py:380
  55.2 1.3 collective-permute-start.8
  56.5 1.8 %select_reduce_fusion = (f32[256,256]{1,0:T(8,128)S(1)}, f32[256,256]{1,0:T(8,128)S(1)}) fusion(s32[256,256]{1,0:T(8,128)S(1)} %get-tuple-element.51, f32[17]{0:T(128)S(1)} %slice_bitcast_fusion, pred[256,256]{1,0:T(8,128)(4,1)S(1)} %get-tuple-element.53, pred[256,256]{1,0:T(8,128)(4,1)S(1)} %get-tuple-element.52, s32[256,256]{1,0:T(8,128)S(1)} %get-tuple-element.50), kind=kLoop, calls=%fused_computation | loop fusion | flops 8781824 | bytes 1179716 | tf_op jit(solution)/shard_map/reduce_sum | solution.py:366
  58.3 0.1 stack.31.refs_0_
  58.4 1.4 collective-permute-done.7.refs_1_.refs_10_
  59.8 3.8 %collective-permute-done.8.refs_2_.refs_11_ = f32[16,24,128]{2,1,0:T(8,128)S(1)} collective-permute-done((f32[16,24,128]{2,1,0:T(8,128)S(1)}, f32[16,24,128]{2,1,0:T(8,128)S(1)}, u32[]{:S(2)}, u32[]{:S(2)}) %collective-permute-start.8) | collective-permute-done | bytes 196640 | tf_op jit(solution)/shard_map/ppermute | solution.py:381
  63.6 1.4 shard_map.53
  65.0 1.3 collective-permute-start.9
  66.3 4.6 %collective-permute-start.10 = (f32[16,16,128]{2,1,0:T(8,128)S(1)}, f32[16,16,128]{2,1,0:T(8,128)S(1)}, u32[]{:S(2)}, u32[]{:S(2)}) collective-permute-start(f32[16,16,128]{2,1,0:T(8,128)S(1)} %get-tuple-element.32), channel_id=1, source_target_pairs={{0,1},{1,2},{2,3},{3,4},{4,5},{5,6},{6,7},{8,9},{9,10},{10,11},{11... | collective-permute-start | bytes 393224 | tf_op jit(solution)/shard_map/ppermute | solution.py:380
  70.9 0.0 collective-permute-done.11.refs_7_
  70.9 0.0 collective-permute-done.12.refs_10_
  70.9 0.0 collective-permute-done.13.refs_11_
  70.9 0.0 copy-start.1
  70.9 7.6 %shard_map.54 = (f32[48,80,128]{2,1,0:T(8,128)S(1)}, f32[48,80,128]{2,1,0:T(8,128)S(1)}, f32[48,80,128]{2,1,0:T(8,128)S(1)}, f32[48,80,128]{2,1,0:T(8,128)S(1)}) custom-call(s32[7]{0:T(128)S(1)} %stack.31.refs_0_, f32[256,256]{1,0:T(8,128)S(1)} %get-tuple-element.49.refs_1_.refs_2_, f32[16,32,128]{2,1,0:T(8,128)} %refs_2_.1, ...), custom_call_target="tpu_custom_call" | custom-call | flops 2000000000 | bytes 10485788 | tf_op jit(solution)/shard_map/pallas_call | solution.py:55
  78.5 0.0 collective-permute-done.9.refs_12_
  78.5 0.0 collective-permute-done.10.refs_13_
  78.5 0.0 copy-done.1
  78.5 14.0 %shard_map.55 = (f32[16,32,128]{2,1,0:T(8,128)}, f32[16,48,128]{2,1,0:T(8,128)S(1)}, f32[16,48,128]{2,1,0:T(8,128)S(1)}, f32[37,8,128]{2,1,0:T(8,128)S(1)}, f32[...) custom-call(s32[7]{0:T(128)S(1)} %stack.31.refs_0_, ...), custom_call_target="tpu_custom_call", output_to_operand_aliasing={{5}: (14, {}), {6}: (15, {}), {7}: (16, {}), {8}: (17, {})} | custom-call | flops 4000000000 | bytes 19701992 | tf_op jit(solution)/shard_map/pallas_call | solution.py:55
  92.6 6.1 %collective-permute-start.14 = (f32[37,8,128]{2,1,0:T(8,128)S(1)}, f32[37,8,128]{2,1,0:T(8,128)S(1)}, u32[]{:S(2)}, u32[]{:S(2)}) collective-permute-start(f32[37,8,128]{2,1,0:T(8,128)S(1)} %get-tuple-element.43), channel_id=1, source_target_pairs={{32,64},{64,32},{96,128},{128,96},{160,192},{192,160},{224,256},{2... | collective-permute-start | bytes 454664 | tf_op jit(solution)/shard_map/ppermute | solution.py:371
  98.7 3.9 %collective-permute-start.15 = (f32[37,8,128]{2,1,0:T(8,128)S(1)}, f32[37,8,128]{2,1,0:T(8,128)S(1)}, u32[]{:S(2)}, u32[]{:S(2)}) collective-permute-start(f32[37,8,128]{2,1,0:T(8,128)S(1)} %get-tuple-element.44), channel_id=1, source_target_pairs={{0,32},{32,0},{64,96},{96,64},{128,160},{160,128},{192,224},{224,1... | collective-permute-start | bytes 454664 | tf_op jit(solution)/shard_map/ppermute | solution.py:375
  102.6 5.9 %shard_map.56 = (f32[32,48,128]{2,1,0:T(8,128)S(1)}, f32[32,48,128]{2,1,0:T(8,128)S(1)}) custom-call(f32[48,80,128]{2,1,0:T(8,128)S(1)} %get-tuple-element.37.refs_0_.refs_3_, f32[48,80,128]{2,1,0:T(8,128)S(1)} %get-tuple-element.38.refs_1_.refs_4_), custom_call_target="tpu_custom_call" | custom-call | flops 2000000000 | bytes 5505024 | tf_op jit(solution)/shard_map/pallas_call | solution.py:55
  108.4 2.9 %collective-permute-done.14.refs_7_ = f32[37,8,128]{2,1,0:T(8,128)S(1)} collective-permute-done((f32[37,8,128]{2,1,0:T(8,128)S(1)}, f32[37,8,128]{2,1,0:T(8,128)S(1)}, u32[]{:S(2)}, u32[]{:S(2)}) %collective-permute-start.14) | collective-permute-done | bytes 151584 | tf_op jit(solution)/shard_map/ppermute | solution.py:371
  111.3 0.0 collective-permute-done.15.refs_8_
  111.3 7.4 %shard_map.57 = (f32[16,32,128]{2,1,0:T(8,128)S(1)}, f32[1,128]{1,0:T(1,128)S(1)}) custom-call(s32[7]{0:T(128)S(1)} %stack.31.refs_0_, f32[32,48,128]{2,1,0:T(8,128)S(1)} %get-tuple-element.39.refs_1_, f32[32,48,128]{2,1,0:T(8,128)S(1)} %get-tuple-element.40.refs_2_, f32[48,80,128]{2,1,0:T(8,128)S(1)} %get-tuple-element.37.refs_0_.refs_3_, ...), custom_call_target="tpu_custom_call" | custom-call | flops 2000000000 | bytes 6857244 | tf_op jit(solution)/shard_map/pallas_call | solution.py:55
  118.7 26.7 %all_to_all.10 = f32[32,1,128]{2,1,0:T(1,128)S(1)} all-to-all(f32[32,1,128]{2,1,0:T(1,128)S(1)} %broadcast_in_dim.19), channel_id=1, replica_groups=mesh['gx_0'=4,'gx_1'=2,'gx_2'=2,'gy'=4,'gz'=8] {'gx_1','gx_2','gz'}, dimensions={0} | all-to-all | bytes 32768 | tf_op jit(solution)/shard_map/all_to_all | solution.py:387
  145.4 13.1 %all_to_all.11.refs_0_ = f32[16,1,128]{2,1,0:T(1,128)S(1)} all-to-all(f32[16,1,128]{2,1,0:T(1,128)S(1)} %broadcast_in_dim.20), channel_id=1, replica_groups=mesh['gx_0'=4,'gx_1'=2,'gx_2'=2,'gy'=4,'gz'=8] {'gx_0','gy'}, dimensions={0} | all-to-all | bytes 16384 | tf_op jit(solution)/shard_map/all_to_all | solution.py:387
  158.5 0.8 shard_map.58
  (7 shorter events, 0.1 us)
Async XLA Ops:
  0.6 42.7 %collective-permute-start.4 = (f32[16,32,128]{2,1,0:T(8,128)}, f32[16,32,128]{2,1,0:T(8,128)S(1)}, u32[]{:S(2)}, u32[]{:S(2)}) collective-permute-start(f32[16,32,128]{2,1,0:T(8,128)} %refs_2_.1), channel_id=1, source_target_pairs={{32,64},{64,32},{96,128},{128,96},{160,192},{192,160},{224,256},{2... | collective-permute-start | bytes 786440 | tf_op jit(solution)/shard_map/ppermute | solution.py:371
  15.8 1.0 copy-start
  16.7 26.6 %copy-start.2 = (f32[3,17]{1,0:T(4,128)S(1)}, f32[3,17]{1,0:T(4,128)}, u32[]{:S(2)}) copy-start(f32[3,17]{1,0:T(4,128)} %refs_1_.5) | copy-start | bytes 616
  17.7 9.9 %collective-permute-start = (f32[16,32,128]{2,1,0:T(8,128)S(1)}, f32[16,32,128]{2,1,0:T(8,128)S(1)}, u32[]{:S(2)}, u32[]{:S(2)}) collective-permute-start(f32[16,32,128]{2,1,0:T(8,128)S(1)} %get-tuple-element.25), channel_id=1, source_target_pairs={{0,8},{8,16},{16,24},{1,9},{9,17},{17,25},{2,10},{10,18},{18,26},{... | collective-permute-start | bytes 786440 | tf_op jit(solution)/shard_map/ppermute | solution.py:380
  21.2 10.5 %collective-permute-start.1 = (f32[16,32,128]{2,1,0:T(8,128)S(1)}, f32[16,32,128]{2,1,0:T(8,128)S(1)}, u32[]{:S(2)}, u32[]{:S(2)}) collective-permute-start(f32[16,32,128]{2,1,0:T(8,128)S(1)} %get-tuple-element.26), channel_id=1, source_target_pairs={{8,0},{16,8},{24,16},{9,1},{17,9},{25,17},{10,2},{18,10},{26,18},{... | collective-permute-start | bytes 786440 | tf_op jit(solution)/shard_map/ppermute | solution.py:381
  27.6 23.4 %collective-permute-start.5 = (f32[16,32,128]{2,1,0:T(8,128)S(1)}, f32[16,32,128]{2,1,0:T(8,128)S(1)}, u32[]{:S(2)}, u32[]{:S(2)}) collective-permute-start(f32[16,32,128]{2,1,0:T(8,128)S(1)} %collective-permute-done.refs_2_.refs_3_.refs_5_), channel_id=1, source_target_pairs={{0,32},{32,0},{64,96},{96,64},{128,160},{160,128},{192,224},{224,1... | collective-permute-start | bytes 786440 | tf_op jit(solution)/shard_map/ppermute | solution.py:375
  31.8 19.2 %collective-permute-start.6 = (f32[16,32,128]{2,1,0:T(8,128)S(1)}, f32[16,32,128]{2,1,0:T(8,128)S(1)}, u32[]{:S(2)}, u32[]{:S(2)}) collective-permute-start(f32[16,32,128]{2,1,0:T(8,128)S(1)} %collective-permute-done.1.refs_3_.refs_4_.refs_6_), channel_id=1, source_target_pairs={{0,32},{32,0},{64,96},{96,64},{128,160},{160,128},{192,224},{224,1... | collective-permute-start | bytes 786440 | tf_op jit(solution)/shard_map/ppermute | solution.py:375
  37.5 9.2 %collective-permute-start.2 = (f32[16,24,128]{2,1,0:T(8,128)S(1)}, f32[16,24,128]{2,1,0:T(8,128)S(1)}, u32[]{:S(2)}, u32[]{:S(2)}) collective-permute-start(f32[16,24,128]{2,1,0:T(8,128)S(1)} %get-tuple-element.27), channel_id=1, source_target_pairs={{1,0},{2,1},{3,2},{4,3},{5,4},{6,5},{7,6},{9,8},{10,9},{11,10},{12... | collective-permute-start | bytes 589832 | tf_op jit(solution)/shard_map/ppermute | solution.py:381
  38.8 9.8 %collective-permute-start.3 = (f32[16,24,128]{2,1,0:T(8,128)S(1)}, f32[16,24,128]{2,1,0:T(8,128)S(1)}, u32[]{:S(2)}, u32[]{:S(2)}) collective-permute-start(f32[16,24,128]{2,1,0:T(8,128)S(1)} %get-tuple-element.28), channel_id=1, source_target_pairs={{0,1},{1,2},{2,3},{3,4},{4,5},{5,6},{6,7},{8,9},{9,10},{10,11},{11... | collective-permute-start | bytes 589832 | tf_op jit(solution)/shard_map/ppermute | solution.py:380
  43.4 27.5 %collective-permute-start.11 = (f32[16,32,128]{2,1,0:T(8,128)}, f32[16,32,128]{2,1,0:T(8,128)S(1)}, u32[]{:S(2)}, u32[]{:S(2)}) collective-permute-start(f32[16,32,128]{2,1,0:T(8,128)} %refs_2_.1), channel_id=1, source_target_pairs={{0,32},{32,0},{64,96},{96,64},{128,160},{160,128},{192,224},{224,1... | collective-permute-start | bytes 786440 | tf_op jit(solution)/shard_map/ppermute | solution.py:375
  46.7 24.3 %collective-permute-start.12 = (f32[16,24,128]{2,1,0:T(8,128)S(1)}, f32[16,24,128]{2,1,0:T(8,128)S(1)}, u32[]{:S(2)}, u32[]{:S(2)}) collective-permute-start(f32[16,24,128]{2,1,0:T(8,128)S(1)} %collective-permute-done.2.refs_2_.refs_5_.refs_7_), channel_id=1, source_target_pairs={{0,32},{32,0},{64,96},{96,64},{128,160},{160,128},{192,224},{224,1... | collective-permute-start | bytes 589832 | tf_op jit(solution)/shard_map/ppermute | solution.py:375
  48.6 22.3 %collective-permute-start.13 = (f32[16,24,128]{2,1,0:T(8,128)S(1)}, f32[16,24,128]{2,1,0:T(8,128)S(1)}, u32[]{:S(2)}, u32[]{:S(2)}) collective-permute-start(f32[16,24,128]{2,1,0:T(8,128)S(1)} %collective-permute-done.3.refs_1_.refs_6_.refs_8_), channel_id=1, source_target_pairs={{0,32},{32,0},{64,96},{96,64},{128,160},{160,128},{192,224},{224,1... | collective-permute-start | bytes 589832 | tf_op jit(solution)/shard_map/ppermute | solution.py:375
  51.7 8.1 %collective-permute-start.7 = (f32[16,24,128]{2,1,0:T(8,128)}, f32[16,24,128]{2,1,0:T(8,128)S(1)}, u32[]{:S(2)}, u32[]{:S(2)}) collective-permute-start(f32[16,24,128]{2,1,0:T(8,128)} %get-tuple-element.29), channel_id=1, source_target_pairs={{0,8},{8,16},{16,24},{1,9},{9,17},{17,25},{2,10},{10,18},{18,26},{... | collective-permute-start | bytes 589832 | tf_op jit(solution)/shard_map/ppermute | solution.py:380
  55.2 8.4 %collective-permute-start.8 = (f32[16,24,128]{2,1,0:T(8,128)S(1)}, f32[16,24,128]{2,1,0:T(8,128)S(1)}, u32[]{:S(2)}, u32[]{:S(2)}) collective-permute-start(f32[16,24,128]{2,1,0:T(8,128)S(1)} %get-tuple-element.30), channel_id=1, source_target_pairs={{8,0},{16,8},{24,16},{9,1},{17,9},{25,17},{10,2},{18,10},{26,18},{... | collective-permute-start | bytes 589832 | tf_op jit(solution)/shard_map/ppermute | solution.py:381
  65.0 13.5 %collective-permute-start.9 = (f32[16,16,128]{2,1,0:T(8,128)S(1)}, f32[16,16,128]{2,1,0:T(8,128)S(1)}, u32[]{:S(2)}, u32[]{:S(2)}) collective-permute-start(f32[16,16,128]{2,1,0:T(8,128)S(1)} %get-tuple-element.31), channel_id=1, source_target_pairs={{1,0},{2,1},{3,2},{4,3},{5,4},{6,5},{7,6},{9,8},{10,9},{11,10},{12... | collective-permute-start | bytes 393224 | tf_op jit(solution)/shard_map/ppermute | solution.py:381
  66.3 12.2 %collective-permute-start.10 = (f32[16,16,128]{2,1,0:T(8,128)S(1)}, f32[16,16,128]{2,1,0:T(8,128)S(1)}, u32[]{:S(2)}, u32[]{:S(2)}) collective-permute-start(f32[16,16,128]{2,1,0:T(8,128)S(1)} %get-tuple-element.32), channel_id=1, source_target_pairs={{0,1},{1,2},{2,3},{3,4},{4,5},{5,6},{6,7},{8,9},{9,10},{10,11},{11... | collective-permute-start | bytes 393224 | tf_op jit(solution)/shard_map/ppermute | solution.py:380
  70.9 7.6 %copy-start.1 = (f32[16,32,128]{2,1,0:T(8,128)S(1)}, f32[16,32,128]{2,1,0:T(8,128)}, u32[]{:S(2)}) copy-start(f32[16,32,128]{2,1,0:T(8,128)} %refs_4_.1) | copy-start | bytes 786436
  92.6 18.7 %collective-permute-start.14 = (f32[37,8,128]{2,1,0:T(8,128)S(1)}, f32[37,8,128]{2,1,0:T(8,128)S(1)}, u32[]{:S(2)}, u32[]{:S(2)}) collective-permute-start(f32[37,8,128]{2,1,0:T(8,128)S(1)} %get-tuple-element.43), channel_id=1, source_target_pairs={{32,64},{64,32},{96,128},{128,96},{160,192},{192,160},{224,256},{2... | collective-permute-start | bytes 454664 | tf_op jit(solution)/shard_map/ppermute | solution.py:371
  98.7 12.7 %collective-permute-start.15 = (f32[37,8,128]{2,1,0:T(8,128)S(1)}, f32[37,8,128]{2,1,0:T(8,128)S(1)}, u32[]{:S(2)}, u32[]{:S(2)}) collective-permute-start(f32[37,8,128]{2,1,0:T(8,128)S(1)} %get-tuple-element.44), channel_id=1, source_target_pairs={{0,32},{32,0},{64,96},{96,64},{128,160},{160,128},{192,224},{224,1... | collective-permute-start | bytes 454664 | tf_op jit(solution)/shard_map/ppermute | solution.py:375

commit v4 on v3

v4 whole, which is shorter than its diff:
```python
import functools

import jax
import jax.numpy as jnp
import numpy as np
from jax import lax
from jax.experimental import pallas as pl
from jax.experimental.pallas import tpu as pltpu
from jax.sharding import Mesh
from jax.sharding import PartitionSpec as P

RINGS = (("gx_1", "gx_2", "gz"), ("gx_0", "gy"))
GX = ("gx_0", "gx_1", "gx_2")
LAP_COEF = (-205.0 / 72.0, 8.0 / 5.0, -1.0 / 5.0, 8.0 / 315.0, -1.0 / 560.0)
STEP = 0.08
F32 = jnp.float32
LANES = 128


def lane_ids(shape):
    return lax.broadcasted_iota(jnp.int32, shape, len(shape) - 1)


def pack(rows_of, count, cells, offset):
    lanes = lane_ids((8, LANES))
    first = last = None
    for q in range(count):
        at = offset + cells * q
        here = (lanes >= at) & (lanes < at + cells)
        rows = rows_of(q)
        head = pltpu.roll(rows, at, 1) if at else rows
        tail = pltpu.roll(rows, (at + cells) % LANES, 1)
        first = jnp.where(here, head, 0.0 if first is None else first)
        last = jnp.where(here, tail, 0.0 if last is None else last)
    return first, last


def unpack(right, left, at, cells):
    lanes = lane_ids((8, LANES))
    high = pltpu.roll(right, (LANES - at) % LANES, 1) if at % LANES else right
    low = pltpu.roll(left, (2 * LANES - cells - at) % LANES, 1)
    return jnp.where(lanes < cells, high, jnp.where(lanes >= LANES - cells, low, 0.0))


def skipping(body, start, count, *refs):
    body(*refs[:start], *refs[start + count :])


def call(body, outs, scratch, *args, scalars=0, flops=1000, after=()):
    specs = [pl.BlockSpec(memory_space=pltpu.SMEM)] * scalars
    specs += [pl.BlockSpec(memory_space=pltpu.VMEM)] * (len(args) - scalars)
    specs += [pl.BlockSpec(memory_space=pl.ANY)] * len(after)
    body = functools.partial(skipping, body, len(args), len(after))
    shapes = [jax.ShapeDtypeStruct(s, F32) for s in outs]
    nbytes = 4 * sum(a.size for a in args) + 4 * sum(s.size for s in shapes)
    return pl.pallas_call(
        body,
        out_shape=shapes,
        in_specs=specs,
        out_specs=[pl.BlockSpec(memory_space=pltpu.VMEM)] * len(outs),
        scratch_shapes=[pltpu.VMEM(s, F32) for s in scratch],
        compiler_params=pltpu.CompilerParams(vmem_limit_bytes=20 * 1024 * 1024),
        cost_estimate=pl.CostEstimate(flops=flops, bytes_accessed=nbytes, transcendentals=0),
    )(*args, *after)


def cut(wave, external, head, tail):
    head[:, 0:24, :] = wave[:, 0:24, :]
    head[:, 24:32, :] = external[:, 0:8, :]
    tail[:, 0:24, :] = wave[:, 8:32, :]
    tail[:, 24:32, :] = external[:, 24:32, :]


def cut_outer(outer, head, tail):
    head[...] = outer[:, 0:24, :]
    tail[...] = outer[:, 8:32, :]


def stacked(x, low, mid, high):
    def rows_of(q):
        for ref, start, stop in (low, mid, high):
            count = (stop - start) // 8
            if q < count:
                return ref[x, start + 8 * q : start + 8 * q + 8, :]
            q -= count

    return rows_of


def pack_cells(wave, low, high, first, last):
    def plane(x, carry):
        rows_of = stacked(x, (low, 0, 24), (wave, 0, 32), (high, 0, 24))
        for r in range(2):
            rows = slice(8 * r, 8 * r + 8)
            first[x, rows, :], last[x, rows, :] = pack(lambda q: rows_of(q + 5 * r), 5, 24, 0)
        return carry

    lax.fori_loop(0, 16, plane, 0, unroll=2)


def pack_both(wave, external, low, high, first, last, rows):
    pack_cells(wave, low, high, first, last)
    rows[:, 0:24, :] = low[:, 0:24, :]
    rows[:, 24:48, :] = high[:, 0:24, :]

    def plane(x, carry):
        rows_of = stacked(x, (low, 24, 32), (external, 0, 32), (high, 24, 32))
        first[x, 16:24, :], last[x, 16:24, :] = pack(rows_of, 6, 8, 0)
        return carry

    lax.fori_loop(0, 16, plane, 0, unroll=2)


def pack_outer(wave, low, high, right, left, first, last, sides):
    pack_cells(wave, low, high, first, last)
    sides[:, 0:16, :] = right[:, 0:16, :]
    sides[:, 16:32, :] = left[:, 0:16, :]


def fill(own, rim, base, mid, low, high, right, left):
    def plane(x, carry):
        own[base + x, 0:24, :] = low[x, 0:24, :]
        own[base + x, 24:56, :] = mid[x]
        own[base + x, 56:80, :] = high[x, 0:24, :]
        for g in range(10):
            rows = slice(8 * (g // 5), 8 * (g // 5) + 8)
            rim[base + x, 8 * g : 8 * g + 8, :] = unpack(right[x, rows, :], left[x, rows, :], 24 * (g % 5), 24)
        return carry

    lax.fori_loop(0, 16, plane, 0, unroll=4)


def halves(x):
    top = x.astype(jnp.bfloat16)
    return top, (x - top.astype(F32)).astype(jnp.bfloat16)


def times(x, matrix_halves):
    top, rest = halves(x)
    big, small = matrix_halves
    dot = functools.partial(jnp.dot, preferred_element_type=F32)
    return dot(top, big) + (dot(top, small) + dot(rest, big))


def slide(src, base, dst, taps, groups):
    count = dst.shape[0]

    def column(g, carry):
        rows = pl.ds(pl.multiple_of(8 * g, 8), 8)
        sums = {}
        for j in range(count + 16):
            value = src[base + j, rows, :]
            for a in range(17):
                i = j - a
                if 0 <= i < count:
                    term = taps[a] * value
                    sums[i] = sums[i] + term if a else term
            if j >= 16:
                dst[j - 16, rows, :] = sums.pop(j - 16)
        return carry

    lax.fori_loop(0, groups, column, 0)


def along_rows(src, x, taps, count):
    total = taps[0] * src[x, 0:count, :]
    for b in range(1, 17):
        total = total + taps[b] * src[x, b : b + count, :]
    return total


def along_z(own, rim, g_own, g_rim, base, spread_halves, start=None):
    start = base if start is None else start

    def chunk(k, carry):
        planes = pl.ds(start + 8 * k, 8)
        a = own[planes].reshape(640, LANES)
        b = rim[planes].reshape(640, LANES)
        out = times(jnp.concatenate([a * a, b * b], axis=1), spread_halves)
        planes = pl.ds(base + 8 * k, 8)
        g_own[planes] = out[:, :LANES].reshape(8, 80, LANES)
        g_rim[planes] = out[:, LANES:].reshape(8, 80, LANES)
        return carry

    lax.fori_loop(0, 2, chunk, 0)


def sources(weights, field, at, g_own, g_rim, base, s_own, s_rim, to, c_own, c_rim, h_own, h_rim):
    x_taps = [weights[0, a] for a in range(17)]
    y_taps = [weights[1, a] for a in range(17)]
    slide(g_own, base, h_own, x_taps, 10)
    slide(g_rim, base, h_rim, x_taps, 10)

    def source(x, carry):
        for h, e, s, c in ((h_own, field[0], s_own, c_own), (h_rim, field[1], s_rim, c_rim)):
            coarse = along_rows(h, x, y_taps, 64)
            wave = e[at + x, 8:72, :]
            density = wave * wave
            s[to + x] = -1.0 * density * coarse + 0.5 * density * coarse * coarse
            c[x] = coarse
        return carry

    lax.fori_loop(0, 16, source, 0)


def band(weights, flip):
    def places(dim):
        at = lax.broadcasted_iota(jnp.int32, (256, 256), dim)
        return jnp.where(at < 192, at, at - 256)

    start, end = places(0), places(1)
    margin = 8 if flip else 16
    offset = (end - start if flip else start - end) + 8
    used = (end >= -margin) & (end < LANES + margin) & (start >= -margin - 8) & (start < LANES + margin + 8)
    offset = jnp.where(used, offset, -1)
    matrix = jnp.zeros((256, 256), F32)
    for tap in range(17):
        matrix = jnp.where(offset == tap, weights[2, tap], matrix)
    return matrix


def bands(weights, spread, gather):
    spread[...] = band(weights, False)
    gather[...] = band(weights, True)


def prepare(
    flags, weights, spread, wave, low, high, right, left, inner, i_rows, i_sides,
    own, rim, g_own, g_rim, s_own, s_rim, c_own, c_rim, k_own, k_rim, h_own, h_rim,
):
    spread_halves = halves(spread[...])
    upper = flags[0]
    mine, other = 16 * upper, 16 * (1 - upper)
    fill(own, rim, mine, wave, low, high, right, left)
    i_low, i_high = i_rows.at[:, 0:24, :], i_rows.at[:, 24:48, :]
    i_right, i_left = i_sides.at[:, 0:16, :], i_sides.at[:, 16:32, :]
    fill(own, rim, other, inner, i_low, i_high, i_right, i_left)
    along_z(own, rim, k_own, k_rim, 0, spread_halves)
    along_z(own, rim, k_own, k_rim, 16, spread_halves)
    g_own[...] = k_own[pl.ds(mine, 16)]
    g_rim[...] = k_rim[pl.ds(mine, 16)]
    sources(weights, (own, rim), 8, k_own, k_rim, 0, s_own, s_rim, 0, c_own, c_rim, h_own, h_rim)


def potentials(
    side, weights, gather, external, low, high, right, left, s_own, s_rim, c_own, c_rim, at_c,
    corr, v_own, v_rim, slab, t_own, t_rim, u_own, u_rim,
):
    x_taps = [weights[0, 16 - a] for a in range(17)]
    y_taps = [weights[1, 16 - a] for a in range(17)]
    base = 8 * side
    slide(s_own, base, t_own, x_taps, 8)
    slide(s_rim, base, t_rim, x_taps, 8)

    def back(x, carry):
        u_own[x] = along_rows(t_own, x, y_taps, 48)
        u_rim[x] = along_rows(t_rim, x, y_taps, 48)
        return carry

    lax.fori_loop(0, 8, back, 0)
    both = jnp.concatenate([u_own[...].reshape(384, LANES), u_rim[...].reshape(384, LANES)], axis=1)
    smeared = times(both, halves(gather[...]))
    planes = pl.ds(base, 8)
    for c, v, part in ((c_own, v_own, smeared[:, :LANES]), (c_rim, v_rim, smeared[:, LANES:])):
        coarse = c[pl.ds(at_c, 8), 8:56, :]
        v[...] = -0.5 * coarse * coarse + 0.5 / 3.0 * coarse * coarse * coarse + part.reshape(8, 48, LANES)
    corr[...] = v_own[:, 8:40, :]
    v_own[:, 0:8, :] += low[planes, 24:32, :]
    v_own[:, 8:40, :] += external[planes]
    v_own[:, 40:48, :] += high[planes, 24:32, :]
    for x in range(8):
        for q in range(6):
            v_rim[x, 8 * q : 8 * q + 8, :] += unpack(right[base + x, 16:24, :], left[base + x, 16:24, :], 8 * q, 8)

    lanes = lane_ids((8, LANES))
    edge, beyond = 4 * side, 4 - 4 * side
    rims = jnp.zeros((8, LANES), F32)
    for i in range(4):
        for q in range(5):
            slab[5 * i + q] = v_own[edge + i, 4 + 8 * q : 12 + 8 * q, :]
        for q in range(4):
            slab[20 + 4 * i + q] = v_own[beyond + i, 8 + 8 * q : 16 + 8 * q, :]
            at = 8 * (4 * i + q)
            these = (lanes >= at) & (lanes < at + 8)
            rims = jnp.where(these, pltpu.roll(v_rim[edge + i, 8 + 8 * q : 16 + 8 * q, :], (at + 4) % LANES, 1), rims)
    slab[36] = rims


def far_side(
    flags, weights, spread, gather, external, low, high, right, left, outer, o_low, o_high, o_right, o_left,
    own, rim, g_own, g_rim, s_own, s_rim, out_own, out_rim, s_all_own, s_all_rim, corr, v_own, v_rim, slab,
    e_own, e_rim, k_own, k_rim, c_own, c_rim, h_own, h_rim, t_own, t_rim, u_own, u_rim,
):
    upper = flags[0]
    below = 1 - upper
    fill(out_own, out_rim, 0, outer, o_low, o_high, o_right, o_left)
    along_z(out_own, out_rim, k_own, k_rim, 16 * upper, halves(spread[...]), 0)
    mine = pl.ds(16 * below, 16)
    k_own[mine] = g_own[...]
    k_rim[mine] = g_rim[...]
    for e, out, field in ((e_own, out_own, own), (e_rim, out_rim, rim)):
        e[pl.ds(8 * upper, 8)] = out[pl.ds(8 * below, 8)]
        e[pl.ds(8 * below, 8)] = field[pl.ds(24 * upper, 8)]
    for s_all, s in ((s_all_own, s_own), (s_all_rim, s_rim)):
        s_all[pl.ds(16 * below, 16)] = s[...]
    sources(
        weights, (e_own, e_rim), 0, k_own, k_rim, 0, s_all_own, s_all_rim, 16 * upper, c_own, c_rim, h_own, h_rim
    )
    potentials(
        upper, weights, gather, external, low, high, right, left, s_all_own, s_all_rim, c_own, c_rim, 8 * below,
        corr, v_own, v_rim, slab, t_own, t_rim, u_own, u_rim,
    )


def near_side(
    flags, weights, gather, external, low, high, right, left, s_own, s_rim, c_own, c_rim, far_corr,
    corr, v_own, v_rim, slab, near_corr, t_own, t_rim, u_own, u_rim,
):
    upper = flags[0]
    below = 1 - upper
    potentials(
        below, weights, gather, external, low, high, right, left, s_own, s_rim, c_own, c_rim, 8 * upper,
        near_corr, v_own, v_rim, slab, t_own, t_rim, u_own, u_rim,
    )
    corr[pl.ds(8 * below, 8)] = near_corr[...]
    corr[pl.ds(8 * upper, 8)] = far_corr[...]


def laplace(own, rim, x, count, start, rows, shifts, with_rim):
    planes = pl.ds(x, count)
    here = slice(start, start + rows)
    centers = own[planes, here, :], rim[planes, here, :]
    flat = [c.reshape(count * rows, LANES) for c in centers]
    shifted = times(jnp.concatenate(flat, axis=1), shifts)
    answers = []
    for ref in range(2 if with_rim else 1):
        field = (own, rim)[ref]
        part = shifted[:, LANES * ref : LANES * ref + LANES].reshape(count, rows, LANES)
        total = (1.0 + 0.5 * STEP * 3.0 * LAP_COEF[0]) * centers[ref] + part
        for k in range(1, 5):
            near = field[pl.ds(x + k, count), here, :] + field[pl.ds(x - k, count), here, :]
            near = near + (field[planes, start + k : start + k + rows, :] + field[planes, start - k : start - k + rows, :])
            total = total + (0.5 * STEP * LAP_COEF[k]) * near
        answers.append(total)
    return answers


def ring_shifts():
    gap = np.abs(np.arange(256)[:, None] - np.arange(256)[None, :])
    gap = np.minimum(gap, 256 - gap)
    matrix = np.zeros((256, 256), np.float32)
    for k in range(1, 5):
        matrix[gap == k] = 0.5 * STEP * LAP_COEF[k]
    return matrix


def first_step(flags, shifts, own, rim, out_own, out_rim, p_own, p_rim, e_own, e_rim):
    shift_halves = halves(shifts[...])
    upper = flags[0]
    for e, field, out in ((e_own, own, out_own), (e_rim, rim, out_rim)):
        e[pl.ds(16 * (1 - upper), 32)] = field[...]
        e[pl.ds(32 * upper, 16)] = out[...]

    def planes(k, carry):
        at = pl.ds(4 * k, 4)
        p_own[at], p_rim[at] = laplace(e_own, e_rim, 4 * k + 8, 4, 16, 48, shift_halves, True)
        return carry

    lax.fori_loop(0, 8, planes, 0)


def add_halo(slab, side, v_own, v_rim):
    lanes = lane_ids((8, LANES))
    edge, beyond = 4 + 20 * side, 28 * side
    empty = jnp.zeros((48, LANES), F32)
    for i in range(4):
        v_own[beyond + i] = empty
        v_rim[beyond + i] = empty
        v_own[edge + i] = empty
        v_rim[edge + i] = empty
        for q in range(5):
            v_own[edge + i, 4 + 8 * q : 12 + 8 * q, :] = slab[5 * i + q]
        for q in range(4):
            v_own[beyond + i, 8 + 8 * q : 16 + 8 * q, :] = slab[20 + 4 * i + q]
            rim = pltpu.roll(slab[36], (2 * LANES - 4 - 8 * (4 * i + q)) % LANES, 1)
            v_rim[edge + i, 8 + 8 * q : 16 + 8 * q, :] = jnp.where((lanes < 4) | (lanes >= LANES - 4), rim, 0.0)


def masks(flags, count, edge):
    rows = lax.broadcasted_iota(jnp.int32, (count, LANES), 0) - edge
    lanes = lane_ids((count, LANES))
    in_rows = (rows >= flags[3]) & (rows < flags[4])
    in_rim = ((lanes >= 64) & (flags[5] != 0)) | ((lanes < 64) & (flags[6] != 0))
    rows_one = jnp.where(in_rows, 1.0, 0.0)
    return rows_one, jnp.where(in_rim, rows_one, 0.0)


def steps(
    flags, shifts, p_own, p_rim, q_own, q_rim, at_q, v_own, v_rim, a_own, a_rim, b_own, b_rim, psi, one, two, three
):
    shift_halves = halves(shifts[...])
    last_halves = [m[:, :LANES] for m in shift_halves]

    def inside(x, edge):
        return jnp.where((x - edge >= flags[1]) & (x - edge < flags[2]), 1.0, 0.0)

    keep_own, keep_rim = masks(flags, 48, 8)

    def step_one(k, carry):
        x = one[0] + k
        keep = inside(x, 8)
        a_own[x] = (p_own[x] - STEP * v_own[x] * q_own[at_q + k, 16:64, :]) * (keep * keep_own)
        a_rim[x] = (p_rim[x] - STEP * v_rim[x] * q_rim[at_q + k, 16:64, :]) * (keep * keep_rim)
        return carry

    lax.fori_loop(0, one[1], step_one, 0, unroll=2)
    mid_own, mid_rim = masks(flags, 40, 4)

    def step_two(k, carry):
        x = two[0] + 4 * k
        at = pl.ds(x + 4, 4)
        fields = laplace(a_own, a_rim, x + 4, 4, 4, 40, shift_halves, True)
        for a, b, v, field, mask in (
            (a_own, b_own, v_own, fields[0], mid_own),
            (a_rim, b_rim, v_rim, fields[1], mid_rim),
        ):
            field = field - STEP * (v[at, 4:44, :] * a[at, 4:44, :])
            for i in range(4):
                b[x + i] = field[i] * (inside(x + i, 4) * mask)
        return carry

    lax.fori_loop(0, two[1] // 4, step_two, 0)

    def step_three(k, total):
        x = three[0] + 4 * k
        (field,) = laplace(b_own, b_rim, x + 4, 4, 4, 32, last_halves, False)
        field = field - STEP * (v_own[pl.ds(x + 8, 4), 8:40, :] * b_own[pl.ds(x + 4, 4), 4:36, :])
        psi[pl.ds(4 * k, 4)] = field
        return total + jnp.sum(field * field, axis=0)

    total = lax.fori_loop(0, three[1] // 4, step_three, jnp.zeros((32, LANES), F32))
    return jnp.sum(total, axis=0, keepdims=True)


def near_steps(
    flags, shifts, p_own, p_rim, q_own, q_rim, slab, v_far_own, v_far_rim, v_near_own, v_near_rim,
    a_kept_own, a_kept_rim, b_kept_own, b_kept_rim, psi, squares, v_own, v_rim, a_own, a_rim, b_own, b_rim,
):
    upper = flags[0]
    below = 1 - upper
    for v, far, near in ((v_own, v_far_own, v_near_own), (v_rim, v_far_rim, v_near_rim)):
        v[pl.ds(8 + 8 * upper, 8)] = far[...]
        v[pl.ds(8 + 8 * below, 8)] = near[...]
    add_halo(slab, below, v_own, v_rim)
    squares[...] = steps(
        flags, shifts, p_own, p_rim, q_own, q_rim, 8 * upper, v_own, v_rim, a_own, a_rim, b_own, b_rim, psi,
        (8 * below, 24), (8 * below, 16), (8 * below, 8),
    )
    a_kept_own[...] = a_own[pl.ds(8 + 8 * upper, 8)]
    a_kept_rim[...] = a_rim[pl.ds(8 + 8 * upper, 8)]
    b_kept_own[...] = b_own[8:16]
    b_kept_rim[...] = b_rim[8:16]


def far_steps(
    flags, shifts, p_own, p_rim, q_own, q_rim, slab, v_far_own, v_far_rim, near_squares,
    a_kept_own, a_kept_rim, b_kept_own, b_kept_rim, psi, squares, v_own, v_rim, a_own, a_rim, b_own, b_rim,
):
    upper = flags[0]
    below = 1 - upper
    v_own[pl.ds(8 + 8 * upper, 8)] = v_far_own[...]
    v_rim[pl.ds(8 + 8 * upper, 8)] = v_far_rim[...]
    a_own[pl.ds(8 + 8 * upper, 8)] = a_kept_own[...]
    a_rim[pl.ds(8 + 8 * upper, 8)] = a_kept_rim[...]
    b_own[8:16] = b_kept_own[...]
    b_rim[8:16] = b_kept_rim[...]
    add_halo(slab, upper, v_own, v_rim)
    squares[...] = near_squares[...] + steps(
        flags, shifts, p_own, p_rim, q_own, q_rim, 8 * below, v_own, v_rim, a_own, a_rim, b_own, b_rim, psi,
        (24 * upper, 8), (16 * upper, 8), (8 * upper, 8),
    )


def scale(count, flags, rows, near_psi, far_psi, out):
    total = jnp.sum(rows[...].reshape(-1, LANES), axis=0, keepdims=True)
    total = jnp.sum(total, axis=1, keepdims=True)
    factor = lax.rsqrt(total / count + 1e-06)
    upper = flags[0]
    out[pl.ds(8 * (1 - upper), 8)] = near_psi[...] * factor[None]
    out[pl.ds(8 * upper, 8)] = far_psi[...] * factor[None]


def swap_far(planes):
    count = lax.axis_size(GX)
    return lax.ppermute(planes, GX, [p for k in range(1, count - 1, 2) for p in ((k, k + 1), (k + 1, k))])


def swap_near(planes):
    return lax.ppermute(planes, GX, [(k, k ^ 1) for k in range(lax.axis_size(GX))])


def shift(head, tail, axis):
    ends = lax.axis_size(axis) - 1
    low = lax.ppermute(tail, axis, [(i, i + 1) for i in range(ends)])
    high = lax.ppermute(head, axis, [(i + 1, i) for i in range(ends)])
    return low, high


def spread(row, axes):
    count = lax.axis_size(axes)
    return lax.all_to_all(jnp.broadcast_to(row[None], (count, *row.shape)), axes, 0, 0, tiled=True)


def shards(wave, external, weights):
    at = [lax.axis_index(axis) for axis in (GX, "gy", "gz")]
    last = [at[d] == lax.axis_size(axis) - 1 for d, axis in enumerate((GX, "gy", "gz"))]
    far = 1 << 20
    flags = jnp.stack(
        [
            lax.axis_index("gx_2"),
            jnp.where(at[0] == 0, 0, -far),
            jnp.where(last[0], wave.shape[0], far),
            jnp.where(at[1] == 0, 0, -far),
            jnp.where(last[1], wave.shape[1], far),
            jnp.where(at[2] == 0, 0, 1),
            jnp.where(last[2], 0, 1),
        ]
    ).astype(jnp.int32)
    block = wave.shape
    outer = swap_far(wave)
    inner = swap_near(wave)
    head, tail = call(cut, [block] * 2, [], wave, external)
    low, high = shift(head, tail, "gy")
    smear_z, gather_z = call(bands, [(256, 256)] * 2, [], weights, scalars=1, flops=10**10)
    first, final, rows = call(
        pack_both,
        [(16, 24, LANES)] * 2 + [(16, 48, LANES)],
        [],
        wave, external, low, high,
        after=(inner, smear_z),
    )
    left, right = shift(first, final, "gz")
    i_rows = swap_near(rows)
    o_low, o_high = shift(*call(cut_outer, [(16, 24, LANES)] * 2, [], outer, after=(first, final)), "gy")
    first, final, sides = call(
        pack_outer, [(16, 16, LANES)] * 2 + [(16, 32, LANES)], [], outer, o_low, o_high, right, left
    )
    o_left, o_right = shift(first, final, "gz")
    i_sides = swap_near(sides)

    def twice(*shape):
        return [(*shape, LANES)] * 2

    own, rim, g_own, g_rim, s_own, s_rim, c_own, c_rim = call(
        prepare,
        twice(32, 80) + twice(16, 80) + twice(16, 64) + twice(16, 64),
        twice(32, 80) + twice(16, 80),
        flags, weights, smear_z, wave, low, high, right, left, inner, i_rows, i_sides,
        scalars=2,
    )
    halo = (low, high, right, left)
    out_own, out_rim, s_own, s_rim, far_corr, v_far_own, v_far_rim, outward = call(
        far_side,
        twice(16, 80) + twice(32, 64) + [(8, 32, LANES)] + twice(8, 48) + [(37, 8, LANES)],
        twice(16, 80) + twice(32, 80) + twice(16, 64) + twice(16, 80) + twice(8, 64) + twice(8, 48),
        flags, weights, smear_z, gather_z, external, *halo, outer, o_low, o_high, o_right, o_left,
        own, rim, g_own, g_rim, s_own, s_rim,
        scalars=2,
    )
    v_outer = swap_far(outward)
    corr, v_near_own, v_near_rim, inward = call(
        near_side,
        [block] + twice(8, 48) + [(37, 8, LANES)],
        [(8, 32, LANES)] + twice(8, 64) + twice(8, 48),
        flags, weights, gather_z, external, *halo, s_own, s_rim, c_own, c_rim, far_corr,
        scalars=2,
    )
    v_inner = swap_near(inward)
    shifts = jnp.asarray(ring_shifts())
    p_own, p_rim = call(
        first_step, twice(32, 48), twice(48, 80), flags, shifts, own, rim, out_own, out_rim, scalars=1, flops=10**10
    )
    scratch = twice(32, 48) * 2 + twice(24, 40)
    *kept, near_psi, squares = call(
        near_steps, twice(8, 48) + twice(8, 40) + [(8, 32, LANES), (1, LANES)], scratch,
        flags, shifts, p_own, p_rim, own, rim, v_inner, v_far_own, v_far_rim, v_near_own, v_near_rim,
        scalars=1,
    )
    far_psi, squares = call(
        far_steps, [(8, 32, LANES), (1, LANES)], scratch,
        flags, shifts, p_own, p_rim, out_own, out_rim, v_outer, v_far_own, v_far_rim, squares, *kept,
        scalars=1,
    )
    rows = spread(jnp.sum(spread(squares, RINGS[0]), axis=0), RINGS[1])
    count = float(wave.size * lax.axis_size(GX) * lax.axis_size("gy") * lax.axis_size("gz"))
    (wave_next,) = call(functools.partial(scale, count), [block], [], flags, rows, near_psi, far_psi, scalars=1)
    return (wave_next, corr)


def solution(mesh):
    torus = Mesh(
        mesh.devices.reshape(4, 2, 2, mesh.shape["gy"], mesh.shape["gz"]),
        ("gx_0", "gx_1", "gx_2", "gy", "gz"),
    )
    placed = (P(GX, "gy", "gz"), P(GX, "gy", "gz"), P())
    return jax.shard_map(
        shards,
        mesh=torus,
        in_specs=placed,
        out_specs=(P(GX, "gy", "gz"), P(GX, "gy", "gz")),
        check_vma=False,
    )
```

time: 160 us -> 148 us (0.925)
  Pallas kernels: 42.4 us -> 32.6 us
  waiting for transfers between devices: 16.7 us -> 12.6 us
  other arithmetic: 2.08 us -> 0.02 us
  local copies, waits for them, and re-layouts: 1.06 us -> 2.7 us
    pallas_call x9 -> x12, Pallas kernels: 42.4 us -> 32.6 us  [call(): pl.pallas_call(body, out_shape=shapes, in_specs=specs, out_specs=[pl.Bloc...]
    ppermute x6 -> x4, starting transfers between devices: 13.9 us -> 7.81 us  [swap_near(): lax.ppermute(planes, GX, [(k, k ^ 1) for k in range(lax.axis_size(GX))])]
    ppermute x2, starting transfers between devices: 21.2 us -> 27.2 us  [swap_far(): lax.ppermute(planes, GX, [p for k in range(1, count - 1, 2) for p in ((k,...]
    ppermute x4, waiting for transfers between devices: 6.36 us -> 2.62 us  [shift(): low = lax.ppermute(tail, axis, [(i, i + 1) for i in range(ends)])]
    reduce_sum x1 -> x0, other arithmetic: 1.8 us -> none  [band(): return jnp.sum(jnp.where(hits, row, 0.0), axis=2)]
    unnamed x6 -> x14, local copies, waits for them, and re-layouts: 0.96 us -> 2.59 us
  transfers between devices with their start and end apart: 16 -> 14, of which waited for: 6 -> 4; matrix products, arithmetic and copies ran while one was open for 1% -> 0% of each run, Pallas kernels for 13% -> 13%
where the time goes in v4:
time: 148 us; the launch traced here: 147 us
  starting transfers between devices  57.1 us (39%)
  blocking collectives  41.3 us (28%)
  Pallas kernels  32.6 us (22%)
  waiting for transfers between devices  12.6 us (9%)
  local copies, waits for them, and re-layouts  2.7 us (2%)
    all_to_all x2, blocking collectives, spread(): lax.all_to_all(jnp.broadcast_to(row[None], (count, *row.shape)), axes, 0,...  41.3 us
    pallas_call x12, Pallas kernels, call(): pl.pallas_call(body, out_shape=shapes, in_specs=specs, out_specs=[pl.Bloc...  32.6 us
    ppermute x2, starting transfers between devices, swap_far(): lax.ppermute(planes, GX, [p for k in range(1, count - 1, 2) for p in ((k,...  27.2 us
    ppermute x4, starting transfers between devices, shift(): low = lax.ppermute(tail, axis, [(i, i + 1) for i in range(ends)])  16.7 us
    ppermute x4, waiting for transfers between devices, shift(): high = lax.ppermute(head, axis, [(i + 1, i) for i in range(ends)])  8.59 us
    ppermute x4, starting transfers between devices, swap_near(): lax.ppermute(planes, GX, [(k, k ^ 1) for k in range(lax.axis_size(GX))])  7.81 us
    ppermute x4, starting transfers between devices, shift(): high = lax.ppermute(head, axis, [(i + 1, i) for i in range(ends)])  5.29 us
  transfers between devices with their start and end apart: 14, of which 4 were waited for; matrix products, arithmetic and copies ran while one was open for 0% of the time, Pallas kernels for 13%

profile of v4, /device:TPU:2, one launch (start us, length us, event | category | flops | bytes accessed | tf_op | source)
XLA Modules:
  0.0 147.3 jit_solution(12220680321682169308)
XLA Ops:
  0.6 1.9 %collective-permute-start.2 = (f32[16,32,128]{2,1,0:T(8,128)}, f32[16,32,128]{2,1,0:T(8,128)S(1)}, u32[]{:S(2)}, u32[]{:S(2)}) collective-permute-start(f32[16,32,128]{2,1,0:T(8,128)} %refs_3_.2), channel_id=1, source_target_pairs={{0,32},{32,0},{64,96},{96,64},{128,160},{160,128},{192,224},{224,1... | collective-permute-start | bytes 786440 | tf_op jit(solution)/shard_map/ppermute | solution.py:499
  2.6 15.8 %collective-permute-start.6 = (f32[16,32,128]{2,1,0:T(8,128)}, f32[16,32,128]{2,1,0:T(8,128)S(1)}, u32[]{:S(2)}, u32[]{:S(2)}) collective-permute-start(f32[16,32,128]{2,1,0:T(8,128)} %refs_3_.2), channel_id=1, source_target_pairs={{32,64},{64,32},{96,128},{128,96},{160,192},{192,160},{224,256},{2... | collective-permute-start | bytes 786440 | tf_op jit(solution)/shard_map/ppermute | solution.py:495
  18.4 0.0 copy-start
  18.4 0.9 copy-done
  19.3 0.0 copy-start.2
  19.3 0.9 copy-done.2
  20.3 3.5 %collective-permute-start = (f32[16,32,128]{2,1,0:T(8,128)S(1)}, f32[16,32,128]{2,1,0:T(8,128)S(1)}, u32[]{:S(2)}, u32[]{:S(2)}) collective-permute-start(f32[16,32,128]{2,1,0:T(8,128)S(1)} %get-tuple-element.45), channel_id=1, source_target_pairs={{0,8},{8,16},{16,24},{1,9},{9,17},{17,25},{2,10},{10,18},{18,26},{... | collective-permute-start | bytes 786440 | tf_op jit(solution)/shard_map/ppermute | solution.py:504
  23.8 0.0 copy-start.1
  23.8 0.0 copy-start.3
  23.8 1.4 collective-permute-start.1
  25.3 0.0 copy-start.5
  25.3 0.7 copy-done.5
  26.0 1.0 shard_map.59
  26.9 0.0 collective-permute-done.2.refs_4_.refs_8_
  26.9 2.6 %collective-permute-done.refs_2_.refs_4_.refs_5_ = f32[16,32,128]{2,1,0:T(8,128)S(1)} collective-permute-done((f32[16,32,128]{2,1,0:T(8,128)S(1)}, f32[16,32,128]{2,1,0:T(8,128)S(1)}, u32[]{:S(2)}, u32[]{:S(2)}) %collective-permute-start) | collective-permute-done | bytes 262176 | tf_op jit(solution)/shard_map/ppermute | solution.py:504
  29.6 4.3 %collective-permute-done.1.refs_3_.refs_5_.refs_6_ = f32[16,32,128]{2,1,0:T(8,128)S(1)} collective-permute-done((f32[16,32,128]{2,1,0:T(8,128)S(1)}, f32[16,32,128]{2,1,0:T(8,128)S(1)}, u32[]{:S(2)}, u32[]{:S(2)}) %collective-permute-start.1) | collective-permute-done | bytes 262176 | tf_op jit(solution)/shard_map/ppermute | solution.py:505
  33.8 0.0 copy-done.1
  33.8 0.0 copy-done.3
  33.8 0.0 copy-start.6
  33.8 2.3 %shard_map.61 = (f32[16,24,128]{2,1,0:T(8,128)S(1)}, f32[16,24,128]{2,1,0:T(8,128)S(1)}, f32[16,48,128]{2,1,0:T(8,128)}) custom-call(f32[16,32,128]{2,1,0:T(8,128)S(1)} %copy-done.3, f32[16,32,128]{2,1,0:T(8,128)S(1)} %copy-done.1, f32[16,32,128]{2,1,0:T(8,128)S(1)} %collective-permute-done.refs_2_.refs_4_.refs_5_, ...), custom_call_target="tpu_custom_call" | custom-call | flops 1000 | bytes 1835008 | tf_op jit(solution)/shard_map/pallas_call | solution.py:56
  36.1 1.3 collective-permute-start.3
  37.4 4.6 %collective-permute-start.4 = (f32[16,24,128]{2,1,0:T(8,128)S(1)}, f32[16,24,128]{2,1,0:T(8,128)S(1)}, u32[]{:S(2)}, u32[]{:S(2)}) collective-permute-start(f32[16,24,128]{2,1,0:T(8,128)S(1)} %get-tuple-element.48.refs_2_), channel_id=1, source_target_pairs={{0,1},{1,2},{2,3},{3,4},{4,5},{5,6},{6,7},{8,9},{9,10},{10,11},{11... | collective-permute-start | bytes 589832 | tf_op jit(solution)/shard_map/ppermute | solution.py:504
  41.9 0.0 collective-permute-done.6.refs_0_.refs_9_
  42.0 3.5 %collective-permute-start.7 = (f32[16,24,128]{2,1,0:T(8,128)S(1)}, f32[16,24,128]{2,1,0:T(8,128)S(1)}, u32[]{:S(2)}, u32[]{:S(2)}) collective-permute-start(f32[16,24,128]{2,1,0:T(8,128)S(1)} %get-tuple-element.50), channel_id=1, source_target_pairs={{0,8},{8,16},{16,24},{1,9},{9,17},{17,25},{2,10},{10,18},{18,26},{... | collective-permute-start | bytes 589832 | tf_op jit(solution)/shard_map/ppermute | solution.py:504
  45.5 1.3 collective-permute-start.8
  46.8 1.9 %collective-permute-start.5 = (f32[16,48,128]{2,1,0:T(8,128)}, f32[16,48,128]{2,1,0:T(8,128)S(1)}, u32[]{:S(2)}, u32[]{:S(2)}) collective-permute-start(f32[16,48,128]{2,1,0:T(8,128)} %get-tuple-element.49), channel_id=1, source_target_pairs={{0,32},{32,0},{64,96},{96,64},{128,160},{160,128},{192,224},{224,1... | collective-permute-start | bytes 1179656 | tf_op jit(solution)/shard_map/ppermute | solution.py:499
  48.7 0.0 collective-permute-done.3.refs_3_.refs_6_.refs_7_
  48.7 0.0 collective-permute-done.4.refs_4_.refs_7_.refs_8_
  48.7 0.0 collective-permute-done.7.refs_1_.refs_10_
  48.7 4.3 %collective-permute-done.8.refs_2_.refs_11_ = f32[16,24,128]{2,1,0:T(8,128)S(1)} collective-permute-done((f32[16,24,128]{2,1,0:T(8,128)S(1)}, f32[16,24,128]{2,1,0:T(8,128)S(1)}, u32[]{:S(2)}, u32[]{:S(2)}) %collective-permute-start.8) | collective-permute-done | bytes 196640 | tf_op jit(solution)/shard_map/ppermute | solution.py:505
  53.0 1.6 %shard_map.63 = (f32[16,16,128]{2,1,0:T(8,128)}, f32[16,16,128]{2,1,0:T(8,128)}, f32[16,32,128]{2,1,0:T(8,128)}) custom-call(f32[16,32,128]{2,1,0:T(8,128)S(1)} %collective-permute-done.6.refs_0_.refs_9_, f32[16,24,128]{2,1,0:T(8,128)S(1)} %collective-permute-done.7.refs_1_.refs_10_, f32[16,24,128]{2,1,0:T(8,128)S(1)} %collective-permute-done.8.refs_2_.refs_11_, ...), custom_call_target="tpu_custom_call" | custom-call | flops 1000 | bytes 1572864 | tf_op jit(solution)/shard_map/pallas_call | solution.py:56
  54.7 1.9 %collective-permute-start.9 = (f32[16,32,128]{2,1,0:T(8,128)}, f32[16,32,128]{2,1,0:T(8,128)S(1)}, u32[]{:S(2)}, u32[]{:S(2)}) collective-permute-start(f32[16,32,128]{2,1,0:T(8,128)} %get-tuple-element.52), channel_id=1, source_target_pairs={{0,32},{32,0},{64,96},{96,64},{128,160},{160,128},{192,224},{224,1... | collective-permute-start | bytes 786440 | tf_op jit(solution)/shard_map/ppermute | solution.py:499
  56.6 1.3 collective-permute-start.10
  57.9 5.2 %collective-permute-start.11 = (f32[16,16,128]{2,1,0:T(8,128)}, f32[16,16,128]{2,1,0:T(8,128)}, u32[]{:S(2)}, u32[]{:S(2)}) collective-permute-start(f32[16,16,128]{2,1,0:T(8,128)} %get-tuple-element.57), channel_id=1, source_target_pairs={{0,1},{1,2},{2,3},{3,4},{4,5},{5,6},{6,7},{8,9},{9,10},{10,11},{11... | collective-permute-start | bytes 393224 | tf_op jit(solution)/shard_map/ppermute | solution.py:504
  63.1 0.1 stack.31.refs_0_
  63.2 0.0 collective-permute-done.5.refs_9_
  63.2 0.0 collective-permute-done.9.refs_10_
  63.2 0.0 copy-done.6
  63.2 6.8 %shard_map.64 = (f32[32,80,128]{2,1,0:T(8,128)S(1)}, f32[32,80,128]{2,1,0:T(8,128)S(1)}, f32[16,80,128]{2,1,0:T(8,128)S(1)}, f32[16,80,128]{2,1,0:T(8,128)S(1)},...) custom-call(s32[7]{0:T(128)S(1)} %stack.31.refs_0_, ...), custom_call_target="tpu_custom_call" | custom-call | flops 1000 | bytes 8388840 | tf_op jit(solution)/shard_map/pallas_call | solution.py:56
  70.0 0.0 collective-permute-done.10.refs_12_
  70.0 0.0 collective-permute-done.11.refs_13_
  70.0 7.6 %shard_map.65 = (f32[16,80,128]{2,1,0:T(8,128)S(1)}, f32[16,80,128]{2,1,0:T(8,128)S(1)}, f32[32,64,128]{2,1,0:T(8,128)S(1)}, f32[32,64,128]{2,1,0:T(8,128)S(1)},...) custom-call(s32[7]{0:T(128)S(1)} %stack.31.refs_0_, ...), custom_call_target="tpu_custom_call" | custom-call | flops 1000 | bytes 11686120 | tf_op jit(solution)/shard_map/pallas_call | solution.py:56
  77.7 0.0 copy-start.4
  77.7 2.9 %shard_map.67 = (f32[16,32,128]{2,1,0:T(8,128)}, f32[8,48,128]{2,1,0:T(8,128)S(1)}, f32[8,48,128]{2,1,0:T(8,128)S(1)}, f32[37,8,128]{2,1,0:T(8,128)S(1)}) custom-call(s32[7]{0:T(128)S(1)} %stack.31.refs_0_, f32[3,17]{1,0:T(4,128)S(1)} %copy-done.6, f32[256,256]{1,0:T(8,128)S(1)} %get-tuple-element.55.refs_3_.refs_2_, f32[16,32,128]{2,1,0:T(8,128)S(1)} %copy-done.1, ...), custom_call_target="tpu_custom_call" | custom-call | flops 1000 | bytes 5525736 | tf_op jit(solution)/shard_map/pallas_call | solution.py:56
  80.6 2.1 %collective-permute-start.13 = (f32[37,8,128]{2,1,0:T(8,128)S(1)}, f32[37,8,128]{2,1,0:T(8,128)S(1)}, u32[]{:S(2)}, u32[]{:S(2)}) collective-permute-start(f32[37,8,128]{2,1,0:T(8,128)S(1)} %get-tuple-element.74), channel_id=1, source_target_pairs={{0,32},{32,0},{64,96},{96,64},{128,160},{160,128},{192,224},{224,1... | collective-permute-start | bytes 454664 | tf_op jit(solution)/shard_map/ppermute | solution.py:499
  82.7 11.4 %collective-permute-start.12 = (f32[37,8,128]{2,1,0:T(8,128)S(1)}, f32[37,8,128]{2,1,0:T(8,128)S(1)}, u32[]{:S(2)}, u32[]{:S(2)}) collective-permute-start(f32[37,8,128]{2,1,0:T(8,128)S(1)} %get-tuple-element.66), channel_id=1, source_target_pairs={{32,64},{64,32},{96,128},{128,96},{160,192},{192,160},{224,256},{2... | collective-permute-start | bytes 454664 | tf_op jit(solution)/shard_map/ppermute | solution.py:495
  94.1 0.0 copy-done.4
  94.2 3.9 %shard_map.66 = (f32[32,48,128]{2,1,0:T(8,128)S(1)}, f32[32,48,128]{2,1,0:T(8,128)S(1)}) custom-call(s32[7]{0:T(128)S(1)} %stack.31.refs_0_, f32[256,256]{1,0:T(8,128)S(1)} %copy-done.4, f32[32,80,128]{2,1,0:T(8,128)S(1)} %get-tuple-element.53.refs_14_.refs_2_.refs_4_, f32[32,80,128]{2,1,0:T(8,128)S(1)} %get-tuple-element.54.refs_15_.refs_3_.refs_5_, ...), custom_call_target="tpu_custom_call" | custom-call | flops 10000000000 | bytes 5767196 | tf_op jit(solution)/shard_map/pallas_call | solution.py:56
  98.1 0.0 collective-permute-done.13.refs_6_
  98.1 3.0 %shard_map.68 = (f32[8,48,128]{2,1,0:T(8,128)S(1)}, f32[8,48,128]{2,1,0:T(8,128)S(1)}, f32[8,40,128]{2,1,0:T(8,128)S(1)}, f32[8,40,128]{2,1,0:T(8,128)S(1)}, f32...) custom-call(s32[7]{0:T(128)S(1)} %stack.31.refs_0_, f32[256,256]{1,0:T(8,128)S(1)} %copy-done.4, ...), custom_call_target="tpu_custom_call" | custom-call | flops 1000 | bytes 6246940 | tf_op jit(solution)/shard_map/pallas_call | solution.py:56
  101.1 1.4 collective-permute-done.12.refs_6_
  102.5 2.0 %shard_map.69 = (f32[8,32,128]{2,1,0:T(8,128)S(1)}, f32[1,128]{1,0:T(1,128)S(1)}) custom-call(s32[7]{0:T(128)S(1)} %stack.31.refs_0_, f32[256,256]{1,0:T(8,128)S(1)} %copy-done.4, f32[32,48,128]{2,1,0:T(8,128)S(1)} %get-tuple-element.64.refs_2_, f32[32,48,128]{2,1,0:T(8,128)S(1)} %get-tuple-element.65.refs_3_, f32[16,80,128]{2,1,0:T(8,128)S(1)} %get-tuple-element.62.refs_4_, ...), custom_call_target="tpu_custom_call" | custom-call | flops 1000 | bytes 4543516 | tf_op jit(solution)/shard_map/pallas_call | solution.py:56
  104.6 29.3 %all_to_all.10 = f32[32,1,128]{2,1,0:T(1,128)S(1)} all-to-all(f32[32,1,128]{2,1,0:T(1,128)S(1)} %broadcast_in_dim.7), channel_id=1, replica_groups=mesh['gx_0'=4,'gx_1'=2,'gx_2'=2,'gy'=4,'gz'=8] {'gx_1','gx_2','gz'}, dimensions={0} | all-to-all | bytes 32768 | tf_op jit(solution)/shard_map/all_to_all | solution.py:511
  133.9 12.0 %all_to_all.11.refs_1_ = f32[16,1,128]{2,1,0:T(1,128)S(1)} all-to-all(f32[16,1,128]{2,1,0:T(1,128)S(1)} %broadcast_in_dim.16), channel_id=1, replica_groups=mesh['gx_0'=4,'gx_1'=2,'gx_2'=2,'gy'=4,'gz'=8] {'gx_0','gy'}, dimensions={0} | all-to-all | bytes 16384 | tf_op jit(solution)/shard_map/all_to_all | solution.py:511
  145.9 1.4 shard_map.70
  (5 shorter events, 0.1 us)
Async XLA Ops:
  0.6 26.3 %collective-permute-start.2 = (f32[16,32,128]{2,1,0:T(8,128)}, f32[16,32,128]{2,1,0:T(8,128)S(1)}, u32[]{:S(2)}, u32[]{:S(2)}) collective-permute-start(f32[16,32,128]{2,1,0:T(8,128)} %refs_3_.2), channel_id=1, source_target_pairs={{0,32},{32,0},{64,96},{96,64},{128,160},{160,128},{192,224},{224,1... | collective-permute-start | bytes 786440 | tf_op jit(solution)/shard_map/ppermute | solution.py:499
  2.6 39.4 %collective-permute-start.6 = (f32[16,32,128]{2,1,0:T(8,128)}, f32[16,32,128]{2,1,0:T(8,128)S(1)}, u32[]{:S(2)}, u32[]{:S(2)}) collective-permute-start(f32[16,32,128]{2,1,0:T(8,128)} %refs_3_.2), channel_id=1, source_target_pairs={{32,64},{64,32},{96,128},{128,96},{160,192},{192,160},{224,256},{2... | collective-permute-start | bytes 786440 | tf_op jit(solution)/shard_map/ppermute | solution.py:495
  18.4 1.0 copy-start
  19.3 0.9 copy-start.2
  20.3 9.2 %collective-permute-start = (f32[16,32,128]{2,1,0:T(8,128)S(1)}, f32[16,32,128]{2,1,0:T(8,128)S(1)}, u32[]{:S(2)}, u32[]{:S(2)}) collective-permute-start(f32[16,32,128]{2,1,0:T(8,128)S(1)} %get-tuple-element.45), channel_id=1, source_target_pairs={{0,8},{8,16},{16,24},{1,9},{9,17},{17,25},{2,10},{10,18},{18,26},{... | collective-permute-start | bytes 786440 | tf_op jit(solution)/shard_map/ppermute | solution.py:504
  23.8 10.0 %copy-start.1 = (f32[16,32,128]{2,1,0:T(8,128)S(1)}, f32[16,32,128]{2,1,0:T(8,128)}, u32[]{:S(2)}) copy-start(f32[16,32,128]{2,1,0:T(8,128)} %refs_3_.3) | copy-start | bytes 786436
  23.8 10.0 %copy-start.3 = (f32[16,32,128]{2,1,0:T(8,128)S(1)}, f32[16,32,128]{2,1,0:T(8,128)}, u32[]{:S(2)}) copy-start(f32[16,32,128]{2,1,0:T(8,128)} %refs_3_.2) | copy-start | bytes 786436
  23.8 10.0 %collective-permute-start.1 = (f32[16,32,128]{2,1,0:T(8,128)S(1)}, f32[16,32,128]{2,1,0:T(8,128)S(1)}, u32[]{:S(2)}, u32[]{:S(2)}) collective-permute-start(f32[16,32,128]{2,1,0:T(8,128)S(1)} %get-tuple-element.46), channel_id=1, source_target_pairs={{8,0},{16,8},{24,16},{9,1},{17,9},{25,17},{10,2},{18,10},{26,18},{... | collective-permute-start | bytes 786440 | tf_op jit(solution)/shard_map/ppermute | solution.py:505
  25.3 0.7 copy-start.5
  33.8 29.4 %copy-start.6 = (f32[3,17]{1,0:T(4,128)S(1)}, f32[3,17]{1,0:T(4,128)}, u32[]{:S(2)}) copy-start(f32[3,17]{1,0:T(4,128)} %refs_1_.12) | copy-start | bytes 616
  36.1 12.6 %collective-permute-start.3 = (f32[16,24,128]{2,1,0:T(8,128)S(1)}, f32[16,24,128]{2,1,0:T(8,128)S(1)}, u32[]{:S(2)}, u32[]{:S(2)}) collective-permute-start(f32[16,24,128]{2,1,0:T(8,128)S(1)} %get-tuple-element.47.refs_1_), channel_id=1, source_target_pairs={{1,0},{2,1},{3,2},{4,3},{5,4},{6,5},{7,6},{9,8},{10,9},{11,10},{12... | collective-permute-start | bytes 589832 | tf_op jit(solution)/shard_map/ppermute | solution.py:505
  37.4 11.3 %collective-permute-start.4 = (f32[16,24,128]{2,1,0:T(8,128)S(1)}, f32[16,24,128]{2,1,0:T(8,128)S(1)}, u32[]{:S(2)}, u32[]{:S(2)}) collective-permute-start(f32[16,24,128]{2,1,0:T(8,128)S(1)} %get-tuple-element.48.refs_2_), channel_id=1, source_target_pairs={{0,1},{1,2},{2,3},{3,4},{4,5},{5,6},{6,7},{8,9},{9,10},{10,11},{11... | collective-permute-start | bytes 589832 | tf_op jit(solution)/shard_map/ppermute | solution.py:504
  42.0 6.7 %collective-permute-start.7 = (f32[16,24,128]{2,1,0:T(8,128)S(1)}, f32[16,24,128]{2,1,0:T(8,128)S(1)}, u32[]{:S(2)}, u32[]{:S(2)}) collective-permute-start(f32[16,24,128]{2,1,0:T(8,128)S(1)} %get-tuple-element.50), channel_id=1, source_target_pairs={{0,8},{8,16},{16,24},{1,9},{9,17},{17,25},{2,10},{10,18},{18,26},{... | collective-permute-start | bytes 589832 | tf_op jit(solution)/shard_map/ppermute | solution.py:504
  45.5 7.6 %collective-permute-start.8 = (f32[16,24,128]{2,1,0:T(8,128)S(1)}, f32[16,24,128]{2,1,0:T(8,128)S(1)}, u32[]{:S(2)}, u32[]{:S(2)}) collective-permute-start(f32[16,24,128]{2,1,0:T(8,128)S(1)} %get-tuple-element.51), channel_id=1, source_target_pairs={{8,0},{16,8},{24,16},{9,1},{17,9},{25,17},{10,2},{18,10},{26,18},{... | collective-permute-start | bytes 589832 | tf_op jit(solution)/shard_map/ppermute | solution.py:505
  46.8 16.4 %collective-permute-start.5 = (f32[16,48,128]{2,1,0:T(8,128)}, f32[16,48,128]{2,1,0:T(8,128)S(1)}, u32[]{:S(2)}, u32[]{:S(2)}) collective-permute-start(f32[16,48,128]{2,1,0:T(8,128)} %get-tuple-element.49), channel_id=1, source_target_pairs={{0,32},{32,0},{64,96},{96,64},{128,160},{160,128},{192,224},{224,1... | collective-permute-start | bytes 1179656 | tf_op jit(solution)/shard_map/ppermute | solution.py:499
  54.7 8.5 %collective-permute-start.9 = (f32[16,32,128]{2,1,0:T(8,128)}, f32[16,32,128]{2,1,0:T(8,128)S(1)}, u32[]{:S(2)}, u32[]{:S(2)}) collective-permute-start(f32[16,32,128]{2,1,0:T(8,128)} %get-tuple-element.52), channel_id=1, source_target_pairs={{0,32},{32,0},{64,96},{96,64},{128,160},{160,128},{192,224},{224,1... | collective-permute-start | bytes 786440 | tf_op jit(solution)/shard_map/ppermute | solution.py:499
  56.6 13.4 %collective-permute-start.10 = (f32[16,16,128]{2,1,0:T(8,128)}, f32[16,16,128]{2,1,0:T(8,128)}, u32[]{:S(2)}, u32[]{:S(2)}) collective-permute-start(f32[16,16,128]{2,1,0:T(8,128)} %get-tuple-element.56), channel_id=1, source_target_pairs={{1,0},{2,1},{3,2},{4,3},{5,4},{6,5},{7,6},{9,8},{10,9},{11,10},{12... | collective-permute-start | bytes 393224 | tf_op jit(solution)/shard_map/ppermute | solution.py:505
  57.9 12.1 %collective-permute-start.11 = (f32[16,16,128]{2,1,0:T(8,128)}, f32[16,16,128]{2,1,0:T(8,128)}, u32[]{:S(2)}, u32[]{:S(2)}) collective-permute-start(f32[16,16,128]{2,1,0:T(8,128)} %get-tuple-element.57), channel_id=1, source_target_pairs={{0,1},{1,2},{2,3},{3,4},{4,5},{5,6},{6,7},{8,9},{9,10},{10,11},{11... | collective-permute-start | bytes 393224 | tf_op jit(solution)/shard_map/ppermute | solution.py:504
  77.7 16.5 %copy-start.4 = (f32[256,256]{1,0:T(8,128)S(1)}, f32[256,256]{1,0:T(8,128)}, u32[]{:S(2)}) copy-start(f32[256,256]{1,0:T(8,128)} %constant.47.clone.refs_1_) | copy-start | bytes 786436
  80.6 17.5 %collective-permute-start.13 = (f32[37,8,128]{2,1,0:T(8,128)S(1)}, f32[37,8,128]{2,1,0:T(8,128)S(1)}, u32[]{:S(2)}, u32[]{:S(2)}) collective-permute-start(f32[37,8,128]{2,1,0:T(8,128)S(1)} %get-tuple-element.74), channel_id=1, source_target_pairs={{0,32},{32,0},{64,96},{96,64},{128,160},{160,128},{192,224},{224,1... | collective-permute-start | bytes 454664 | tf_op jit(solution)/shard_map/ppermute | solution.py:499
  82.7 19.8 %collective-permute-start.12 = (f32[37,8,128]{2,1,0:T(8,128)S(1)}, f32[37,8,128]{2,1,0:T(8,128)S(1)}, u32[]{:S(2)}, u32[]{:S(2)}) collective-permute-start(f32[37,8,128]{2,1,0:T(8,128)S(1)} %get-tuple-element.66), channel_id=1, source_target_pairs={{32,64},{64,32},{96,128},{128,96},{160,192},{192,160},{224,256},{2... | collective-permute-start | bytes 454664 | tf_op jit(solution)/shard_map/ppermute | solution.py:495

commit v5 on v4

--- a/solution.py
+++ b/solution.py
@@ -64,7 +64,8 @@
     )(*args, *after)
 
 
-def cut(wave, external, head, tail):
+def cut(wave, external, head, tail, same):
+    same[...] = wave[...]
     head[:, 0:24, :] = wave[:, 0:24, :]
     head[:, 24:32, :] = external[:, 0:8, :]
     tail[:, 0:24, :] = wave[:, 8:32, :]
@@ -187,20 +188,30 @@
 
 def sources(weights, field, at, g_own, g_rim, base, s_own, s_rim, to, c_own, c_rim, h_own, h_rim):
     x_taps = [weights[0, a] for a in range(17)]
-    y_taps = [weights[1, a] for a in range(17)]
     slide(g_own, base, h_own, x_taps, 10)
     slide(g_rim, base, h_rim, x_taps, 10)
-
-    def source(x, carry):
-        for h, e, s, c in ((h_own, field[0], s_own, c_own), (h_rim, field[1], s_rim, c_rim)):
-            coarse = along_rows(h, x, y_taps, 64)
-            wave = e[at + x, 8:72, :]
-            density = wave * wave
-            s[to + x] = -1.0 * density * coarse + 0.5 * density * coarse * coarse
-            c[x] = coarse
-        return carry
-
-    lax.fori_loop(0, 16, source, 0)
+    offset = lax.broadcasted_iota(jnp.int32, (64, 80), 1) - lax.broadcasted_iota(jnp.int32, (64, 80), 0)
+    rows = jnp.zeros((64, 80), F32)
+    for tap in range(17):
+        rows = jnp.where(offset == tap, weights[1, tap], rows)
+    top, rest = halves(rows)
+    stack = jnp.concatenate([top, rest], axis=0)
+    dot = functools.partial(jnp.dot, preferred_element_type=F32)
+
+    def source(k, carry):
+        for i in range(4):
+            x = 4 * k + i
+            for h, e, s, c in ((h_own, field[0], s_own, c_own), (h_rim, field[1], s_rim, c_rim)):
+                big, small = halves(h[x])
+                both = dot(stack, big)
+                coarse = both[:64] + (both[64:] + dot(top, small))
+                wave = e[at + x, 8:72, :]
+                density = wave * wave
+                s[to + x] = -1.0 * density * coarse + 0.5 * density * coarse * coarse
+                c[x] = coarse
+        return carry
+
+    lax.fori_loop(0, 4, source, 0)
 
 
 def band(weights, flip):
@@ -219,7 +230,8 @@
     return matrix
 
 
-def bands(weights, spread, gather):
+def bands(weights, spread, gather, token):
+    token[...] = jnp.zeros_like(token)
     spread[...] = band(weights, False)
     gather[...] = band(weights, True)
 
@@ -231,9 +243,9 @@
     spread_halves = halves(spread[...])
     upper = flags[0]
     mine, other = 16 * upper, 16 * (1 - upper)
-    fill(own, rim, mine, wave, low, high, right, left)
     i_low, i_high = i_rows.at[:, 0:24, :], i_rows.at[:, 24:48, :]
     i_right, i_left = i_sides.at[:, 0:16, :], i_sides.at[:, 16:32, :]
+    fill(own, rim, mine, wave, low, high, right, left)
     fill(own, rim, other, inner, i_low, i_high, i_right, i_left)
     along_z(own, rim, k_own, k_rim, 0, spread_halves)
     along_z(own, rim, k_own, k_rim, 16, spread_halves)
@@ -528,16 +540,16 @@
     ).astype(jnp.int32)
     block = wave.shape
     outer = swap_far(wave)
-    inner = swap_near(wave)
-    head, tail = call(cut, [block] * 2, [], wave, external)
+    head, tail, same = call(cut, [block] * 3, [], wave, external)
+    inner = swap_near(same)
     low, high = shift(head, tail, "gy")
-    smear_z, gather_z = call(bands, [(256, 256)] * 2, [], weights, scalars=1, flops=10**10)
+    smear_z, gather_z, token = call(bands, [(256, 256)] * 2 + [(8, LANES)], [], weights, scalars=1, flops=5 * 10**9)
     first, final, rows = call(
         pack_both,
         [(16, 24, LANES)] * 2 + [(16, 48, LANES)],
         [],
         wave, external, low, high,
-        after=(inner, smear_z),
+        after=(inner, token),
     )
     left, right = shift(first, final, "gz")
     i_rows = swap_near(rows)
@@ -568,18 +580,27 @@
         scalars=2,
     )
     v_outer = swap_far(outward)
-    corr, v_near_own, v_near_rim, inward = call(
-        near_side,
-        [block] + twice(8, 48) + [(37, 8, LANES)],
-        [(8, 32, LANES)] + twice(8, 64) + twice(8, 48),
-        flags, weights, gather_z, external, *halo, s_own, s_rim, c_own, c_rim, far_corr,
-        scalars=2,
-    )
-    v_inner = swap_near(inward)
     shifts = jnp.asarray(ring_shifts())
-    p_own, p_rim = call(
-        first_step, twice(32, 48), twice(48, 80), flags, shifts, own, rim, out_own, out_rim, scalars=1, flops=10**10
-    )
+
+    def beside(*args):
+        corr, v_near_own, v_near_rim, inward = call(
+            near_side,
+            [block] + twice(8, 48) + [(37, 8, LANES)],
+            [(8, 32, LANES)] + twice(8, 64) + twice(8, 48),
+            flags, weights, gather_z, external, *halo, s_own, s_rim, c_own, c_rim, far_corr,
+            scalars=2,
+        )
+        v_inner = swap_near(inward)
+        p_own, p_rim = call(
+            first_step, twice(32, 48), twice(48, 80), flags, shifts, own, rim, out_own, out_rim, scalars=1
+        )
+        return corr, v_near_own, v_near_rim, v_inner, p_own, p_rim
+
+    def nothing(*args):
+        shapes = [block, *twice(8, 48), (37, 8, LANES), *twice(32, 48)]
+        return tuple(jnp.zeros(shape, F32) for shape in shapes)
+
+    corr, v_near_own, v_near_rim, v_inner, p_own, p_rim = lax.cond(flags[0] >= 0, beside, nothing)
     scratch = twice(32, 48) * 2 + twice(24, 40)
     *kept, near_psi, squares = call(
         near_steps, twice(8, 48) + twice(8, 40) + [(8, 32, LANES), (1, LANES)], scratch,

time: 148 us -> 144 us (0.973)
  blocking collectives: 41.3 us -> 34.2 us
  Pallas kernels: 32.6 us -> 37.9 us
  waiting for transfers between devices: 12.6 us -> 9.63 us
  starting transfers between devices: 57.1 us -> 58.7 us
  local copies, waits for them, and re-layouts: 2.7 us -> 1.16 us
    all_to_all x2, blocking collectives: 41.3 us -> 34.2 us  [spread(): lax.all_to_all(jnp.broadcast_to(row[None], (count, *row.shape)), axes, 0,...]
    pallas_call x12, Pallas kernels: 32.6 us -> 37.9 us  [call(): pl.pallas_call(body, out_shape=shapes, in_specs=specs, out_specs=[pl.Bloc...]
    ppermute x4, starting transfers between devices: 7.81 us -> 11.4 us  [swap_near(): lax.ppermute(planes, GX, [(k, k ^ 1) for k in range(lax.axis_size(GX))])]
    ppermute x2, starting transfers between devices: 27.2 us -> 25.2 us  [swap_far(): lax.ppermute(planes, GX, [p for k in range(1, count - 1, 2) for p in ((k,...]
    unnamed x14 -> x34, local copies, waits for them, and re-layouts: 2.59 us -> 1.03 us
  transfers between devices with their start and end apart: 14 -> 14, of which waited for: 4 -> 4; matrix products, arithmetic and copies ran while one was open for 0% -> 0% of each run, Pallas kernels for 13% -> 18%
where the time goes in v5:
time: 144 us; the launch traced here: 143 us
  starting transfers between devices  58.7 us (41%)
  Pallas kernels  37.9 us (26%)
  blocking collectives  34.2 us (24%)
  waiting for transfers between devices  9.63 us (7%)
    pallas_call x12, Pallas kernels, call(): pl.pallas_call(body, out_shape=shapes, in_specs=specs, out_specs=[pl.Bloc...  37.9 us
    all_to_all x2, blocking collectives, spread(): lax.all_to_all(jnp.broadcast_to(row[None], (count, *row.shape)), axes, 0,...  34.2 us
    ppermute x2, starting transfers between devices, swap_far(): lax.ppermute(planes, GX, [p for k in range(1, count - 1, 2) for p in ((k,...  25.2 us
    ppermute x4, starting transfers between devices, shift(): low = lax.ppermute(tail, axis, [(i, i + 1) for i in range(ends)])  16.9 us
    ppermute x4, starting transfers between devices, swap_near(): lax.ppermute(planes, GX, [(k, k ^ 1) for k in range(lax.axis_size(GX))])  11.4 us
    ppermute x4, waiting for transfers between devices, shift(): high = lax.ppermute(head, axis, [(i + 1, i) for i in range(ends)])  8.27 us
    ppermute x4, starting transfers between devices, shift(): high = lax.ppermute(head, axis, [(i + 1, i) for i in range(ends)])  5.17 us
  transfers between devices with their start and end apart: 14, of which 4 were waited for; matrix products, arithmetic and copies ran while one was open for 0% of the time, Pallas kernels for 18%

profile of v5, /device:TPU:2, one launch (start us, length us, event | category | flops | bytes accessed | tf_op | source)
XLA Modules:
  0.0 142.9 jit_solution(3935228843481579414)
XLA Ops:
  0.6 15.1 %collective-permute-start.6 = (f32[16,32,128]{2,1,0:T(8,128)}, f32[16,32,128]{2,1,0:T(8,128)S(1)}, u32[]{:S(2)}, u32[]{:S(2)}) collective-permute-start(f32[16,32,128]{2,1,0:T(8,128)} %refs_3_.1), channel_id=1, source_target_pairs={{32,64},{64,32},{96,128},{128,96},{160,192},{192,160},{224,256},{2... | collective-permute-start | bytes 786440 | tf_op jit(solution)/shard_map/ppermute | solution.py:507
  15.8 0.0 copy-start
  15.8 0.9 copy-done
  16.7 1.0 shard_map.60
  17.7 3.5 %collective-permute-start.1 = (f32[16,32,128]{2,1,0:T(8,128)S(1)}, f32[16,32,128]{2,1,0:T(8,128)S(1)}, u32[]{:S(2)}, u32[]{:S(2)}) collective-permute-start(f32[16,32,128]{2,1,0:T(8,128)S(1)} %get-tuple-element.107), channel_id=1, source_target_pairs={{0,8},{8,16},{16,24},{1,9},{9,17},{17,25},{2,10},{10,18},{18,26},{... | collective-permute-start | bytes 786440 | tf_op jit(solution)/shard_map/ppermute | solution.py:516
  21.2 1.3 collective-permute-start.2
  22.5 0.0 copy-start.1
  22.6 0.0 copy-start.8
  22.6 2.5 %collective-permute-start.3 = (f32[16,32,128]{2,1,0:T(8,128)S(1)}, f32[16,32,128]{2,1,0:T(8,128)S(1)}, u32[]{:S(2)}, u32[]{:S(2)}) collective-permute-start(f32[16,32,128]{2,1,0:T(8,128)S(1)} %get-tuple-element.109), channel_id=1, source_target_pairs={{0,32},{32,0},{64,96},{96,64},{128,160},{160,128},{192,224},{224,1... | collective-permute-start | bytes 786440 | tf_op jit(solution)/shard_map/ppermute | solution.py:511
  25.0 1.6 %shard_map.59 = (f32[256,256]{1,0:T(8,128)S(1)}, f32[256,256]{1,0:T(8,128)}, f32[8,128]{1,0:T(8,128)S(1)}) custom-call(f32[3,17]{1,0:T(4,128)} %refs_1_.9), custom_call_target="tpu_custom_call" | custom-call | flops 5000000000 | bytes 528588 | tf_op jit(solution)/shard_map/pallas_call | solution.py:56
  26.6 1.0 collective-permute-done.1.refs_2_.refs_4_.refs_5_
  27.6 4.1 %collective-permute-done.2.refs_3_.refs_5_.refs_6_ = f32[16,32,128]{2,1,0:T(8,128)S(1)} collective-permute-done((f32[16,32,128]{2,1,0:T(8,128)S(1)}, f32[16,32,128]{2,1,0:T(8,128)S(1)}, u32[]{:S(2)}, u32[]{:S(2)}) %collective-permute-start.2) | collective-permute-done | bytes 262176 | tf_op jit(solution)/shard_map/ppermute | solution.py:517
  31.8 0.0 collective-permute-done.3.refs_4_.refs_8_
  31.8 0.0 copy-done.1
  31.8 0.0 copy-done.8
  31.8 0.0 copy-start.21
  31.8 1.6 %shard_map.61 = (f32[16,24,128]{2,1,0:T(8,128)S(1)}, f32[16,24,128]{2,1,0:T(8,128)S(1)}, f32[16,48,128]{2,1,0:T(8,128)S(1)}) custom-call(f32[16,32,128]{2,1,0:T(8,128)S(1)} %copy-done.1, f32[16,32,128]{2,1,0:T(8,128)S(1)} %copy-done.8, f32[16,32,128]{2,1,0:T(8,128)S(1)} %collective-permute-done.1.refs_2_.refs_4_.refs_5_, ...), custom_call_target="tpu_custom_call" | custom-call | flops 1000 | bytes 1835008 | tf_op jit(solution)/shard_map/pallas_call | solution.py:56
  33.4 1.3 collective-permute-start.4
  34.7 4.6 %collective-permute-start.5 = (f32[16,24,128]{2,1,0:T(8,128)S(1)}, f32[16,24,128]{2,1,0:T(8,128)S(1)}, u32[]{:S(2)}, u32[]{:S(2)}) collective-permute-start(f32[16,24,128]{2,1,0:T(8,128)S(1)} %get-tuple-element.112.refs_2_), channel_id=1, source_target_pairs={{0,1},{1,2},{2,3},{3,4},{4,5},{5,6},{6,7},{8,9},{9,10},{10,11},{11... | collective-permute-start | bytes 589832 | tf_op jit(solution)/shard_map/ppermute | solution.py:516
  39.3 0.0 collective-permute-done.6.refs_0_.refs_9_
  39.3 0.0 copy-done.6
  39.3 3.5 %collective-permute-start.7 = (f32[16,24,128]{2,1,0:T(8,128)S(1)}, f32[16,24,128]{2,1,0:T(8,128)S(1)}, u32[]{:S(2)}, u32[]{:S(2)}) collective-permute-start(f32[16,24,128]{2,1,0:T(8,128)S(1)} %get-tuple-element.114), channel_id=1, source_target_pairs={{0,8},{8,16},{16,24},{1,9},{9,17},{17,25},{2,10},{10,18},{18,26},{... | collective-permute-start | bytes 589832 | tf_op jit(solution)/shard_map/ppermute | solution.py:516
  42.8 1.3 collective-permute-start.8
  44.1 1.9 %collective-permute-start.11 = (f32[16,48,128]{2,1,0:T(8,128)S(1)}, f32[16,48,128]{2,1,0:T(8,128)S(1)}, u32[]{:S(2)}, u32[]{:S(2)}) collective-permute-start(f32[16,48,128]{2,1,0:T(8,128)S(1)} %get-tuple-element.118), channel_id=1, source_target_pairs={{0,32},{32,0},{64,96},{96,64},{128,160},{160,128},{192,224},{224,1... | collective-permute-start | bytes 1179656 | tf_op jit(solution)/shard_map/ppermute | solution.py:511
  46.0 0.0 collective-permute-done.4.refs_3_.refs_6_.refs_7_
  46.1 0.0 copy-start.10
  46.1 0.0 collective-permute-done.5.refs_4_.refs_7_.refs_8_
  46.1 0.0 copy-start.12
  46.1 0.3 collective-permute-done.7.refs_1_.refs_10_
  46.4 4.1 %collective-permute-done.8.refs_2_.refs_11_ = f32[16,24,128]{2,1,0:T(8,128)S(1)} collective-permute-done((f32[16,24,128]{2,1,0:T(8,128)S(1)}, f32[16,24,128]{2,1,0:T(8,128)S(1)}, u32[]{:S(2)}, u32[]{:S(2)}) %collective-permute-start.8) | collective-permute-done | bytes 196640 | tf_op jit(solution)/shard_map/ppermute | solution.py:517
  50.5 0.9 shard_map.63
  51.4 0.0 copy-done.10
  51.4 1.9 %collective-permute-start.12 = (f32[16,32,128]{2,1,0:T(8,128)S(1)}, f32[16,32,128]{2,1,0:T(8,128)S(1)}, u32[]{:S(2)}, u32[]{:S(2)}) collective-permute-start(f32[16,32,128]{2,1,0:T(8,128)S(1)} %get-tuple-element.119), channel_id=1, source_target_pairs={{0,32},{32,0},{64,96},{96,64},{128,160},{160,128},{192,224},{224,1... | collective-permute-start | bytes 786440 | tf_op jit(solution)/shard_map/ppermute | solution.py:511
  53.3 1.3 collective-permute-start.9
  54.6 5.4 %collective-permute-start.10 = (f32[16,16,128]{2,1,0:T(8,128)S(1)}, f32[16,16,128]{2,1,0:T(8,128)S(1)}, u32[]{:S(2)}, u32[]{:S(2)}) collective-permute-start(f32[16,16,128]{2,1,0:T(8,128)S(1)} %get-tuple-element.117), channel_id=1, source_target_pairs={{0,1},{1,2},{2,3},{3,4},{4,5},{5,6},{6,7},{8,9},{9,10},{10,11},{11... | collective-permute-start | bytes 393224 | tf_op jit(solution)/shard_map/ppermute | solution.py:516
  60.0 0.0 copy-done.12
  60.1 0.1 stack.31.refs_0_
  60.2 0.0 copy-start.13
  60.2 0.0 copy-start.20
  60.2 0.0 collective-permute-done.11.refs_9_
  60.2 0.0 collective-permute-done.12.refs_10_
  60.2 0.0 copy-done.21
  60.2 7.9 %shard_map.64 = (f32[32,80,128]{2,1,0:T(8,128)S(1)}, f32[32,80,128]{2,1,0:T(8,128)S(1)}, f32[16,80,128]{2,1,0:T(8,128)S(1)}, f32[16,80,128]{2,1,0:T(8,128)S(1)},...) custom-call(s32[7]{0:T(128)S(1)} %stack.31.refs_0_, ...), custom_call_target="tpu_custom_call" | custom-call | flops 1000 | bytes 8388840 | tf_op jit(solution)/shard_map/pallas_call | solution.py:56
  68.1 0.0 collective-permute-done.9.refs_12_
  68.1 0.0 collective-permute-done.10.refs_13_
  68.1 0.0 copy-done.7
  68.1 0.0 copy-done.9
  68.1 0.0 copy-done.11
  68.2 8.5 %shard_map.65 = (f32[16,80,128]{2,1,0:T(8,128)}, f32[16,80,128]{2,1,0:T(8,128)}, f32[32,64,128]{2,1,0:T(8,128)}, f32[32,64,128]{2,1,0:T(8,128)}, f32[8,32,128]{2...) custom-call(s32[7]{0:T(128)S(1)} %stack.31.refs_0_, ...), custom_call_target="tpu_custom_call" | custom-call | flops 1000 | bytes 11686120 | tf_op jit(solution)/shard_map/pallas_call | solution.py:56
  76.6 0.0 copy-done.4
  76.6 10.1 %collective-permute-start.13 = (f32[37,8,128]{2,1,0:T(8,128)S(1)}, f32[37,8,128]{2,1,0:T(8,128)S(1)}, u32[]{:S(2)}, u32[]{:S(2)}) collective-permute-start(f32[37,8,128]{2,1,0:T(8,128)S(1)} %get-tuple-element.135), channel_id=1, source_target_pairs={{32,64},{64,32},{96,128},{128,96},{160,192},{192,160},{224,256},{2... | collective-permute-start | bytes 454664 | tf_op jit(solution)/shard_map/ppermute | solution.py:507
  86.7 14.0 %conditional.1 = (f32[16,32,128]{2,1,0:T(8,128)}, f32[8,48,128]{2,1,0:T(8,128)}, f32[8,48,128]{2,1,0:T(8,128)}, f32[37,8,128]{2,1,0:T(8,128)}, f32[32,48,128]{2,1,0:T(8,128)S(1)}, /*index=5*/f32[32,48,128]{2,1,0:T(8,128)S(1)}) conditional(s32[]{:T(128)} %convert_element_type.3, () %tuple.16, (s32[7]{0:T(128)S(1)}, f32[3,17]{1,0:T(4,128)S(1)}, ...), branch_computations={%region_0.1_spmd, %region_1.2_spmd} | conditional | flops 2000 | bytes 28676584 | solution.py:603
  86.8 0.0 copy-start.19
  86.8 4.8 %branch_1_fun.2 = (f32[16,32,128]{2,1,0:T(8,128)}, f32[8,48,128]{2,1,0:T(8,128)}, f32[8,48,128]{2,1,0:T(8,128)}, f32[37,8,128]{2,1,0:T(8,128)S(1)}) custom-call(s32[7]{0:T(128)S(1)} %get-tuple-element.36.refs_0_, f32[3,17]{1,0:T(4,128)S(1)} %get-tuple-element.37.refs_1_, f32[256,256]{1,0:T(8,128)} %get-tuple-element.38.refs_2_, ...), custom_call_target="tpu_custom_call" | custom-call | flops 1000 | bytes 5525736 | tf_op jit(solution)/shard_map/cond/branch_1_fun/pallas_call | solution.py:56
  91.7 5.1 %collective-permute-start = (f32[37,8,128]{2,1,0:T(8,128)S(1)}, f32[37,8,128]{2,1,0:T(8,128)}, u32[]{:S(2)}, u32[]{:S(2)}) collective-permute-start(f32[37,8,128]{2,1,0:T(8,128)S(1)} %get-tuple-element.52), channel_id=1, source_target_pairs={{0,32},{32,0},{64,96},{96,64},{128,160},{160,128},{192,224},{224,1... | collective-permute-start | bytes 454664 | tf_op jit(solution)/shard_map/cond/branch_1_fun/ppermute | solution.py:511
  96.8 3.9 %branch_1_fun.3 = (f32[32,48,128]{2,1,0:T(8,128)S(1)}, f32[32,48,128]{2,1,0:T(8,128)S(1)}) custom-call(s32[7]{0:T(128)S(1)} %get-tuple-element.36.refs_0_, f32[256,256]{1,0:T(8,128)S(1)} %copy-done.19, f32[32,80,128]{2,1,0:T(8,128)S(1)} %copy-done.3, f32[32,80,128]{2,1,0:T(8,128)S(1)} %copy-done.5, f32[16,80,128]{2,1,0:T(8,128)S(1)} %copy-done.15, ...), custom_call_target="tpu_custom_call" | custom-call | flops 1000 | bytes 5767196 | tf_op jit(solution)/shard_map/cond/branch_1_fun/pallas_call | solution.py:56
  100.7 0.0 collective-permute-done
  100.8 0.0 copy-start.18
  100.8 4.4 %shard_map.66 = (f32[8,48,128]{2,1,0:T(8,128)S(1)}, f32[8,48,128]{2,1,0:T(8,128)S(1)}, f32[8,40,128]{2,1,0:T(8,128)S(1)}, f32[8,40,128]{2,1,0:T(8,128)S(1)}, f32...) custom-call(s32[7]{0:T(128)S(1)} %stack.31.refs_0_, f32[256,256]{1,0:T(8,128)} %constant.52.clone.refs_1_, ...), custom_call_target="tpu_custom_call" | custom-call | flops 1000 | bytes 6246940 | tf_op jit(solution)/shard_map/pallas_call | solution.py:56
  105.2 0.0 collective-permute-done.13.refs_6_
  105.3 2.0 %shard_map.67 = (f32[8,32,128]{2,1,0:T(8,128)S(1)}, f32[1,128]{1,0:T(1,128)S(1)}) custom-call(s32[7]{0:T(128)S(1)} %stack.31.refs_0_, f32[256,256]{1,0:T(8,128)S(1)} %copy-done.18, f32[32,48,128]{2,1,0:T(8,128)S(1)} %get-tuple-element.133.refs_2_, f32[32,48,128]{2,1,0:T(8,128)S(1)} %get-tuple-element.134.refs_3_, f32[16,80,128]{2,1,0:T(8,128)S(1)} %copy-done.14, ...), custom_call_target="tpu_custom_call" | custom-call | flops 1000 | bytes 4543516 | tf_op jit(solution)/shard_map/pallas_call | solution.py:56
  107.3 22.9 %all_to_all.10 = f32[32,1,128]{2,1,0:T(1,128)S(1)} all-to-all(f32[32,1,128]{2,1,0:T(1,128)S(1)} %broadcast_in_dim.7), channel_id=1, replica_groups=mesh['gx_0'=4,'gx_1'=2,'gx_2'=2,'gy'=4,'gz'=8] {'gx_1','gx_2','gz'}, dimensions={0} | all-to-all | bytes 32768 | tf_op jit(solution)/shard_map/all_to_all | solution.py:523
  130.2 11.4 %all_to_all.11.refs_1_ = f32[16,1,128]{2,1,0:T(1,128)S(1)} all-to-all(f32[16,1,128]{2,1,0:T(1,128)S(1)} %broadcast_in_dim.16), channel_id=1, replica_groups=mesh['gx_0'=4,'gx_1'=2,'gx_2'=2,'gy'=4,'gz'=8] {'gx_0','gy'}, dimensions={0} | all-to-all | bytes 16384 | tf_op jit(solution)/shard_map/all_to_all | solution.py:523
  141.5 1.4 shard_map.68
  (27 shorter events, 0.1 us)
Async XLA Ops:
  0.6 38.6 %collective-permute-start.6 = (f32[16,32,128]{2,1,0:T(8,128)}, f32[16,32,128]{2,1,0:T(8,128)S(1)}, u32[]{:S(2)}, u32[]{:S(2)}) collective-permute-start(f32[16,32,128]{2,1,0:T(8,128)} %refs_3_.1), channel_id=1, source_target_pairs={{32,64},{64,32},{96,128},{128,96},{160,192},{192,160},{224,256},{2... | collective-permute-start | bytes 786440 | tf_op jit(solution)/shard_map/ppermute | solution.py:507
  15.8 1.0 copy-start
  17.7 9.9 %collective-permute-start.1 = (f32[16,32,128]{2,1,0:T(8,128)S(1)}, f32[16,32,128]{2,1,0:T(8,128)S(1)}, u32[]{:S(2)}, u32[]{:S(2)}) collective-permute-start(f32[16,32,128]{2,1,0:T(8,128)S(1)} %get-tuple-element.107), channel_id=1, source_target_pairs={{0,8},{8,16},{16,24},{1,9},{9,17},{17,25},{2,10},{10,18},{18,26},{... | collective-permute-start | bytes 786440 | tf_op jit(solution)/shard_map/ppermute | solution.py:516
  21.2 10.5 %collective-permute-start.2 = (f32[16,32,128]{2,1,0:T(8,128)S(1)}, f32[16,32,128]{2,1,0:T(8,128)S(1)}, u32[]{:S(2)}, u32[]{:S(2)}) collective-permute-start(f32[16,32,128]{2,1,0:T(8,128)S(1)} %get-tuple-element.108), channel_id=1, source_target_pairs={{8,0},{16,8},{24,16},{9,1},{17,9},{25,17},{10,2},{18,10},{26,18},{... | collective-permute-start | bytes 786440 | tf_op jit(solution)/shard_map/ppermute | solution.py:517
  22.5 9.3 %copy-start.1 = (f32[16,32,128]{2,1,0:T(8,128)S(1)}, f32[16,32,128]{2,1,0:T(8,128)}, u32[]{:S(2)}) copy-start(f32[16,32,128]{2,1,0:T(8,128)} %refs_3_.1) | copy-start | bytes 786436
  22.6 9.2 %copy-start.8 = (f32[16,32,128]{2,1,0:T(8,128)S(1)}, f32[16,32,128]{2,1,0:T(8,128)}, u32[]{:S(2)}) copy-start(f32[16,32,128]{2,1,0:T(8,128)} %refs_4_.1) | copy-start | bytes 786436
  22.6 9.2 %collective-permute-start.3 = (f32[16,32,128]{2,1,0:T(8,128)S(1)}, f32[16,32,128]{2,1,0:T(8,128)S(1)}, u32[]{:S(2)}, u32[]{:S(2)}) collective-permute-start(f32[16,32,128]{2,1,0:T(8,128)S(1)} %get-tuple-element.109), channel_id=1, source_target_pairs={{0,32},{32,0},{64,96},{96,64},{128,160},{160,128},{192,224},{224,1... | collective-permute-start | bytes 786440 | tf_op jit(solution)/shard_map/ppermute | solution.py:511
  31.8 7.5 %copy-start.6 = (f32[16,32,128]{2,1,0:T(8,128)}, f32[16,32,128]{2,1,0:T(8,128)S(1)}, u32[]{:S(2)}) copy-start(f32[16,32,128]{2,1,0:T(8,128)S(1)} %collective-permute-done.2.refs_3_.refs_5_.refs_6_) | copy-start | bytes 786436
  31.8 28.4 %copy-start.21 = (f32[3,17]{1,0:T(4,128)S(1)}, f32[3,17]{1,0:T(4,128)}, u32[]{:S(2)}) copy-start(f32[3,17]{1,0:T(4,128)} %refs_1_.9) | copy-start | bytes 616
  33.4 12.6 %collective-permute-start.4 = (f32[16,24,128]{2,1,0:T(8,128)S(1)}, f32[16,24,128]{2,1,0:T(8,128)S(1)}, u32[]{:S(2)}, u32[]{:S(2)}) collective-permute-start(f32[16,24,128]{2,1,0:T(8,128)S(1)} %get-tuple-element.111.refs_1_), channel_id=1, source_target_pairs={{1,0},{2,1},{3,2},{4,3},{5,4},{6,5},{7,6},{9,8},{10,9},{11,10},{12... | collective-permute-start | bytes 589832 | tf_op jit(solution)/shard_map/ppermute | solution.py:517
  34.7 11.4 %collective-permute-start.5 = (f32[16,24,128]{2,1,0:T(8,128)S(1)}, f32[16,24,128]{2,1,0:T(8,128)S(1)}, u32[]{:S(2)}, u32[]{:S(2)}) collective-permute-start(f32[16,24,128]{2,1,0:T(8,128)S(1)} %get-tuple-element.112.refs_2_), channel_id=1, source_target_pairs={{0,1},{1,2},{2,3},{3,4},{4,5},{5,6},{6,7},{8,9},{9,10},{10,11},{11... | collective-permute-start | bytes 589832 | tf_op jit(solution)/shard_map/ppermute | solution.py:516
  39.3 7.1 %collective-permute-start.7 = (f32[16,24,128]{2,1,0:T(8,128)S(1)}, f32[16,24,128]{2,1,0:T(8,128)S(1)}, u32[]{:S(2)}, u32[]{:S(2)}) collective-permute-start(f32[16,24,128]{2,1,0:T(8,128)S(1)} %get-tuple-element.114), channel_id=1, source_target_pairs={{0,8},{8,16},{16,24},{1,9},{9,17},{17,25},{2,10},{10,18},{18,26},{... | collective-permute-start | bytes 589832 | tf_op jit(solution)/shard_map/ppermute | solution.py:516
  42.8 7.7 %collective-permute-start.8 = (f32[16,24,128]{2,1,0:T(8,128)S(1)}, f32[16,24,128]{2,1,0:T(8,128)S(1)}, u32[]{:S(2)}, u32[]{:S(2)}) collective-permute-start(f32[16,24,128]{2,1,0:T(8,128)S(1)} %get-tuple-element.115), channel_id=1, source_target_pairs={{8,0},{16,8},{24,16},{9,1},{17,9},{25,17},{10,2},{18,10},{26,18},{... | collective-permute-start | bytes 589832 | tf_op jit(solution)/shard_map/ppermute | solution.py:517
  44.1 16.1 %collective-permute-start.11 = (f32[16,48,128]{2,1,0:T(8,128)S(1)}, f32[16,48,128]{2,1,0:T(8,128)S(1)}, u32[]{:S(2)}, u32[]{:S(2)}) collective-permute-start(f32[16,48,128]{2,1,0:T(8,128)S(1)} %get-tuple-element.118), channel_id=1, source_target_pairs={{0,32},{32,0},{64,96},{96,64},{128,160},{160,128},{192,224},{224,1... | collective-permute-start | bytes 1179656 | tf_op jit(solution)/shard_map/ppermute | solution.py:511
  46.1 5.4 %copy-start.10 = (f32[16,24,128]{2,1,0:T(8,128)}, f32[16,24,128]{2,1,0:T(8,128)S(1)}, u32[]{:S(2)}) copy-start(f32[16,24,128]{2,1,0:T(8,128)S(1)} %collective-permute-done.4.refs_3_.refs_6_.refs_7_) | copy-start | bytes 589828
  46.1 14.0 %copy-start.12 = (f32[16,24,128]{2,1,0:T(8,128)}, f32[16,24,128]{2,1,0:T(8,128)S(1)}, u32[]{:S(2)}) copy-start(f32[16,24,128]{2,1,0:T(8,128)S(1)} %collective-permute-done.5.refs_4_.refs_7_.refs_8_) | copy-start | bytes 589828
  51.4 8.8 %collective-permute-start.12 = (f32[16,32,128]{2,1,0:T(8,128)S(1)}, f32[16,32,128]{2,1,0:T(8,128)S(1)}, u32[]{:S(2)}, u32[]{:S(2)}) collective-permute-start(f32[16,32,128]{2,1,0:T(8,128)S(1)} %get-tuple-element.119), channel_id=1, source_target_pairs={{0,32},{32,0},{64,96},{96,64},{128,160},{160,128},{192,224},{224,1... | collective-permute-start | bytes 786440 | tf_op jit(solution)/shard_map/ppermute | solution.py:511
  53.3 14.8 %collective-permute-start.9 = (f32[16,16,128]{2,1,0:T(8,128)S(1)}, f32[16,16,128]{2,1,0:T(8,128)S(1)}, u32[]{:S(2)}, u32[]{:S(2)}) collective-permute-start(f32[16,16,128]{2,1,0:T(8,128)S(1)} %get-tuple-element.116), channel_id=1, source_target_pairs={{1,0},{2,1},{3,2},{4,3},{5,4},{6,5},{7,6},{9,8},{10,9},{11,10},{12... | collective-permute-start | bytes 393224 | tf_op jit(solution)/shard_map/ppermute | solution.py:517
  54.6 13.5 %collective-permute-start.10 = (f32[16,16,128]{2,1,0:T(8,128)S(1)}, f32[16,16,128]{2,1,0:T(8,128)S(1)}, u32[]{:S(2)}, u32[]{:S(2)}) collective-permute-start(f32[16,16,128]{2,1,0:T(8,128)S(1)} %get-tuple-element.117), channel_id=1, source_target_pairs={{0,1},{1,2},{2,3},{3,4},{4,5},{5,6},{6,7},{8,9},{9,10},{10,11},{11... | collective-permute-start | bytes 393224 | tf_op jit(solution)/shard_map/ppermute | solution.py:516
  60.2 8.0 %copy-start.7 = (f32[16,32,128]{2,1,0:T(8,128)S(1)}, f32[16,32,128]{2,1,0:T(8,128)}, u32[]{:S(2)}) copy-start(f32[16,32,128]{2,1,0:T(8,128)} %copy-done.6) | copy-start | bytes 786436
  60.2 8.0 %copy-start.9 = (f32[16,32,128]{2,1,0:T(8,128)S(1)}, f32[16,32,128]{2,1,0:T(8,128)}, u32[]{:S(2)}) copy-start(f32[16,32,128]{2,1,0:T(8,128)} %refs_4_.1) | copy-start | bytes 786436
  60.2 8.0 %copy-start.11 = (f32[16,24,128]{2,1,0:T(8,128)S(1)}, f32[16,24,128]{2,1,0:T(8,128)}, u32[]{:S(2)}) copy-start(f32[16,24,128]{2,1,0:T(8,128)} %copy-done.10) | copy-start | bytes 589828
  60.2 8.0 %copy-start.13 = (f32[16,24,128]{2,1,0:T(8,128)S(1)}, f32[16,24,128]{2,1,0:T(8,128)}, u32[]{:S(2)}) copy-start(f32[16,24,128]{2,1,0:T(8,128)} %copy-done.12) | copy-start | bytes 589828
  60.2 8.0 %copy-start.20 = (f32[256,256]{1,0:T(8,128)S(1)}, f32[256,256]{1,0:T(8,128)}, u32[]{:S(2)}) copy-start(f32[256,256]{1,0:T(8,128)} %get-tuple-element.106.refs_3_) | copy-start | bytes 786436
  68.1 8.5 %copy-start.2 = (f32[32,80,128]{2,1,0:T(8,128)}, f32[32,80,128]{2,1,0:T(8,128)S(1)}, u32[]{:S(2)}) copy-start(f32[32,80,128]{2,1,0:T(8,128)S(1)} %get-tuple-element.120.refs_14_.refs_4_) | copy-start | bytes 3932164
  68.1 8.5 %copy-start.4 = (f32[32,80,128]{2,1,0:T(8,128)}, f32[32,80,128]{2,1,0:T(8,128)S(1)}, u32[]{:S(2)}) copy-start(f32[32,80,128]{2,1,0:T(8,128)S(1)} %get-tuple-element.121.refs_15_.refs_5_) | copy-start | bytes 3932164
  76.6 28.6 %collective-permute-start.13 = (f32[37,8,128]{2,1,0:T(8,128)S(1)}, f32[37,8,128]{2,1,0:T(8,128)S(1)}, u32[]{:S(2)}, u32[]{:S(2)}) collective-permute-start(f32[37,8,128]{2,1,0:T(8,128)S(1)} %get-tuple-element.135), channel_id=1, source_target_pairs={{32,64},{64,32},{96,128},{128,96},{160,192},{192,160},{224,256},{2... | collective-permute-start | bytes 454664 | tf_op jit(solution)/shard_map/ppermute | solution.py:507
  86.8 10.0 %copy-start.3 = (f32[32,80,128]{2,1,0:T(8,128)S(1)}, f32[32,80,128]{2,1,0:T(8,128)}, u32[]{:S(2)}) copy-start(f32[32,80,128]{2,1,0:T(8,128)} %get-tuple-element.54.refs_2_) | copy-start | bytes 3932164 | tf_op jit(solution)/shard_map/cond
  86.8 10.0 %copy-start.5 = (f32[32,80,128]{2,1,0:T(8,128)S(1)}, f32[32,80,128]{2,1,0:T(8,128)}, u32[]{:S(2)}) copy-start(f32[32,80,128]{2,1,0:T(8,128)} %get-tuple-element.55.refs_3_) | copy-start | bytes 3932164 | tf_op jit(solution)/shard_map/cond
  86.8 10.0 %copy-start.15 = (f32[16,80,128]{2,1,0:T(8,128)S(1)}, f32[16,80,128]{2,1,0:T(8,128)}, u32[]{:S(2)}) copy-start(f32[16,80,128]{2,1,0:T(8,128)} %get-tuple-element.56.refs_4_) | copy-start | bytes 1966084 | tf_op jit(solution)/shard_map/cond
  86.8 10.0 %copy-start.17 = (f32[16,80,128]{2,1,0:T(8,128)S(1)}, f32[16,80,128]{2,1,0:T(8,128)}, u32[]{:S(2)}) copy-start(f32[16,80,128]{2,1,0:T(8,128)} %get-tuple-element.57.refs_5_) | copy-start | bytes 1966084 | tf_op jit(solution)/shard_map/cond
  86.8 10.0 %copy-start.19 = (f32[256,256]{1,0:T(8,128)S(1)}, f32[256,256]{1,0:T(8,128)}, u32[]{:S(2)}) copy-start(f32[256,256]{1,0:T(8,128)} %get-tuple-element.53.refs_1_) | copy-start | bytes 786436 | tf_op jit(solution)/shard_map/cond
  91.7 9.1 %collective-permute-start = (f32[37,8,128]{2,1,0:T(8,128)S(1)}, f32[37,8,128]{2,1,0:T(8,128)}, u32[]{:S(2)}, u32[]{:S(2)}) collective-permute-start(f32[37,8,128]{2,1,0:T(8,128)S(1)} %get-tuple-element.52), channel_id=1, source_target_pairs={{0,32},{32,0},{64,96},{96,64},{128,160},{160,128},{192,224},{224,1... | collective-permute-start | bytes 454664 | tf_op jit(solution)/shard_map/cond/branch_1_fun/ppermute | solution.py:511
  100.7 4.5 %copy-start.14 = (f32[16,80,128]{2,1,0:T(8,128)S(1)}, f32[16,80,128]{2,1,0:T(8,128)}, u32[]{:S(2)}) copy-start(f32[16,80,128]{2,1,0:T(8,128)} %get-tuple-element.131.refs_4_) | copy-start | bytes 1966084
  100.8 4.5 %copy-start.16 = (f32[16,80,128]{2,1,0:T(8,128)S(1)}, f32[16,80,128]{2,1,0:T(8,128)}, u32[]{:S(2)}) copy-start(f32[16,80,128]{2,1,0:T(8,128)} %get-tuple-element.132.refs_5_) | copy-start | bytes 1966084
  100.8 4.5 %copy-start.18 = (f32[256,256]{1,0:T(8,128)S(1)}, f32[256,256]{1,0:T(8,128)}, u32[]{:S(2)}) copy-start(f32[256,256]{1,0:T(8,128)} %constant.52.clone.refs_1_) | copy-start | bytes 786436

commit v6 on v5

--- a/solution.py
+++ b/solution.py
@@ -104,18 +104,18 @@
     rows[:, 0:24, :] = low[:, 0:24, :]
     rows[:, 24:48, :] = high[:, 0:24, :]
 
-    def plane(x, carry):
-        rows_of = stacked(x, (low, 24, 32), (external, 0, 32), (high, 24, 32))
-        first[x, 16:24, :], last[x, 16:24, :] = pack(rows_of, 6, 8, 0)
-        return carry
-
-    lax.fori_loop(0, 16, plane, 0, unroll=2)
+    for j in range(8):
+        rows_of = [stacked(2 * j + i, (low, 24, 32), (external, 0, 32), (high, 24, 32)) for i in range(2)]
+        one, two = pack(rows_of[0], 6, 8, 0), pack(rows_of[1], 6, 8, 48)
+        here = 16 + j // 2, slice(8 * (j % 2), 8 * (j % 2) + 8)
+        first[here] = one[0] + two[0]
+        last[here] = one[1] + two[1]
 
 
 def pack_outer(wave, low, high, right, left, first, last, sides):
     pack_cells(wave, low, high, first, last)
-    sides[:, 0:16, :] = right[:, 0:16, :]
-    sides[:, 16:32, :] = left[:, 0:16, :]
+    sides[:, 0:16, :] = right[0:16]
+    sides[:, 16:32, :] = left[0:16]
 
 
 def fill(own, rim, base, mid, low, high, right, left):
@@ -281,8 +281,9 @@
     v_own[:, 8:40, :] += external[planes]
     v_own[:, 40:48, :] += high[planes, 24:32, :]
     for x in range(8):
+        here = 16 + 2 * side + x // 4, slice(8 * (x // 2 % 2), 8 * (x // 2 % 2) + 8)
         for q in range(6):
-            v_rim[x, 8 * q : 8 * q + 8, :] += unpack(right[base + x, 16:24, :], left[base + x, 16:24, :], 8 * q, 8)
+            v_rim[x, 8 * q : 8 * q + 8, :] += unpack(right[here], left[here], 48 * (x % 2) + 8 * q, 8)
 
     lanes = lane_ids((8, LANES))
     edge, beyond = 4 * side, 4 - 4 * side
@@ -546,7 +547,7 @@
     smear_z, gather_z, token = call(bands, [(256, 256)] * 2 + [(8, LANES)], [], weights, scalars=1, flops=5 * 10**9)
     first, final, rows = call(
         pack_both,
-        [(16, 24, LANES)] * 2 + [(16, 48, LANES)],
+        [(20, 16, LANES)] * 2 + [(16, 48, LANES)],
         [],
         wave, external, low, high,
         after=(inner, token),

time: 144 us -> 149 us (1.035)
  blocking collectives: 34.2 us -> 37 us
  waiting for transfers between devices: 9.63 us -> 12 us
    ppermute x2, waiting for transfers between devices: 0.01 us -> 5.35 us  [swap_far(): lax.ppermute(planes, GX, [p for k in range(1, count - 1, 2) for p in ((k,...]
    ppermute x4, waiting for transfers between devices: 8.27 us -> 4.5 us  [shift(): high = lax.ppermute(head, axis, [(i + 1, i) for i in range(ends)])]
    all_to_all x2, blocking collectives: 34.2 us -> 37 us  [spread(): lax.all_to_all(jnp.broadcast_to(row[None], (count, *row.shape)), axes, 0,...]
  transfers between devices with their start and end apart: 14 -> 14, of which waited for: 4 -> 5; matrix products, arithmetic and copies ran while one was open for 0% -> 0% of each run, Pallas kernels for 18% -> 17%
where the time goes in v6:
time: 149 us; the launch traced here: 148 us
  starting transfers between devices  59.2 us (40%)
  Pallas kernels  37.4 us (25%)
  blocking collectives  37 us (25%)
  waiting for transfers between devices  12 us (8%)
    pallas_call x12, Pallas kernels, call(): pl.pallas_call(body, out_shape=shapes, in_specs=specs, out_specs=[pl.Bloc...  37.4 us
    all_to_all x2, blocking collectives, spread(): lax.all_to_all(jnp.broadcast_to(row[None], (count, *row.shape)), axes, 0,...  37 us
    ppermute x2, starting transfers between devices, swap_far(): lax.ppermute(planes, GX, [p for k in range(1, count - 1, 2) for p in ((k,...  26.1 us
    ppermute x4, starting transfers between devices, shift(): low = lax.ppermute(tail, axis, [(i, i + 1) for i in range(ends)])  16.9 us
    ppermute x4, starting transfers between devices, swap_near(): lax.ppermute(planes, GX, [(k, k ^ 1) for k in range(lax.axis_size(GX))])  11 us
    ppermute x2, waiting for transfers between devices, swap_far(): lax.ppermute(planes, GX, [p for k in range(1, count - 1, 2) for p in ((k,...  5.35 us
    ppermute x4, starting transfers between devices, shift(): high = lax.ppermute(head, axis, [(i + 1, i) for i in range(ends)])  5.17 us
    ppermute x4, waiting for transfers between devices, shift(): high = lax.ppermute(head, axis, [(i + 1, i) for i in range(ends)])  4.5 us
  transfers between devices with their start and end apart: 14, of which 5 were waited for; matrix products, arithmetic and copies ran while one was open for 0% of the time, Pallas kernels for 17%

profile of v6, /device:TPU:2, one launch (start us, length us, event | category | flops | bytes accessed | tf_op | source)
XLA Modules:
  0.0 147.9 jit_solution(18300714919497330417)
XLA Ops:
  0.6 15.1 %collective-permute-start.6 = (f32[16,32,128]{2,1,0:T(8,128)}, f32[16,32,128]{2,1,0:T(8,128)S(1)}, u32[]{:S(2)}, u32[]{:S(2)}) collective-permute-start(f32[16,32,128]{2,1,0:T(8,128)} %refs_3_.1), channel_id=1, source_target_pairs={{32,64},{64,32},{96,128},{128,96},{160,192},{192,160},{224,256},{2... | collective-permute-start | bytes 786440 | tf_op jit(solution)/shard_map/ppermute | solution.py:508
  15.8 0.0 copy-start
  15.8 0.9 copy-done
  16.7 1.0 shard_map.60
  17.7 3.5 %collective-permute-start.1 = (f32[16,32,128]{2,1,0:T(8,128)S(1)}, f32[16,32,128]{2,1,0:T(8,128)S(1)}, u32[]{:S(2)}, u32[]{:S(2)}) collective-permute-start(f32[16,32,128]{2,1,0:T(8,128)S(1)} %get-tuple-element.107), channel_id=1, source_target_pairs={{0,8},{8,16},{16,24},{1,9},{9,17},{17,25},{2,10},{10,18},{18,26},{... | collective-permute-start | bytes 786440 | tf_op jit(solution)/shard_map/ppermute | solution.py:517
  21.2 1.3 collective-permute-start.2
  22.5 0.0 copy-start.1
  22.6 0.0 copy-start.8
  22.6 2.5 %collective-permute-start.3 = (f32[16,32,128]{2,1,0:T(8,128)S(1)}, f32[16,32,128]{2,1,0:T(8,128)S(1)}, u32[]{:S(2)}, u32[]{:S(2)}) collective-permute-start(f32[16,32,128]{2,1,0:T(8,128)S(1)} %get-tuple-element.109), channel_id=1, source_target_pairs={{0,32},{32,0},{64,96},{96,64},{128,160},{160,128},{192,224},{224,1... | collective-permute-start | bytes 786440 | tf_op jit(solution)/shard_map/ppermute | solution.py:512
  25.0 1.6 %shard_map.59 = (f32[256,256]{1,0:T(8,128)S(1)}, f32[256,256]{1,0:T(8,128)}, f32[8,128]{1,0:T(8,128)S(1)}) custom-call(f32[3,17]{1,0:T(4,128)} %refs_1_.9), custom_call_target="tpu_custom_call" | custom-call | flops 5000000000 | bytes 528588 | tf_op jit(solution)/shard_map/pallas_call | solution.py:56
  26.6 1.0 collective-permute-done.1.refs_2_.refs_4_.refs_5_
  27.6 4.1 %collective-permute-done.2.refs_3_.refs_5_.refs_6_ = f32[16,32,128]{2,1,0:T(8,128)S(1)} collective-permute-done((f32[16,32,128]{2,1,0:T(8,128)S(1)}, f32[16,32,128]{2,1,0:T(8,128)S(1)}, u32[]{:S(2)}, u32[]{:S(2)}) %collective-permute-start.2) | collective-permute-done | bytes 262176 | tf_op jit(solution)/shard_map/ppermute | solution.py:518
  31.8 0.0 collective-permute-done.3.refs_4_.refs_8_
  31.8 0.0 copy-done.1
  31.8 0.0 copy-done.8
  31.8 0.0 copy-start.21
  31.8 1.1 shard_map.61
  32.9 5.4 %collective-permute-done.6.refs_0_.refs_9_ = f32[16,32,128]{2,1,0:T(8,128)S(1)} collective-permute-done((f32[16,32,128]{2,1,0:T(8,128)}, f32[16,32,128]{2,1,0:T(8,128)S(1)}, u32[]{:S(2)}, u32[]{:S(2)}) %collective-permute-start.6) | collective-permute-done | bytes 262176 | tf_op jit(solution)/shard_map/ppermute | solution.py:508
  38.3 0.0 copy-done.6
  38.3 3.5 %collective-permute-start.7 = (f32[16,24,128]{2,1,0:T(8,128)S(1)}, f32[16,24,128]{2,1,0:T(8,128)S(1)}, u32[]{:S(2)}, u32[]{:S(2)}) collective-permute-start(f32[16,24,128]{2,1,0:T(8,128)S(1)} %get-tuple-element.114), channel_id=1, source_target_pairs={{0,8},{8,16},{16,24},{1,9},{9,17},{17,25},{2,10},{10,18},{18,26},{... | collective-permute-start | bytes 589832 | tf_op jit(solution)/shard_map/ppermute | solution.py:517
  41.8 1.3 collective-permute-start.8
  43.1 1.3 collective-permute-start.4
  44.4 4.9 %collective-permute-start.5 = (f32[20,16,128]{2,1,0:T(8,128)S(1)}, f32[20,16,128]{2,1,0:T(8,128)S(1)}, u32[]{:S(2)}, u32[]{:S(2)}) collective-permute-start(f32[20,16,128]{2,1,0:T(8,128)S(1)} %get-tuple-element.112.refs_2_), channel_id=1, source_target_pairs={{0,1},{1,2},{2,3},{3,4},{4,5},{5,6},{6,7},{8,9},{9,10},{10,11},{11... | collective-permute-start | bytes 491528 | tf_op jit(solution)/shard_map/ppermute | solution.py:517
  49.3 1.9 %collective-permute-start.11 = (f32[16,48,128]{2,1,0:T(8,128)S(1)}, f32[16,48,128]{2,1,0:T(8,128)S(1)}, u32[]{:S(2)}, u32[]{:S(2)}) collective-permute-start(f32[16,48,128]{2,1,0:T(8,128)S(1)} %get-tuple-element.118), channel_id=1, source_target_pairs={{0,32},{32,0},{64,96},{96,64},{128,160},{160,128},{192,224},{224,1... | collective-permute-start | bytes 1179656 | tf_op jit(solution)/shard_map/ppermute | solution.py:512
  51.2 0.3 collective-permute-done.4.refs_3_.refs_6_.refs_7_
  51.6 1.2 collective-permute-done.5.refs_4_.refs_7_.refs_8_
  52.8 0.0 collective-permute-done.7.refs_1_.refs_10_
  52.8 0.0 collective-permute-done.8.refs_2_.refs_11_
  52.8 0.9 shard_map.63
  53.6 0.0 copy-done.14
  53.7 1.9 %collective-permute-start.12 = (f32[16,32,128]{2,1,0:T(8,128)S(1)}, f32[16,32,128]{2,1,0:T(8,128)S(1)}, u32[]{:S(2)}, u32[]{:S(2)}) collective-permute-start(f32[16,32,128]{2,1,0:T(8,128)S(1)} %get-tuple-element.119), channel_id=1, source_target_pairs={{0,32},{32,0},{64,96},{96,64},{128,160},{160,128},{192,224},{224,1... | collective-permute-start | bytes 786440 | tf_op jit(solution)/shard_map/ppermute | solution.py:512
  55.6 1.3 collective-permute-start.9
  56.9 5.0 %collective-permute-start.10 = (f32[16,16,128]{2,1,0:T(8,128)S(1)}, f32[16,16,128]{2,1,0:T(8,128)S(1)}, u32[]{:S(2)}, u32[]{:S(2)}) collective-permute-start(f32[16,16,128]{2,1,0:T(8,128)S(1)} %get-tuple-element.117), channel_id=1, source_target_pairs={{0,1},{1,2},{2,3},{3,4},{4,5},{5,6},{6,7},{8,9},{9,10},{10,11},{11... | collective-permute-start | bytes 393224 | tf_op jit(solution)/shard_map/ppermute | solution.py:517
  61.9 0.0 copy-done.16
  62.0 0.1 stack.31.refs_0_
  62.1 0.0 copy-start.17
  62.1 0.0 copy-start.20
  62.1 0.0 collective-permute-done.11.refs_9_
  62.1 0.0 collective-permute-done.12.refs_10_
  62.1 0.0 copy-done.21
  62.1 7.8 %shard_map.64 = (f32[32,80,128]{2,1,0:T(8,128)S(1)}, f32[32,80,128]{2,1,0:T(8,128)S(1)}, f32[16,80,128]{2,1,0:T(8,128)S(1)}, f32[16,80,128]{2,1,0:T(8,128)S(1)},...) custom-call(s32[7]{0:T(128)S(1)} %stack.31.refs_0_, ...), custom_call_target="tpu_custom_call" | custom-call | flops 1000 | bytes 8323304 | tf_op jit(solution)/shard_map/pallas_call | solution.py:56
  70.0 0.0 collective-permute-done.9.refs_12_
  70.0 0.0 collective-permute-done.10.refs_13_
  70.0 0.0 copy-done.7
  70.0 0.0 copy-done.9
  70.0 8.5 %shard_map.65 = (f32[16,80,128]{2,1,0:T(8,128)}, f32[16,80,128]{2,1,0:T(8,128)}, f32[32,64,128]{2,1,0:T(8,128)}, f32[32,64,128]{2,1,0:T(8,128)}, f32[8,32,128]{2...) custom-call(s32[7]{0:T(128)S(1)} %stack.31.refs_0_, ...), custom_call_target="tpu_custom_call" | custom-call | flops 1000 | bytes 11620584 | tf_op jit(solution)/shard_map/pallas_call | solution.py:56
  78.5 11.0 %collective-permute-start.13 = (f32[37,8,128]{2,1,0:T(8,128)S(1)}, f32[37,8,128]{2,1,0:T(8,128)S(1)}, u32[]{:S(2)}, u32[]{:S(2)}) collective-permute-start(f32[37,8,128]{2,1,0:T(8,128)S(1)} %get-tuple-element.135), channel_id=1, source_target_pairs={{32,64},{64,32},{96,128},{128,96},{160,192},{192,160},{224,256},{2... | collective-permute-start | bytes 454664 | tf_op jit(solution)/shard_map/ppermute | solution.py:508
  89.5 13.5 %conditional.1 = (f32[16,32,128]{2,1,0:T(8,128)}, f32[8,48,128]{2,1,0:T(8,128)}, f32[8,48,128]{2,1,0:T(8,128)}, f32[37,8,128]{2,1,0:T(8,128)}, f32[32,48,128]{2,1,0:T(8,128)S(1)}, /*index=5*/f32[32,48,128]{2,1,0:T(8,128)S(1)}) conditional(s32[]{:T(128)} %convert_element_type.3, () %tuple.16, (s32[7]{0:T(128)S(1)}, f32[3,17]{1,0:T(4,128)S(1)}, ...), branch_computations={%region_0.1_spmd, %region_1.2_spmd} | conditional | flops 2000 | bytes 28611048 | solution.py:604
  89.5 0.0 copy-start.3
  89.5 0.0 copy-start.5
  89.5 0.0 copy-start.11
  89.5 0.0 copy-start.13
  89.5 0.0 copy-start.19
  89.5 4.8 %branch_1_fun.2 = (f32[16,32,128]{2,1,0:T(8,128)}, f32[8,48,128]{2,1,0:T(8,128)}, f32[8,48,128]{2,1,0:T(8,128)}, f32[37,8,128]{2,1,0:T(8,128)S(1)}) custom-call(s32[7]{0:T(128)S(1)} %get-tuple-element.36.refs_0_, f32[3,17]{1,0:T(4,128)S(1)} %get-tuple-element.37.refs_1_, f32[256,256]{1,0:T(8,128)} %get-tuple-element.38.refs_2_, ...), custom_call_target="tpu_custom_call" | custom-call | flops 1000 | bytes 5460200 | tf_op jit(solution)/shard_map/cond/branch_1_fun/pallas_call | solution.py:56
  94.4 4.6 %collective-permute-start = (f32[37,8,128]{2,1,0:T(8,128)S(1)}, f32[37,8,128]{2,1,0:T(8,128)}, u32[]{:S(2)}, u32[]{:S(2)}) collective-permute-start(f32[37,8,128]{2,1,0:T(8,128)S(1)} %get-tuple-element.52), channel_id=1, source_target_pairs={{0,32},{32,0},{64,96},{96,64},{128,160},{160,128},{192,224},{224,1... | collective-permute-start | bytes 454664 | tf_op jit(solution)/shard_map/cond/branch_1_fun/ppermute | solution.py:512
  99.1 3.9 %branch_1_fun.3 = (f32[32,48,128]{2,1,0:T(8,128)S(1)}, f32[32,48,128]{2,1,0:T(8,128)S(1)}) custom-call(s32[7]{0:T(128)S(1)} %get-tuple-element.36.refs_0_, f32[256,256]{1,0:T(8,128)S(1)} %copy-done.19, f32[32,80,128]{2,1,0:T(8,128)S(1)} %copy-done.3, f32[32,80,128]{2,1,0:T(8,128)S(1)} %copy-done.5, f32[16,80,128]{2,1,0:T(8,128)S(1)} %copy-done.11, ...), custom_call_target="tpu_custom_call" | custom-call | flops 1000 | bytes 5767196 | tf_op jit(solution)/shard_map/cond/branch_1_fun/pallas_call | solution.py:56
  103.0 0.0 collective-permute-done
  103.0 0.0 copy-start.18
  103.0 4.4 %shard_map.66 = (f32[8,48,128]{2,1,0:T(8,128)S(1)}, f32[8,48,128]{2,1,0:T(8,128)S(1)}, f32[8,40,128]{2,1,0:T(8,128)S(1)}, f32[8,40,128]{2,1,0:T(8,128)S(1)}, f32...) custom-call(s32[7]{0:T(128)S(1)} %stack.31.refs_0_, f32[256,256]{1,0:T(8,128)} %constant.52.clone.refs_1_, ...), custom_call_target="tpu_custom_call" | custom-call | flops 1000 | bytes 6246940 | tf_op jit(solution)/shard_map/pallas_call | solution.py:56
  107.5 0.0 collective-permute-done.13.refs_6_
  107.5 2.0 %shard_map.67 = (f32[8,32,128]{2,1,0:T(8,128)S(1)}, f32[1,128]{1,0:T(1,128)S(1)}) custom-call(s32[7]{0:T(128)S(1)} %stack.31.refs_0_, f32[256,256]{1,0:T(8,128)S(1)} %copy-done.18, f32[32,48,128]{2,1,0:T(8,128)S(1)} %get-tuple-element.133.refs_2_, f32[32,48,128]{2,1,0:T(8,128)S(1)} %get-tuple-element.134.refs_3_, f32[16,80,128]{2,1,0:T(8,128)S(1)} %copy-done.10, ...), custom_call_target="tpu_custom_call" | custom-call | flops 1000 | bytes 4543516 | tf_op jit(solution)/shard_map/pallas_call | solution.py:56
  109.5 24.0 %all_to_all.10 = f32[32,1,128]{2,1,0:T(1,128)S(1)} all-to-all(f32[32,1,128]{2,1,0:T(1,128)S(1)} %broadcast_in_dim.7), channel_id=1, replica_groups=mesh['gx_0'=4,'gx_1'=2,'gx_2'=2,'gy'=4,'gz'=8] {'gx_1','gx_2','gz'}, dimensions={0} | all-to-all | bytes 32768 | tf_op jit(solution)/shard_map/all_to_all | solution.py:524
  133.5 13.0 %all_to_all.11.refs_1_ = f32[16,1,128]{2,1,0:T(1,128)S(1)} all-to-all(f32[16,1,128]{2,1,0:T(1,128)S(1)} %broadcast_in_dim.16), channel_id=1, replica_groups=mesh['gx_0'=4,'gx_1'=2,'gx_2'=2,'gy'=4,'gz'=8] {'gx_0','gy'}, dimensions={0} | all-to-all | bytes 16384 | tf_op jit(solution)/shard_map/all_to_all | solution.py:524
  146.5 1.4 shard_map.68
  (27 shorter events, 0.1 us)
Async XLA Ops:
  0.6 37.6 %collective-permute-start.6 = (f32[16,32,128]{2,1,0:T(8,128)}, f32[16,32,128]{2,1,0:T(8,128)S(1)}, u32[]{:S(2)}, u32[]{:S(2)}) collective-permute-start(f32[16,32,128]{2,1,0:T(8,128)} %refs_3_.1), channel_id=1, source_target_pairs={{32,64},{64,32},{96,128},{128,96},{160,192},{192,160},{224,256},{2... | collective-permute-start | bytes 786440 | tf_op jit(solution)/shard_map/ppermute | solution.py:508
  15.8 1.0 copy-start
  17.7 9.9 %collective-permute-start.1 = (f32[16,32,128]{2,1,0:T(8,128)S(1)}, f32[16,32,128]{2,1,0:T(8,128)S(1)}, u32[]{:S(2)}, u32[]{:S(2)}) collective-permute-start(f32[16,32,128]{2,1,0:T(8,128)S(1)} %get-tuple-element.107), channel_id=1, source_target_pairs={{0,8},{8,16},{16,24},{1,9},{9,17},{17,25},{2,10},{10,18},{18,26},{... | collective-permute-start | bytes 786440 | tf_op jit(solution)/shard_map/ppermute | solution.py:517
  21.2 10.5 %collective-permute-start.2 = (f32[16,32,128]{2,1,0:T(8,128)S(1)}, f32[16,32,128]{2,1,0:T(8,128)S(1)}, u32[]{:S(2)}, u32[]{:S(2)}) collective-permute-start(f32[16,32,128]{2,1,0:T(8,128)S(1)} %get-tuple-element.108), channel_id=1, source_target_pairs={{8,0},{16,8},{24,16},{9,1},{17,9},{25,17},{10,2},{18,10},{26,18},{... | collective-permute-start | bytes 786440 | tf_op jit(solution)/shard_map/ppermute | solution.py:518
  22.5 9.3 %copy-start.1 = (f32[16,32,128]{2,1,0:T(8,128)S(1)}, f32[16,32,128]{2,1,0:T(8,128)}, u32[]{:S(2)}) copy-start(f32[16,32,128]{2,1,0:T(8,128)} %refs_3_.1) | copy-start | bytes 786436
  22.6 9.2 %copy-start.8 = (f32[16,32,128]{2,1,0:T(8,128)S(1)}, f32[16,32,128]{2,1,0:T(8,128)}, u32[]{:S(2)}) copy-start(f32[16,32,128]{2,1,0:T(8,128)} %refs_4_.1) | copy-start | bytes 786436
  22.6 9.2 %collective-permute-start.3 = (f32[16,32,128]{2,1,0:T(8,128)S(1)}, f32[16,32,128]{2,1,0:T(8,128)S(1)}, u32[]{:S(2)}, u32[]{:S(2)}) collective-permute-start(f32[16,32,128]{2,1,0:T(8,128)S(1)} %get-tuple-element.109), channel_id=1, source_target_pairs={{0,32},{32,0},{64,96},{96,64},{128,160},{160,128},{192,224},{224,1... | collective-permute-start | bytes 786440 | tf_op jit(solution)/shard_map/ppermute | solution.py:512
  31.8 6.5 %copy-start.6 = (f32[16,32,128]{2,1,0:T(8,128)}, f32[16,32,128]{2,1,0:T(8,128)S(1)}, u32[]{:S(2)}) copy-start(f32[16,32,128]{2,1,0:T(8,128)S(1)} %collective-permute-done.2.refs_3_.refs_5_.refs_6_) | copy-start | bytes 786436
  31.8 30.3 %copy-start.21 = (f32[3,17]{1,0:T(4,128)S(1)}, f32[3,17]{1,0:T(4,128)}, u32[]{:S(2)}) copy-start(f32[3,17]{1,0:T(4,128)} %refs_1_.9) | copy-start | bytes 616
  38.3 14.5 %collective-permute-start.7 = (f32[16,24,128]{2,1,0:T(8,128)S(1)}, f32[16,24,128]{2,1,0:T(8,128)S(1)}, u32[]{:S(2)}, u32[]{:S(2)}) collective-permute-start(f32[16,24,128]{2,1,0:T(8,128)S(1)} %get-tuple-element.114), channel_id=1, source_target_pairs={{0,8},{8,16},{16,24},{1,9},{9,17},{17,25},{2,10},{10,18},{18,26},{... | collective-permute-start | bytes 589832 | tf_op jit(solution)/shard_map/ppermute | solution.py:517
  41.8 11.0 %collective-permute-start.8 = (f32[16,24,128]{2,1,0:T(8,128)S(1)}, f32[16,24,128]{2,1,0:T(8,128)S(1)}, u32[]{:S(2)}, u32[]{:S(2)}) collective-permute-start(f32[16,24,128]{2,1,0:T(8,128)S(1)} %get-tuple-element.115), channel_id=1, source_target_pairs={{8,0},{16,8},{24,16},{9,1},{17,9},{25,17},{10,2},{18,10},{26,18},{... | collective-permute-start | bytes 589832 | tf_op jit(solution)/shard_map/ppermute | solution.py:518
  43.1 8.5 %collective-permute-start.4 = (f32[20,16,128]{2,1,0:T(8,128)S(1)}, f32[20,16,128]{2,1,0:T(8,128)S(1)}, u32[]{:S(2)}, u32[]{:S(2)}) collective-permute-start(f32[20,16,128]{2,1,0:T(8,128)S(1)} %get-tuple-element.111.refs_1_), channel_id=1, source_target_pairs={{1,0},{2,1},{3,2},{4,3},{5,4},{6,5},{7,6},{9,8},{10,9},{11,10},{12... | collective-permute-start | bytes 491528 | tf_op jit(solution)/shard_map/ppermute | solution.py:518
  44.4 8.4 %collective-permute-start.5 = (f32[20,16,128]{2,1,0:T(8,128)S(1)}, f32[20,16,128]{2,1,0:T(8,128)S(1)}, u32[]{:S(2)}, u32[]{:S(2)}) collective-permute-start(f32[20,16,128]{2,1,0:T(8,128)S(1)} %get-tuple-element.112.refs_2_), channel_id=1, source_target_pairs={{0,1},{1,2},{2,3},{3,4},{4,5},{5,6},{6,7},{8,9},{9,10},{10,11},{11... | collective-permute-start | bytes 491528 | tf_op jit(solution)/shard_map/ppermute | solution.py:517
  49.3 12.8 %collective-permute-start.11 = (f32[16,48,128]{2,1,0:T(8,128)S(1)}, f32[16,48,128]{2,1,0:T(8,128)S(1)}, u32[]{:S(2)}, u32[]{:S(2)}) collective-permute-start(f32[16,48,128]{2,1,0:T(8,128)S(1)} %get-tuple-element.118), channel_id=1, source_target_pairs={{0,32},{32,0},{64,96},{96,64},{128,160},{160,128},{192,224},{224,1... | collective-permute-start | bytes 1179656 | tf_op jit(solution)/shard_map/ppermute | solution.py:512
  51.6 2.1 %copy-start.14 = (f32[20,16,128]{2,1,0:T(8,128)}, f32[20,16,128]{2,1,0:T(8,128)S(1)}, u32[]{:S(2)}) copy-start(f32[20,16,128]{2,1,0:T(8,128)S(1)} %collective-permute-done.4.refs_3_.refs_6_.refs_7_) | copy-start | bytes 491524
  52.8 9.1 %copy-start.16 = (f32[20,16,128]{2,1,0:T(8,128)}, f32[20,16,128]{2,1,0:T(8,128)S(1)}, u32[]{:S(2)}) copy-start(f32[20,16,128]{2,1,0:T(8,128)S(1)} %collective-permute-done.5.refs_4_.refs_7_.refs_8_) | copy-start | bytes 491524
  53.7 8.4 %collective-permute-start.12 = (f32[16,32,128]{2,1,0:T(8,128)S(1)}, f32[16,32,128]{2,1,0:T(8,128)S(1)}, u32[]{:S(2)}, u32[]{:S(2)}) collective-permute-start(f32[16,32,128]{2,1,0:T(8,128)S(1)} %get-tuple-element.119), channel_id=1, source_target_pairs={{0,32},{32,0},{64,96},{96,64},{128,160},{160,128},{192,224},{224,1... | collective-permute-start | bytes 786440 | tf_op jit(solution)/shard_map/ppermute | solution.py:512
  55.6 14.4 %collective-permute-start.9 = (f32[16,16,128]{2,1,0:T(8,128)S(1)}, f32[16,16,128]{2,1,0:T(8,128)S(1)}, u32[]{:S(2)}, u32[]{:S(2)}) collective-permute-start(f32[16,16,128]{2,1,0:T(8,128)S(1)} %get-tuple-element.116), channel_id=1, source_target_pairs={{1,0},{2,1},{3,2},{4,3},{5,4},{6,5},{7,6},{9,8},{10,9},{11,10},{12... | collective-permute-start | bytes 393224 | tf_op jit(solution)/shard_map/ppermute | solution.py:518
  56.9 13.1 %collective-permute-start.10 = (f32[16,16,128]{2,1,0:T(8,128)S(1)}, f32[16,16,128]{2,1,0:T(8,128)S(1)}, u32[]{:S(2)}, u32[]{:S(2)}) collective-permute-start(f32[16,16,128]{2,1,0:T(8,128)S(1)} %get-tuple-element.117), channel_id=1, source_target_pairs={{0,1},{1,2},{2,3},{3,4},{4,5},{5,6},{6,7},{8,9},{9,10},{10,11},{11... | collective-permute-start | bytes 393224 | tf_op jit(solution)/shard_map/ppermute | solution.py:517
  62.0 7.9 %copy-start.7 = (f32[16,32,128]{2,1,0:T(8,128)S(1)}, f32[16,32,128]{2,1,0:T(8,128)}, u32[]{:S(2)}) copy-start(f32[16,32,128]{2,1,0:T(8,128)} %copy-done.6) | copy-start | bytes 786436
  62.0 7.9 %copy-start.9 = (f32[16,32,128]{2,1,0:T(8,128)S(1)}, f32[16,32,128]{2,1,0:T(8,128)}, u32[]{:S(2)}) copy-start(f32[16,32,128]{2,1,0:T(8,128)} %refs_4_.1) | copy-start | bytes 786436
  62.0 8.0 %copy-start.15 = (f32[20,16,128]{2,1,0:T(8,128)S(1)}, f32[20,16,128]{2,1,0:T(8,128)}, u32[]{:S(2)}) copy-start(f32[20,16,128]{2,1,0:T(8,128)} %copy-done.14) | copy-start | bytes 491524
  62.1 8.0 %copy-start.17 = (f32[20,16,128]{2,1,0:T(8,128)S(1)}, f32[20,16,128]{2,1,0:T(8,128)}, u32[]{:S(2)}) copy-start(f32[20,16,128]{2,1,0:T(8,128)} %copy-done.16) | copy-start | bytes 491524
  62.1 8.0 %copy-start.20 = (f32[256,256]{1,0:T(8,128)S(1)}, f32[256,256]{1,0:T(8,128)}, u32[]{:S(2)}) copy-start(f32[256,256]{1,0:T(8,128)} %get-tuple-element.106.refs_3_) | copy-start | bytes 786436
  70.0 8.5 %copy-start.2 = (f32[32,80,128]{2,1,0:T(8,128)}, f32[32,80,128]{2,1,0:T(8,128)S(1)}, u32[]{:S(2)}) copy-start(f32[32,80,128]{2,1,0:T(8,128)S(1)} %get-tuple-element.120.refs_14_.refs_4_) | copy-start | bytes 3932164
  70.0 8.5 %copy-start.4 = (f32[32,80,128]{2,1,0:T(8,128)}, f32[32,80,128]{2,1,0:T(8,128)S(1)}, u32[]{:S(2)}) copy-start(f32[32,80,128]{2,1,0:T(8,128)S(1)} %get-tuple-element.121.refs_15_.refs_5_) | copy-start | bytes 3932164
  78.5 29.0 %collective-permute-start.13 = (f32[37,8,128]{2,1,0:T(8,128)S(1)}, f32[37,8,128]{2,1,0:T(8,128)S(1)}, u32[]{:S(2)}, u32[]{:S(2)}) collective-permute-start(f32[37,8,128]{2,1,0:T(8,128)S(1)} %get-tuple-element.135), channel_id=1, source_target_pairs={{32,64},{64,32},{96,128},{128,96},{160,192},{192,160},{224,256},{2... | collective-permute-start | bytes 454664 | tf_op jit(solution)/shard_map/ppermute | solution.py:508
  89.5 9.5 %copy-start.3 = (f32[32,80,128]{2,1,0:T(8,128)S(1)}, f32[32,80,128]{2,1,0:T(8,128)}, u32[]{:S(2)}) copy-start(f32[32,80,128]{2,1,0:T(8,128)} %get-tuple-element.54.refs_2_) | copy-start | bytes 3932164 | tf_op jit(solution)/shard_map/cond
  89.5 9.5 %copy-start.5 = (f32[32,80,128]{2,1,0:T(8,128)S(1)}, f32[32,80,128]{2,1,0:T(8,128)}, u32[]{:S(2)}) copy-start(f32[32,80,128]{2,1,0:T(8,128)} %get-tuple-element.55.refs_3_) | copy-start | bytes 3932164 | tf_op jit(solution)/shard_map/cond
  89.5 9.5 %copy-start.11 = (f32[16,80,128]{2,1,0:T(8,128)S(1)}, f32[16,80,128]{2,1,0:T(8,128)}, u32[]{:S(2)}) copy-start(f32[16,80,128]{2,1,0:T(8,128)} %get-tuple-element.56.refs_4_) | copy-start | bytes 1966084 | tf_op jit(solution)/shard_map/cond
  89.5 9.5 %copy-start.13 = (f32[16,80,128]{2,1,0:T(8,128)S(1)}, f32[16,80,128]{2,1,0:T(8,128)}, u32[]{:S(2)}) copy-start(f32[16,80,128]{2,1,0:T(8,128)} %get-tuple-element.57.refs_5_) | copy-start | bytes 1966084 | tf_op jit(solution)/shard_map/cond
  89.5 9.5 %copy-start.19 = (f32[256,256]{1,0:T(8,128)S(1)}, f32[256,256]{1,0:T(8,128)}, u32[]{:S(2)}) copy-start(f32[256,256]{1,0:T(8,128)} %get-tuple-element.53.refs_1_) | copy-start | bytes 786436 | tf_op jit(solution)/shard_map/cond
  94.4 8.6 %collective-permute-start = (f32[37,8,128]{2,1,0:T(8,128)S(1)}, f32[37,8,128]{2,1,0:T(8,128)}, u32[]{:S(2)}, u32[]{:S(2)}) collective-permute-start(f32[37,8,128]{2,1,0:T(8,128)S(1)} %get-tuple-element.52), channel_id=1, source_target_pairs={{0,32},{32,0},{64,96},{96,64},{128,160},{160,128},{192,224},{224,1... | collective-permute-start | bytes 454664 | tf_op jit(solution)/shard_map/cond/branch_1_fun/ppermute | solution.py:512
  103.0 4.5 %copy-start.10 = (f32[16,80,128]{2,1,0:T(8,128)S(1)}, f32[16,80,128]{2,1,0:T(8,128)}, u32[]{:S(2)}) copy-start(f32[16,80,128]{2,1,0:T(8,128)} %get-tuple-element.131.refs_4_) | copy-start | bytes 1966084
  103.0 4.5 %copy-start.12 = (f32[16,80,128]{2,1,0:T(8,128)S(1)}, f32[16,80,128]{2,1,0:T(8,128)}, u32[]{:S(2)}) copy-start(f32[16,80,128]{2,1,0:T(8,128)} %get-tuple-element.132.refs_5_) | copy-start | bytes 1966084
  103.0 4.5 %copy-start.18 = (f32[256,256]{1,0:T(8,128)S(1)}, f32[256,256]{1,0:T(8,128)}, u32[]{:S(2)}) copy-start(f32[256,256]{1,0:T(8,128)} %constant.52.clone.refs_1_) | copy-start | bytes 786436
